TPU v7x, 32 devices: a whole 2x2x4 slice. The times are simulated.
32 devices in a mesh: chain: 2 (over x), slab: 16 (over z, y, core).
Axes of the slice: x: 2, y: 2, z: 4, core: 2. Of those that a mesh axis runs over, the one named last changes fastest.
Arguments:
- whitened: float32 [1024, 256, 256], P(('chain', 'slab')), parts along dimension 0, may hold values from -6 to 6
- counts: int32 [1024, 256, 256], P(('chain', 'slab')), parts along dimension 0, may hold values from 0 to 24
- exposure: int32 [1024, 256, 256], P(('chain', 'slab')), parts along dimension 0, may hold values from 1 to 12
- cholesky_east: float32 [512, 512], replicated, as said below
- cholesky_north: float32 [256, 256], replicated, as said below
- cholesky_time: float32 [256, 256], replicated, as said below
Outputs:
- gradient: float32 [1024, 256, 256], P(('chain', 'slab')), parts along dimension 0
- density: float32 [2], P('chain'), parts along dimension 0
There are 2 independent parts, one for each index of `chain`. A program takes and returns all parts, laid end to end along the dimension named above; an argument that names none is the same for every part. Nothing has to cross between parts.
Inputs may be any that keep to these rules, and one draw needn't show every extreme that they name: `cholesky_east`: lower triangular with a positive diagonal, each row of unit length. `cholesky_north`: lower triangular with a positive diagonal, each row of unit length. `cholesky_time`: lower triangular with a positive diagonal, each row of unit length.
All inputs are finite; a program needn't handle non-finite values.
Results may differ from a plain program's by a relative error of at most 0.00008.
Values sent between devices are 32-bit elements; how exact they have to be, the bound alone decides.
No kernel may reach another device: no remote copies, remote signals or barrier semaphores. Data moves between devices by JAX's collectives and lax.ppermute only.
A program may use at most 128 MiB of HBM per device.

v0:
```python
import jax
import jax.numpy as jnp
from jax import lax
from jax.sharding import PartitionSpec as P

field_scale = 0.6


def mode_last(values, matrix):
    return jnp.einsum("abc,tc->abt", values, matrix, precision=lax.Precision.HIGHEST)


def mode_middle(values, matrix):
    return jnp.einsum("abc,yb->ayc", values, matrix, precision=lax.Precision.HIGHEST)


def mode_first(values, matrix):
    return jnp.einsum("abc,xa->xbc", values, matrix, precision=lax.Precision.HIGHEST)


def adjoint_last(values, matrix):
    return jnp.einsum("abt,tc->abc", values, matrix, precision=lax.Precision.HIGHEST)


def adjoint_middle(values, matrix):
    return jnp.einsum("ayc,yb->abc", values, matrix, precision=lax.Precision.HIGHEST)


def adjoint_first(values, matrix):
    return jnp.einsum("xbc,xa->abc", values, matrix, precision=lax.Precision.HIGHEST)


def to_lines(values):
    return lax.all_to_all(values, "slab", split_axis=1, concat_axis=0, tiled=True)


def to_planes(values):
    return lax.all_to_all(values, "slab", split_axis=0, concat_axis=1, tiled=True)


def per_device(whitened, counts, exposure, cholesky_east, cholesky_north, cholesky_time):
    cell_count = whitened.shape[0] * whitened.shape[1] * whitened.shape[2]
    prior_term = -0.5 * jnp.sum(whitened * whitened)
    partly = mode_middle(mode_last(whitened, cholesky_time), cholesky_north)
    counts_lines, exposure_lines = (
        lax.all_to_all(counts, "slab", split_axis=1, concat_axis=0, tiled=True),
        lax.all_to_all(exposure, "slab", split_axis=1, concat_axis=0, tiled=True),
    )
    log_lines = field_scale * mode_first(to_lines(partly), cholesky_east)
    observed = counts_lines.astype(jnp.float32)
    intensity = exposure_lines.astype(jnp.float32) * jnp.exp(log_lines)
    residual = observed - intensity
    partial_sum = jnp.sum(observed * log_lines - intensity) + prior_term
    adjoint_lines = adjoint_first(residual, cholesky_east)
    adjoint = to_planes(adjoint_lines)
    adjoint = adjoint_last(adjoint_middle(adjoint, cholesky_north), cholesky_time)
    gradient = field_scale * adjoint - whitened
    total_sum = lax.psum(partial_sum, "slab")
    density = total_sum / (cell_count * lax.axis_size("slab"))
    return (gradient, jnp.reshape(density, (1,)))


def solution(mesh):
    placed = (
        P(("chain", "slab"), None, None),
        P(("chain", "slab"), None, None),
        P(("chain", "slab"), None, None),
        P(),
        P(),
        P(),
    )
    return jax.shard_map(
        per_device,
        mesh=mesh,
        in_specs=placed,
        out_specs=(P(("chain", "slab"), None, None), P("chain")),
        check_vma=False,
    )
```

profile of v0, /device:TPU:18, one launch (start us, length us, event | category | flops | bytes accessed | tf_op | source)
XLA Modules:
  0.0 900.6 jit_solution(4330136956723541852)
XLA Ops:
  0.6 0.0 copy-start
  0.6 11.5 %copy.35 = s32[32,256,256]{2,0,1:T(8,128)} copy(s32[32,256,256]{2,1,0:T(8,128)} %param.8) | data formatting | bytes 16777216 | tf_op args[2]
  12.2 6.2 all-to-all-start.1
  18.4 11.6 %copy.32 = s32[32,256,256]{2,0,1:T(8,128)} copy(s32[32,256,256]{2,1,0:T(8,128)} %param.7) | data formatting | bytes 16777216 | tf_op args[1]
  30.0 0.0 copy-start.2
  30.0 170.9 %all-to-all-done.1 = s32[32,256,256]{2,0,1:T(8,128)} async-done(((s32[32,256,256]{2,0,1:T(8,128)}), s32[32,256,256]{2,0,1:T(8,128)}, u32[]{:S(2)}, u32[]{:S(2)}) %all-to-all-start.1) | async-done | bytes 8388640 | tf_op jit(solution)/shard_map/all_to_all | solution.py:47
  200.9 5.0 all-to-all-start
  206.0 0.0 copy-done.2
  206.0 0.0 copy-start.1
  206.0 10.7 %fusion.22 = f32[32,256,256]{1,2,0:T(8,128)S(1)} fusion(f32[32,256,256]{2,1,0:T(8,128)} %param.6, f32[256,256]{1,0:T(8,128)S(1)} %copy-done.2), kind=kOutput, calls=%fused_computation.24 | convolution fusion | flops 6442450944 | bytes 17039360 | tf_op jit(solution)/shard_map/abc,tc->abt/dot_general | solution.py:10
  216.7 0.0 copy-done.1
  216.8 8.9 convolution_bitcast_fusion
  225.7 10.3 %copy.39 = f32[32,256,256]{2,0,1:T(8,128)} copy(f32[32,256,256]{1,2,0:T(8,128)} %convolution_bitcast_fusion) | data formatting | bytes 16777216 | tf_op jit(solution)/shard_map/abc,yb->ayc/transpose | solution.py:14
  235.9 152.5 %all-to-all-done = s32[32,256,256]{2,0,1:T(8,128)} async-done(((s32[32,256,256]{2,0,1:T(8,128)}), s32[32,256,256]{2,0,1:T(8,128)}, u32[]{:S(2)}, u32[]{:S(2)}) %all-to-all-start) | async-done | bytes 8388640 | tf_op jit(solution)/shard_map/all_to_all | solution.py:46
  388.4 5.1 all-to-all-start.2
  393.5 8.2 copy_convert_fusion
  401.7 4.4 copy.37
  406.1 10.4 %copy.43 = f32[512,16,256]{0,2,1:T(8,128)} copy(f32[512,16,256]{2,1,0:T(8,128)} %bitcast.68) | data formatting | bytes 16777216 | tf_op jit(solution)/shard_map/convert_element_type | solution.py:51
  416.5 8.2 copy_convert_fusion.1
  424.8 4.4 copy.34
  429.2 10.1 %copy.44 = f32[512,16,256]{0,2,1:T(8,128)} copy(f32[512,16,256]{2,1,0:T(8,128)} %bitcast.70) | data formatting | bytes 16777216 | tf_op jit(solution)/shard_map/convert_element_type | solution.py:50
  439.3 136.6 %all-to-all-done.2 = f32[32,256,256]{2,0,1:T(8,128)} async-done(((f32[32,256,256]{2,0,1:T(8,128)}), f32[32,256,256]{2,0,1:T(8,128)}, u32[]{:S(2)}, u32[]{:S(2)}) %all-to-all-start.2) | async-done | bytes 8388640 | tf_op jit(solution)/shard_map/all_to_all | solution.py:34
  575.9 0.0 slice-start.2
  575.9 13.6 %copy.41 = f32[16,32,16,256]{3,2,1,0:T(8,128)} copy(f32[16,32,16,256]{3,1,2,0:T(8,128)} %bitcast.11) | data formatting | bytes 16777216 | tf_op jit(solution)/shard_map/all_to_all | solution.py:34
  589.5 0.0 copy-done
  589.5 0.0 slice-start.3
  589.5 37.1 %fusion.4 = (f32[]{:T(128)}, f32[16,256,512]{2,1,0:T(8,128)}) fusion(f32[512,16,256]{0,2,1:T(8,128)} %copy.44, f32[512,16,256]{0,2,1:T(8,128)} %copy.43, f32[512,512]{1,0:T(8,128)S(1)} %copy-done, f32[512,16,256]{2,1,0:T(8,128)} %bitcast.66), kind=kOutput, calls=%fused_computation.6 | convolution fusion | flops 12895387648 | bytes 34603012 | tf_op jit(solution)/shard_map/abc,xa->xbc/dot_general | solution.py:18
  626.6 0.0 slice-done.2
  626.6 0.0 slice-done.3
  626.6 20.3 %fusion.13 = f32[512,16,256]{0,2,1:T(8,128)} fusion(f32[512,16,256]{0,2,1:T(8,128)} %copy.44, f32[512,16,256]{0,2,1:T(8,128)S(1)} %bitcast.65, f32[16,256,512]{2,1,0:T(8,128)} %get-tuple-element.3, f32[512,512]{1,0:T(8,128)S(1)} %copy-done), kind=kOutput, calls=%fused_computation.17 | convolution fusion | flops 12891193344 | bytes 34603008 | tf_op jit(solution)/shard_map/xbc,xa->abc/dot_general | solution.py:30
  646.9 10.3 %copy.45 = f32[512,16,256]{2,1,0:T(8,128)} copy(f32[512,16,256]{0,2,1:T(8,128)} %fusion.13) | data formatting | bytes 16777216 | tf_op jit(solution)/shard_map/xbc,xa->abc/dot_general | solution.py:30
  657.2 4.7 all-to-all-start.3
  661.8 6.1 multiply_reduce_fusion
  669.3 193.7 %psum.7 = f32[]{:T(128)} all-reduce(f32[]{:T(128)S(6)} %add.5), channel_id=1, replica_groups=mesh['chain'=2,'slab'=16] {'slab'}, use_global_device_ids=true, to_apply=%region_2.0 | all-reduce | flops 1 | bytes 8 | tf_op jit(solution)/shard_map/psum | solution.py:58
  863.6 0.0 all-to-all-done.3
  863.7 0.0 slice-start
  863.7 4.6 copy.46
  868.2 0.0 slice-start.1
  868.2 14.6 %fusion.18 = f32[32,256,256]{2,1,0:T(8,128)S(1)} fusion(f32[32,256,256]{2,1,0:T(8,128)S(1)} %bitcast.71, f32[256,256]{1,0:T(8,128)S(1)} %copy-done.1), kind=kOutput, calls=%fused_computation.20 | convolution fusion | flops 6442450944 | bytes 17039360 | tf_op jit(solution)/shard_map/ayc,yb->abc/dot_general | solution.py:26
  882.8 0.0 slice-done
  882.8 0.0 slice-done.1
  882.9 16.3 %multiply_subtract_fusion = f32[32,256,256]{2,1,0:T(8,128)} fusion(f32[32,256,256]{2,1,0:T(8,128)S(1)} %bitcast.63, f32[32,256,256]{2,1,0:T(8,128)S(1)} %fusion.18, f32[256,256]{1,0:T(8,128)S(1)} %copy-done.2), kind=kOutput, calls=%fused_computation.12 | convolution fusion | flops 6446645248 | bytes 25427968 | tf_op jit(solution)/shard_map/abt,tc->abc/dot_general | solution.py:22
  (2 shorter events, 0.0 us)
Async XLA Ops:
  0.6 588.9 %copy-start = (f32[512,512]{1,0:T(8,128)S(1)}, f32[512,512]{1,0:T(8,128)}, u32[]{:S(2)}) copy-start(f32[512,512]{1,0:T(8,128)} %param.9) | copy-start | bytes 3145732
  12.2 188.8 %all-to-all-start.1 = ((s32[32,256,256]{2,0,1:T(8,128)}), s32[32,256,256]{2,0,1:T(8,128)}, u32[]{:S(2)}, u32[]{:S(2)}) async-start(s32[32,256,256]{2,0,1:T(8,128)} %copy.35), calls=%async_computation.1 | async-start | bytes 16777216 | tf_op jit(solution)/shard_map/all_to_all | solution.py:47
  30.0 176.0 %copy-start.2 = (f32[256,256]{1,0:T(8,128)S(1)}, f32[256,256]{1,0:T(8,128)}, u32[]{:S(2)}) copy-start(f32[256,256]{1,0:T(8,128)} %param.11) | copy-start | bytes 786436
  200.9 187.5 %all-to-all-start = ((s32[32,256,256]{2,0,1:T(8,128)}), s32[32,256,256]{2,0,1:T(8,128)}, u32[]{:S(2)}, u32[]{:S(2)}) async-start(s32[32,256,256]{2,0,1:T(8,128)} %copy.32), calls=%async_computation | async-start | bytes 16777216 | tf_op jit(solution)/shard_map/all_to_all | solution.py:46
  206.0 10.7 %copy-start.1 = (f32[256,256]{1,0:T(8,128)S(1)}, f32[256,256]{1,0:T(8,128)}, u32[]{:S(2)}) copy-start(f32[256,256]{1,0:T(8,128)} %param.10) | copy-start | bytes 786436
  388.4 187.5 %all-to-all-start.2 = ((f32[32,256,256]{2,0,1:T(8,128)}), f32[32,256,256]{2,0,1:T(8,128)}, u32[]{:S(2)}, u32[]{:S(2)}) async-start(f32[32,256,256]{2,0,1:T(8,128)} %copy.39), calls=%async_computation.2 | async-start | bytes 16777216 | tf_op jit(solution)/shard_map/all_to_all | solution.py:34
  575.9 50.7 %slice-start.2 = ((s8[8388608]{0:T(1024)(128)(4,1)}), s8[4194304]{0:T(1024)(128)(4,1)S(1)}, s32[]{:S(2)}) async-start(s8[8388608]{0:T(1024)(128)(4,1)} %bitcast.64), calls=%async_computation.6 | async-start | bytes 8388608
  589.5 37.1 %slice-start.3 = ((s8[8388608]{0:T(1024)(128)(4,1)}), s8[4194304]{0:T(1024)(128)(4,1)S(1)}, s32[]{:S(2)}) async-start(s8[8388608]{0:T(1024)(128)(4,1)} %bitcast.64), calls=%async_computation.7 | async-start | bytes 8388608
  657.2 206.5 %all-to-all-start.3 = ((f32[512,16,256]{2,1,0:T(8,128)}), f32[512,16,256]{2,1,0:T(8,128)}, u32[]{:S(2)}, u32[]{:S(2)}) async-start(f32[512,16,256]{2,1,0:T(8,128)} %copy.45), calls=%async_computation.3 | async-start | bytes 16777216 | tf_op jit(solution)/shard_map/all_to_all | solution.py:38
  863.7 19.2 %slice-start = ((s8[8388608]{0:T(1024)(128)(4,1)}), s8[4194304]{0:T(1024)(128)(4,1)S(1)}, s32[]{:S(2)}) async-start(s8[8388608]{0:T(1024)(128)(4,1)} %bitcast.62), calls=%async_computation.4 | async-start | bytes 8388608
  868.2 14.6 %slice-start.1 = ((s8[8388608]{0:T(1024)(128)(4,1)}), s8[4194304]{0:T(1024)(128)(4,1)S(1)}, s32[]{:S(2)}) async-start(s8[8388608]{0:T(1024)(128)(4,1)} %bitcast.62), calls=%async_computation.5 | async-start | bytes 8388608
where the time goes:
time: 910 us; the launch traced here: 901 us
  waiting for transfers between devices  460 us (51%)
  blocking collectives  194 us (21%)
  matrix products  108 us (12%)
  local copies, waits for them, and re-layouts  91.2 us (10%)
  other arithmetic  22.6 us (2%)
  starting transfers between devices  21 us (2%)
    psum x1, blocking collectives, per_device(): total_sum = lax.psum(partial_sum, 'slab')  194 us
    all_to_all x1, waiting for transfers between devices, per_device(): lax.all_to_all(exposure, 'slab', split_axis=1, concat_axis=0, tiled=True)  171 us
    all_to_all x1, waiting for transfers between devices, per_device(): lax.all_to_all(counts, 'slab', split_axis=1, concat_axis=0, tiled=True)  152 us
    all_to_all x1, waiting for transfers between devices, to_lines(): lax.all_to_all(values, 'slab', split_axis=1, concat_axis=0, tiled=True)  137 us
    dot_general x1, matrix products, mode_first(): jnp.einsum('abc,xa->xbc', values, matrix, precision=lax.Precision.HIGHEST)  37.1 us
    unnamed x16, local copies, waits for them, and re-layouts  23.2 us
    dot_general x1, matrix products, adjoint_first(): jnp.einsum('xbc,xa->abc', values, matrix, precision=lax.Precision.HIGHEST)  20.3 us
  transfers between devices with their start and end apart: 4, of which 3 were waited for; matrix products, arithmetic and copies ran while one was open for 10% of the time, Pallas kernels for 0%

commit v1 on v0

v1 whole, which is shorter than its diff:
```python
import functools

import jax
import jax.numpy as jnp
from jax import lax
from jax.experimental import pallas as pl
from jax.experimental.pallas import tpu as pltpu
from jax.sharding import PartitionSpec as P

field_scale = 0.6
layers = 4
chunk_target = 16
lanes = 128
f32, bf16 = jnp.float32, jnp.bfloat16
ANY = pl.BlockSpec(memory_space=pl.ANY)
SMEM = pl.BlockSpec(memory_space=pltpu.SMEM)
params = functools.partial(pltpu.CompilerParams, vmem_limit_bytes=48 * 1024 * 1024)


def split(values):
    high = values.astype(bf16)
    return high, (values - high.astype(f32)).astype(bf16)


def dot(left, right):
    return jnp.dot(left, right, preferred_element_type=f32)


def product(left, right):
    return dot(left[0], right[0]) + (dot(left[0], right[1]) + dot(left[1], right[0]))


def whole(shape):
    return pl.BlockSpec(shape, lambda *_: (0,) * len(shape))


def cost(flops, transferred):
    return pl.CostEstimate(flops=int(flops), bytes_accessed=int(transferred), transcendentals=0)


def fold_rows(values):
    return jnp.sum(values.reshape(-1, 8, values.shape[-1]), axis=0)


def permuted_rows(matrix, bounds, peers):
    rows = matrix.shape[0] // peers
    return jnp.concatenate([matrix[q * rows + low : q * rows + high] for low, high in bounds for q in range(peers)], axis=0)


def field_factors(cholesky_north, cholesky_time, bounds, peers):
    def kernel(north, time, north_high, north_low, time_high, time_low):
        north_high[...], north_low[...] = split(permuted_rows(north[...], bounds, peers))
        time_high[...], time_low[...] = split(time[...].T)

    ny, nt = cholesky_north.shape[0], cholesky_time.shape[0]
    pair = lambda size: [jax.ShapeDtypeStruct((size, size), bf16)] * 2
    return pl.pallas_call(kernel, out_shape=pair(ny) + pair(nt), compiler_params=params(), name="field_factors")(cholesky_north, cholesky_time)


def other_factors(layer, cholesky_east, cholesky_north, cholesky_time, bounds, peers, held_back):
    nx = cholesky_east.shape[0]
    span, half = nx // layers, nx // 2

    def kernel(layer_ref, east, north, time, _, *outs):
        def put(place, values):
            outs[2 * place][...], outs[2 * place + 1][...] = split(values)

        here = layer_ref[0]
        put(0, permuted_rows(north[...], bounds, peers).T)
        put(1, time[...])

        @pl.when(here == 1)
        def _():
            put(2, field_scale * east[half:, :half])

        @pl.when(here != 1)
        def _():
            cross = (field_scale * east[half:, :half]).T
            put(2, jnp.concatenate([cross[span:], cross[:span]], axis=0))

        for z in range(layers):

            @pl.when(here == z)
            def _(z=z):
                own = field_scale * east[z * span : (z + 1) * span, z * span : (z + 1) * span]
                put(3, own)
                put(4, own.T)
                if z % 2:
                    put(5, field_scale * east[z * span : (z + 1) * span, (z - 1) * span : z * span])
                else:
                    put(5, (field_scale * east[(z + 1) * span : (z + 2) * span, z * span : (z + 1) * span]).T)

    ny, nt = cholesky_north.shape[0], cholesky_time.shape[0]
    sizes = (ny, nt, half, span, span, span)
    shapes = [jax.ShapeDtypeStruct((size, size), bf16) for size in sizes for _ in range(2)]
    outs = pl.pallas_call(
        kernel,
        out_shape=shapes,
        in_specs=[SMEM, whole((nx, nx)), whole((ny, ny)), whole((nt, nt)), ANY],
        out_specs=[whole(s.shape) for s in shapes],
        grid=(1,),
        compiler_params=params(),
        name="other_factors",
    )(layer, cholesky_east, cholesky_north, cholesky_time, held_back)
    return [tuple(outs[2 * i : 2 * i + 2]) for i in range(len(sizes))]


def field(whitened, factors, bounds, peers):
    planes, ny, nt = whitened.shape
    step = 8
    counts = [peers * (high - low) for low, high in bounds]
    parts = nt // lanes

    def kernel(w, north_high, north_low, time_high, time_low, *outs):
        squares = outs[-1]
        north = (north_high[...], north_low[...])
        time = (time_high[...], time_low[...])

        @pl.when(pl.program_id(0) == 0)
        def _():
            squares[...] = jnp.zeros_like(squares)

        def one(x, total):
            values = w[x]
            mixed = product(north, split(product(split(values), time)))
            start = 0
            for out, rows in zip(outs[:-1], counts):
                for h in range(parts):
                    out.reshape(rows * parts * step, lanes)[pl.ds(h * step + x, rows, stride=parts * step), :] = mixed[
                        start : start + rows, h * lanes : (h + 1) * lanes
                    ]
                start += rows
            return total + fold_rows(values * values)

        squares[...] += lax.fori_loop(0, step, one, jnp.zeros((8, nt), f32), unroll=2)

    *groups, squares = pl.pallas_call(
        kernel,
        grid=(planes // step,),
        in_specs=[pl.BlockSpec((step, ny, nt), lambda i: (i, 0, 0))] + [whole(f.shape) for f in factors],
        out_specs=[pl.BlockSpec((rows, parts, step, lanes), lambda i: (0, 0, i, 0)) for rows in counts] + [whole((8, nt))],
        out_shape=[jax.ShapeDtypeStruct((rows, parts, planes, lanes), f32) for rows in counts] + [jax.ShapeDtypeStruct((8, nt), f32)],
        compiler_params=params(),
        cost_estimate=cost(12 * planes * ny * nt * nt, 8 * whitened.size),
        name="field",
    )(whitened, *factors)
    return [g.reshape(peers, -1, *g.shape[1:]) for g in groups], squares


def packed(counts, exposure, low, high, peers, held_back):
    planes, ny, nt = counts.shape
    rows, parts = high - low, nt // lanes
    band = 8 if rows % 8 == 0 and low % 8 == 0 and (ny // peers) % 8 == 0 else rows
    per_peer = ny // peers // band

    def kernel(c, e, _, out):
        for h in range(parts):
            out[0, 0, h] = c[:, :, h * lanes : (h + 1) * lanes].astype(f32)
            out[0, 1, h] = e[:, :, h * lanes : (h + 1) * lanes].astype(f32)

    source = pl.BlockSpec((planes, band, nt), lambda q, j: (0, q * per_peer + low // band + j, 0))
    return pl.pallas_call(
        kernel,
        grid=(peers, rows // band),
        in_specs=[source, source, ANY],
        out_specs=pl.BlockSpec((1, 2, parts, planes, band, lanes), lambda q, j: (q, 0, 0, 0, j, 0)),
        out_shape=jax.ShapeDtypeStruct((peers, 2, parts, planes, rows, lanes), f32),
        compiler_params=params(),
        cost_estimate=cost(0, 16 * peers * planes * rows * nt),
        name="packed",
    )(counts, exposure, held_back)


def gate(values, held_back):
    def kernel(_, __, out):
        pass

    return pl.pallas_call(
        kernel,
        in_specs=[ANY, ANY],
        out_specs=ANY,
        out_shape=jax.ShapeDtypeStruct(values.shape, values.dtype),
        input_output_aliases={0: 0},
        name="gate",
    )(values, held_back)


def lines(block):
    peers, _, parts = block.shape[:3]
    return jnp.concatenate([jnp.concatenate([block[q, 0, h] for h in range(parts)], axis=1) for q in range(peers)], axis=0)


def put_lines(out, values):
    peers, _, parts, planes, width = out.shape
    for q in range(peers):
        for h in range(parts):
            out[q, 0, h] = values[q * planes : (q + 1) * planes, h * width : (h + 1) * width]


def rows_of(array, start):
    peers, _, *rest = array.shape
    return pl.BlockSpec((peers, 1, *rest), lambda y: (0, start + y, 0, 0, 0))


def cross_terms(layer, cross, crossed, own_field, own_residual, rows):
    operands, specs = [layer, *cross, crossed], [SMEM, whole(cross[0].shape), whole(cross[1].shape), rows_of(crossed, 0)]
    for pair in (own_field, own_residual):
        if pair is not None:
            operands.append(pair[0])
            specs.append(rows_of(*pair))
    peers, _, parts, planes, _ = crossed.shape
    span, nt = peers * planes, parts * lanes

    def kernel(layer_ref, high, low, moved, *rest):
        near, far = rest[-2:]
        rest = list(rest[:-2])
        here = layer_ref[0]

        def run(first, second):
            result = product((high[...], low[...]), split(jnp.concatenate([lines(first), lines(second)], axis=0)))
            put_lines(near, result[:span])
            put_lines(far, result[span:])

        if own_field is not None:
            own_p = rest.pop(0)

            @pl.when(here == 1)
            def _():
                run(moved, own_p)

        if own_residual is not None:
            own_r = rest.pop(0)

            @pl.when(here == 2)
            def _():
                run(own_r, moved)

    shape = jax.ShapeDtypeStruct((peers, rows, parts, planes, lanes), f32)
    return pl.pallas_call(
        kernel,
        grid=(rows,),
        in_specs=specs,
        out_specs=[rows_of(shape, 0)] * 2,
        out_shape=[shape] * 2,
        compiler_params=params(),
        cost_estimate=cost(6 * 4 * span * span * rows * nt, 20 * span * rows * nt),
        name="cross_terms",
    )(*operands)


def cells(layer, factors, moved, near, far, total, own_field, observed, next_field, old_residual, gradient, rows, held_back):
    own, own_t, beside = factors
    peers, _, parts, planes, _ = moved.shape
    span, nt = peers * planes, parts * lanes
    operands = [layer, *beside, moved, near, far, held_back]
    specs = [SMEM, whole((span, span)), whole((span, span)), rows_of(moved, 0), rows_of(near, 0), rows_of(far, 0), ANY]
    shape = jax.ShapeDtypeStruct((peers, rows, parts, planes, lanes), f32)
    shapes, out_specs, aliases = [], [], {}
    names = ["layer", "beside_high", "beside_low", "moved", "near", "far", "_"]
    out_names = []

    def take(name, array, spec):
        names.append(name)
        operands.append(array)
        specs.append(spec)

    def give(name, struct, spec):
        out_names.append(name)
        shapes.append(struct)
        out_specs.append(spec)

    if own_field is not None:
        take("own_high", own[0], whole((span, span)))
        take("own_low", own[1], whole((span, span)))
        take("field", own_field[0], rows_of(*own_field))
        table, first = observed
        band = 8 if table.shape[4] % 8 == 0 else table.shape[4]
        take("observed", table, pl.BlockSpec((peers, 2, parts, planes, band, lanes), lambda y: (0, 0, 0, 0, (first + y) // band, 0)))
        take("total", total, whole(total.shape))
        if next_field is not None:
            take("next_field", next_field[0], rows_of(*next_field))
            give("send", shape, rows_of(shape, 0))
        give("residual", shape, rows_of(shape, 0))
        give("new_total", jax.ShapeDtypeStruct(total.shape, f32), whole(total.shape))
    if old_residual is not None:
        take("own_t_high", own_t[0], whole((span, span)))
        take("own_t_low", own_t[1], whole((span, span)))
        take("old", old_residual, rows_of(old_residual, 0))
        buffer, high, start = gradient
        struct = jax.ShapeDtypeStruct((peers, high, parts, planes, lanes), f32)
        if buffer is not None:
            aliases[len(operands)] = len(shapes)
            take("buffer", buffer, ANY)
        give("gradient", struct, rows_of(struct, start))

    def kernel(*refs):
        ref = dict(zip(names + out_names, refs))
        here = ref["layer"][0]
        odd, upper = here % 2 == 1, here >= layers // 2
        extra = product((ref["beside_high"][...], ref["beside_low"][...]), split(lines(ref["moved"])))
        partial = jnp.where((here == 1) | (here == 2), lines(ref["near"]), lines(ref["far"]))
        if own_field is not None:
            log_rate = product((ref["own_high"][...], ref["own_low"][...]), split(lines(ref["field"])))
            log_rate += jnp.where(odd, extra, 0.0) + jnp.where(upper, partial, 0.0)
            row = lax.rem(first + pl.program_id(0), band)
            seen = ref["observed"]

            def pick(kind):
                one = lambda q, h: seen.at[q, kind, h].reshape(planes * band, lanes)[pl.ds(row, planes, stride=band), :]
                return jnp.concatenate([jnp.concatenate([one(q, h) for h in range(parts)], axis=1) for q in range(peers)], axis=0)

            observed_counts = pick(0)
            intensity = pick(1) * jnp.exp(log_rate)
            residual = observed_counts - intensity
            put_lines(ref["residual"], residual)

            @pl.when(pl.program_id(0) == 0)
            def _():
                ref["new_total"][...] = ref["total"][...]

            ref["new_total"][...] += fold_rows(observed_counts * log_rate - intensity)
            if next_field is not None:

                @pl.when(odd)
                def _():
                    put_lines(ref["send"], residual)

                @pl.when(jnp.logical_not(odd))
                def _():
                    ref["send"][...] = ref["next_field"][...]

        if old_residual is not None:
            out = product((ref["own_t_high"][...], ref["own_t_low"][...]), split(lines(ref["old"])))
            put_lines(ref["gradient"], out + jnp.where(odd, 0.0, extra) + jnp.where(upper, 0.0, partial))

    outs = pl.pallas_call(
        kernel,
        grid=(rows,),
        in_specs=specs,
        out_specs=out_specs,
        out_shape=shapes,
        input_output_aliases=aliases,
        compiler_params=params(),
        cost_estimate=cost(6 * 3 * span * span * rows * nt, 40 * span * rows * nt),
        name="cells",
    )(*operands)
    return dict(zip(out_names, outs))


def finish(groups, whitened, north, time):
    planes, ny, nt = whitened.shape
    step = 8
    flat = [g.reshape(-1, *g.shape[2:]) for g in groups]
    counts = [g.shape[0] for g in flat]
    parts = nt // lanes

    def kernel(w, north_high, north_low, time_high, time_low, *refs):
        out = refs[-1]
        north_pair = (north_high[...], north_low[...])
        time_pair = (time_high[...], time_low[...])

        def one(x, carry):
            line = lambda ref, rows, h: ref.reshape(rows * parts * step, lanes)[pl.ds(h * step + x, rows, stride=parts * step), :]
            values = jnp.concatenate(
                [jnp.concatenate([line(ref, rows, h) for h in range(parts)], axis=1) for ref, rows in zip(refs[:-1], counts)], axis=0
            )
            out[x] = product(north_pair, split(product(split(values), time_pair))) - w[x]
            return carry

        lax.fori_loop(0, step, one, 0, unroll=2)

    planes_block = pl.BlockSpec((step, ny, nt), lambda i: (i, 0, 0))
    return pl.pallas_call(
        kernel,
        grid=(planes // step,),
        in_specs=[planes_block] + [whole(f.shape) for f in (*north, *time)] + [pl.BlockSpec((rows, parts, step, lanes), lambda i: (0, 0, i, 0)) for rows in counts],
        out_specs=planes_block,
        out_shape=jax.ShapeDtypeStruct(whitened.shape, f32),
        compiler_params=params(),
        cost_estimate=cost(12 * planes * ny * nt * nt, 12 * whitened.size),
        name="finish",
    )(whitened, *north, *time, *flat)


def bounds_of(eighths, rows, unit):
    ends = sorted({min(rows, max(unit, rows * e // 8 // unit * unit)) for e in eighths} | {rows})
    return list(zip([0] + ends[:-1], ends))


def containing(bounds, row):
    return next(i for i, (low, high) in enumerate(bounds) if low <= row < high)


def per_device(whitened, counts, exposure, cholesky_east, cholesky_north, cholesky_time):
    devices = lax.axis_size("slab")
    peers = devices // layers
    planes, ny, nt = whitened.shape
    rows = ny // peers
    chunk = max(1, rows // chunk_target)
    number = rows // chunk
    unit = 8 if rows % 8 == 0 else rows
    layer = jnp.reshape(lax.axis_index("slab") // peers, (1,)).astype(jnp.int32)
    in_layer = [[z * peers + q for q in range(peers)] for z in range(layers)]

    def exchange(values):
        return lax.all_to_all(values, "slab", 0, 0, tiled=True, axis_index_groups=in_layer)

    def move(values, pairs):
        return lax.ppermute(values, "slab", [(a * peers + q, b * peers + q) for a, b in pairs for q in range(peers)])

    field_bounds = bounds_of((1, 4), rows, unit)
    cell_bounds = bounds_of((1, 2, 3, 4, 5, 6, 7), rows, unit)
    gradient_bounds = bounds_of((3, 5, 7), rows, chunk)

    tables = [packed(counts, exposure, *cell_bounds[0], peers, whitened)]
    tables[0] = exchange(tables[0])
    groups, squares = field(whitened, field_factors(cholesky_north, cholesky_time, field_bounds, peers), field_bounds, peers)
    fields = [exchange(g) for g in groups]
    north, time, cross, *blocks = other_factors(layer, cholesky_east, cholesky_north, cholesky_time, gradient_bounds, peers, squares)

    def field_chunk(c):
        g = containing(field_bounds, c * chunk)
        return fields[g], c * chunk - field_bounds[g][0]

    def field_slice(c):
        array, start = field_chunk(c)
        return lax.slice_in_dim(array, start, start + chunk, axis=1)

    total = -0.5 * squares
    crossed, residuals, nears, fars = {}, {}, {}, {}
    buffers, results = {}, {}

    def do_cross(k):
        own_field = field_chunk(k) if k < number else None
        own_residual = (residuals[k - 2], 0) if k >= 2 else None
        near, far = cross_terms(layer, cross, crossed[k], own_field, own_residual, chunk)
        forward, backward = k < number, k >= 2
        nears[k + 1] = move(near, [(1, 2)] * forward + [(2, 1)] * backward)
        fars[k + 1] = move(far, [(1, 3)] * forward + [(2, 0)] * backward)
        return near

    for k in (0, 1):
        crossed[k] = move(field_slice(k), [(0, 1), (2, 3)])
    done = do_cross(0)
    done = do_cross(1)
    for k in range(1, number + 3):
        c, g = k - 1, k - 3
        own_field = observed = next_field = old = gradient = None
        if c < number:
            own_field = field_chunk(c)
            t = containing(cell_bounds, c * chunk)
            while len(tables) <= t:
                held = residuals[c - 2 * unit // chunk] if c >= 2 * unit // chunk else done
                tables.append(exchange(packed(counts, exposure, *cell_bounds[len(tables)], peers, held)))
            observed = (tables[t], c * chunk - cell_bounds[t][0])
            if k + 1 < number:
                next_field = field_chunk(k + 1)
        if g >= 0:
            old = residuals[g]
            h = containing(gradient_bounds, g * chunk)
            low, high = gradient_bounds[h]
            gradient = (buffers.get(h), high - low, g * chunk - low)
        outs = cells(layer, blocks, crossed[k - 1], nears[k], fars[k], total, own_field, observed, next_field, old, gradient, chunk, done)
        if c < number:
            residuals[c], total = outs["residual"], outs["new_total"]
        if g >= 0:
            buffers[h] = outs["gradient"]
            if (g + 1) * chunk == high:
                results[h] = exchange(buffers[h])
        if k + 1 < number:
            crossed[k + 1] = move(outs["send"], [(0, 1), (2, 3), (1, 0), (3, 2)])
        elif k + 1 < number + 2:
            crossed[k + 1] = move(outs["residual"], [(1, 0), (3, 2)])
        if k + 1 in crossed:
            done = do_cross(k + 1)
    cell_count = planes * ny * nt * devices
    density = lax.psum(jnp.sum(total), "slab") / cell_count
    gradient = finish([results[h] for h in range(len(gradient_bounds))], whitened, north, time)
    return gradient, jnp.reshape(density, (1,))


def solution(mesh):
    placed = P(("chain", "slab"), None, None)
    return jax.shard_map(
        per_device,
        mesh=mesh,
        in_specs=(placed, placed, placed, P(), P(), P()),
        out_specs=(placed, P("chain")),
        check_vma=False,
    )
```

time: 910 us -> 912 us (level)
  Pallas kernels: 0 us -> 182 us
  starting transfers between devices: 21 us -> 196 us
  matrix products: 108 us -> 0 us
  waiting for transfers between devices: 460 us -> 356 us
  blocking collectives: 194 us -> 130 us
  local copies, waits for them, and re-layouts: 91.2 us -> 29.9 us
  other arithmetic: 22.6 us -> 0.6 us
    all_to_all x4 -> x12, waiting for transfers between devices: 460 us -> 34 us  [exchange(): lax.all_to_all(values, 'slab', 0, 0, tiled=True, axis_index_groups=in_layer)]
    ppermute x0 -> x54, waiting for transfers between devices: none -> 322 us  [move(): lax.ppermute(values, 'slab', [(a * peers + q, b * peers + q) for a, b in...]
    pallas_call x0 -> x48, Pallas kernels: none -> 182 us  [the longest x18 87.8 us: cells(): pl.pallas_call(kernel, grid=(rows,), in_specs=specs, out_specs=out_specs,...]
    psum x1, blocking collectives: 194 us -> 31.1 us  [per_device(): density = lax.psum(jnp.sum(total), 'slab') / cell_count]
    ppermute x0 -> x54, starting transfers between devices: none -> 144 us  [move(): lax.ppermute(values, 'slab', [(a * peers + q, b * peers + q) for a, b in...]
    dot_general x6 -> x0, matrix products: 108 us -> none  [the longest x1 37.1 us: mode_first(): jnp.einsum('abc,xa->xbc', values, matrix, precision=lax.Precision.HIGHEST)]
    all_to_all x0 -> x3, blocking collectives: none -> 98.4 us  [exchange(): lax.all_to_all(values, 'slab', 0, 0, tiled=True, axis_index_groups=in_layer)]
    all_to_all x4 -> x12, starting transfers between devices: 21 us -> 52.2 us  [exchange(): lax.all_to_all(values, 'slab', 0, 0, tiled=True, axis_index_groups=in_layer)]
  transfers between devices with their start and end apart: 4 -> 66, of which waited for: 3 -> 53; matrix products, arithmetic and copies ran while one was open for 10% -> 0% of each run, Pallas kernels for 0% -> 16%
where the time goes in v1:
time: 912 us; the launch traced here: 897 us
  waiting for transfers between devices  356 us (39%)
  starting transfers between devices  196 us (21%)
  Pallas kernels  182 us (20%)
  blocking collectives  130 us (14%)
  local copies, waits for them, and re-layouts  29.9 us (3%)
    ppermute x54, waiting for transfers between devices, move(): lax.ppermute(values, 'slab', [(a * peers + q, b * peers + q) for a, b in...  322 us
    ppermute x54, starting transfers between devices, move(): lax.ppermute(values, 'slab', [(a * peers + q, b * peers + q) for a, b in...  144 us
    all_to_all x3, blocking collectives, exchange(): lax.all_to_all(values, 'slab', 0, 0, tiled=True, axis_index_groups=in_layer)  98.4 us
    pallas_call x18, Pallas kernels, cells(): pl.pallas_call(kernel, grid=(rows,), in_specs=specs, out_specs=out_specs,...  87.8 us
    all_to_all x12, starting transfers between devices, exchange(): lax.all_to_all(values, 'slab', 0, 0, tiled=True, axis_index_groups=in_layer)  52.2 us
    pallas_call x18, Pallas kernels, cross_terms(): pl.pallas_call(kernel, grid=(rows,), in_specs=specs, out_specs=[rows_of(s...  35.6 us
    all_to_all x12, waiting for transfers between devices, exchange(): lax.all_to_all(values, 'slab', 0, 0, tiled=True, axis_index_groups=in_layer)  34 us
    psum x1, blocking collectives, per_device(): density = lax.psum(jnp.sum(total), 'slab') / cell_count  31.1 us
  transfers between devices with their start and end apart: 66, of which 53 were waited for; matrix products, arithmetic and copies ran while one was open for 0% of the time, Pallas kernels for 16%

profile of v1, /device:TPU:18, one launch (start us, length us, event | category | flops | bytes accessed | tf_op | source)
XLA Modules:
  0.0 897.4 jit_solution(10424810626021446519)
XLA Ops:
  2.7 17.9 %field.1 = (f32[32,2,32,128]{3,2,1,0:T(8,128)}, f32[96,2,32,128]{3,2,1,0:T(8,128)S(1)}, f32[128,2,32,128]{3,2,1,0:T(8,128)}, f32[8,256]{1,0:T(8,128)S(1)}) custom-call(f32[32,256,256]{2,1,0:T(8,128)} %w.3, bf16[256,256]{1,0:T(8,128)(2,1)S(1)} %get-tuple-element.118.north_high, bf16[256,256]{1,0:T(8,128)(2,1)S(1)} %get-tuple-element.119.north_low, ...), custom_call_target="tpu_custom_call" | custom-call | flops 6442450944 | bytes 16777216 | tf_op jit(solution)/shard_map/field/pallas_call | solution.py:137
  28.2 12.0 %all-to-all-done.rest_0_.refs_9_ = f32[4,8,2,32,128]{4,3,2,1,0:T(8,128)S(1)} async-done(((f32[4,8,2,32,128]{4,3,2,1,0:T(8,128)}), f32[4,8,2,32,128]{4,3,2,1,0:T(8,128)S(1)}, u32[]{:S(2)}, u32[]{:S(2)}) %all-to-all-start) | async-done | bytes 1048608 | tf_op jit(solution)/shard_map/all_to_all | solution.py:406
  40.3 29.2 %all_to_all.75.refs_10_ = f32[4,2,2,32,8,128]{5,4,3,2,1,0:T(8,128)} all-to-all(f32[4,2,2,32,8,128]{5,4,3,2,1,0:T(8,128)S(1)} %packed.8), channel_id=1, replica_groups={{0,1,2,3},{4,5,6,7},{8,9,10,11},{12,13,14,15},{16,17,18,19},{20,21,22,2..., dimensions={0} | all-to-all | bytes 4194304 | tf_op jit(solution)/shard_map/all_to_all | solution.py:406
  69.5 40.3 %all_to_all.76.refs_12_.rest_0_.refs_9_ = f32[4,24,2,32,128]{4,3,2,1,0:T(8,128)} all-to-all(f32[4,24,2,32,128]{4,3,2,1,0:T(8,128)S(1)} %bitcast.10), channel_id=1, replica_groups={{0,1,2,3},{4,5,6,7},{8,9,10,11},{12,13,14,15},{16,17,18,19},{20,21,22,2..., dimensions={0} | all-to-all | bytes 6291456 | tf_op jit(solution)/shard_map/all_to_all | solution.py:406
  109.7 4.9 all-to-all-start.6
  121.1 10.7 %collective-permute-done.3.moved.refs_3_ = f32[4,4,2,32,128]{4,3,2,1,0:T(8,128)S(1)} collective-permute-done((f32[4,4,2,32,128]{4,3,2,1,0:T(8,128)}, f32[4,4,2,32,128]{4,3,2,1,0:T(8,128)S(1)}, u32[]{:S(2)}, u32[]{:S(2)}) %collective-permute-start.3) | collective-permute-done | bytes 524320 | tf_op jit(solution)/shard_map/ppermute | solution.py:409
  134.0 8.5 collective-permute-done.moved.refs_3_
  142.8 6.0 collective-permute-done.4.refs_4_
  154.0 10.9 %collective-permute-start.6 = (f32[4,4,2,32,128]{4,3,2,1,0:T(8,128)S(1)}, f32[4,4,2,32,128]{4,3,2,1,0:T(8,128)S(1)}, u32[]{:S(2)}, u32[]{:S(2)}) collective-permute-start(f32[4,4,2,32,128]{4,3,2,1,0:T(8,128)S(1)} %get-tuple-element.139), channel_id=1, source_target_pairs={{0,4},{1,5},{2,6},{3,7},{8,12},{9,13},{10,14},{11,15},{4,0},{5,1},... | collective-permute-start | bytes 1572872 | tf_op jit(solution)/shard_map/ppermute | solution.py:409
  166.9 8.4 collective-permute-done.6.moved.refs_3_
  176.7 4.9 collective-permute-done.1.refs_4_
  185.7 9.7 %collective-permute-start.7 = (f32[4,4,2,32,128]{4,3,2,1,0:T(8,128)S(1)}, f32[4,4,2,32,128]{4,3,2,1,0:T(8,128)S(1)}, u32[]{:S(2)}, u32[]{:S(2)}) collective-permute-start(f32[4,4,2,32,128]{4,3,2,1,0:T(8,128)S(1)} %get-tuple-element.143), channel_id=1, source_target_pairs={{0,4},{1,5},{2,6},{3,7},{8,12},{9,13},{10,14},{11,15},{4,0},{5,1},... | collective-permute-start | bytes 1572872 | tf_op jit(solution)/shard_map/ppermute | solution.py:409
  195.4 9.2 %collective-permute-done.7.moved.refs_3_ = f32[4,4,2,32,128]{4,3,2,1,0:T(8,128)S(1)} collective-permute-done((f32[4,4,2,32,128]{4,3,2,1,0:T(8,128)S(1)}, f32[4,4,2,32,128]{4,3,2,1,0:T(8,128)S(1)}, u32[]{:S(2)}, u32[]{:S(2)}) %collective-permute-start.7) | collective-permute-done | bytes 524320 | tf_op jit(solution)/shard_map/ppermute | solution.py:409
  218.7 21.9 %all-to-all-done.3.refs_10_ = f32[4,2,2,32,8,128]{5,4,3,2,1,0:T(8,128)S(1)} async-done(((f32[4,2,2,32,8,128]{5,4,3,2,1,0:T(8,128)}), f32[4,2,2,32,8,128]{5,4,3,2,1,0:T(8,128)S(1)}, u32[]{:S(2)}, u32[]{:S(2)}) %all-to-all-start.3) | async-done | bytes 2097184 | tf_op jit(solution)/shard_map/all_to_all | solution.py:406
  248.4 13.6 %collective-permute-done.10.refs_4_ = f32[4,4,2,32,128]{4,3,2,1,0:T(8,128)S(1)} collective-permute-done((f32[4,4,2,32,128]{4,3,2,1,0:T(8,128)}, f32[4,4,2,32,128]{4,3,2,1,0:T(8,128)S(1)}, u32[]{:S(2)}, u32[]{:S(2)}) %collective-permute-start.10) | collective-permute-done | bytes 524320 | tf_op jit(solution)/shard_map/ppermute | solution.py:409
  261.9 8.7 collective-permute-done.11.refs_5_
  294.8 8.9 collective-permute-done.12.moved.refs_3_
  308.0 8.3 collective-permute-done.9.refs_5_
  316.3 4.9 cells.21
  328.3 7.8 collective-permute-done.13.moved.refs_3_
  341.5 7.0 collective-permute-done.17.refs_5_
  348.5 5.5 cells.22
  371.4 8.9 collective-permute-done.18.moved.refs_3_
  384.5 8.4 collective-permute-done.15.refs_5_
  392.9 5.6 cells.23
  405.8 7.5 collective-permute-done.19.moved.refs_3_
  418.7 7.1 collective-permute-done.23.refs_5_
  425.8 5.4 cells.24
  447.7 8.8 collective-permute-done.24.moved.refs_3_
  460.6 8.4 collective-permute-done.21.refs_5_
  469.0 5.5 cells.25
  481.6 7.6 collective-permute-done.25.moved.refs_3_
  494.6 7.1 collective-permute-done.29.refs_5_
  501.8 5.5 cells.26
  509.7 29.0 %all_to_all.77.refs_10_ = f32[4,2,2,32,8,128]{5,4,3,2,1,0:T(8,128)} all-to-all(f32[4,2,2,32,8,128]{5,4,3,2,1,0:T(8,128)S(1)} %packed.14), channel_id=1, replica_groups={{0,1,2,3},{4,5,6,7},{8,9,10,11},{12,13,14,15},{16,17,18,19},{20,21,22,2..., dimensions={0} | all-to-all | bytes 4194304 | tf_op jit(solution)/shard_map/all_to_all | solution.py:406
  538.7 4.8 all-to-all-start.7
  550.9 8.8 collective-permute-done.30.moved.refs_3_
  563.7 8.5 collective-permute-done.27.refs_5_
  572.1 5.5 cells.27
  584.7 7.6 collective-permute-done.31.moved.refs_3_
  597.7 7.2 collective-permute-done.35.refs_5_
  604.9 5.5 cells.28
  626.9 8.9 collective-permute-done.36.moved.refs_3_
  639.8 8.4 collective-permute-done.33.refs_5_
  648.2 5.4 cells.29
  660.8 7.5 collective-permute-done.37.moved.refs_3_
  673.8 7.2 collective-permute-done.41.refs_5_
  681.0 5.5 cells.30
  707.7 6.1 collective-permute-done.39.refs_5_
  713.8 5.6 cells.31
  726.8 5.4 collective-permute-done.43.moved.refs_3_
  739.5 4.9 collective-permute-done.47.refs_5_
  744.4 5.3 cells.32
  751.0 6.5 collective-permute-start.44
  764.2 6.2 collective-permute-done.44.refs_4_
  770.3 5.1 collective-permute-done.45.refs_5_
  775.4 5.3 cells.33
  787.3 6.5 collective-permute-start.52
  795.1 7.0 collective-permute-done.49.moved.refs_3_
  808.4 9.1 %collective-permute-done.53.refs_5_ = f32[4,4,2,32,128]{4,3,2,1,0:T(8,128)S(1)} collective-permute-done((f32[4,4,2,32,128]{4,3,2,1,0:T(8,128)}, f32[4,4,2,32,128]{4,3,2,1,0:T(8,128)S(1)}, u32[]{:S(2)}, u32[]{:S(2)}) %collective-permute-start.53) | collective-permute-done | bytes 524320 | tf_op jit(solution)/shard_map/ppermute | solution.py:409
  821.9 6.8 collective-permute-done.50.refs_4_
  828.7 10.5 %collective-permute-done.51.refs_5_ = f32[4,4,2,32,128]{4,3,2,1,0:T(8,128)S(1)} collective-permute-done((f32[4,4,2,32,128]{4,3,2,1,0:T(8,128)S(1)}, f32[4,4,2,32,128]{4,3,2,1,0:T(8,128)S(1)}, u32[]{:S(2)}, u32[]{:S(2)}) %collective-permute-start.51) | collective-permute-done | bytes 524320 | tf_op jit(solution)/shard_map/ppermute | solution.py:409
  846.5 31.1 %psum.7 = f32[]{:T(128)} all-reduce(f32[]{:T(128)} %reduce_sum.9), channel_id=1, replica_groups=mesh['chain'=2,'slab'=16] {'slab'}, use_global_device_ids=true, to_apply=%region_1.2 | all-reduce | flops 1 | bytes 8 | tf_op jit(solution)/shard_map/psum | solution.py:477
  878.3 17.9 %finish.1 = f32[32,256,256]{2,1,0:T(8,128)} custom-call(f32[32,256,256]{2,1,0:T(8,128)} %w.3, bf16[256,256]{1,0:T(8,128)(2,1)S(1)} %copy-done.71, bf16[256,256]{1,0:T(8,128)(2,1)S(1)} %copy-done.73, bf16[256,256]{1,0:T(8,128)(2,1)S(1)} %copy-done.75, bf16[256,256]{1,0:T(8,128)(2,1)S(1)} %copy-done.77, f32[96,2,32,128]{3,2,1,0:T(8,128)} %bitcast.4.refs_0_, ...), custom_call_target="tpu_custom_call" | custom-call | flops 6442450944 | bytes 25165824 | tf_op jit(solution)/shard_map/finish/pallas_call | solution.py:373
  (303 shorter events, 289.5 us)
Async XLA Ops:
  22.3 18.0 %all-to-all-start = ((f32[4,8,2,32,128]{4,3,2,1,0:T(8,128)}), f32[4,8,2,32,128]{4,3,2,1,0:T(8,128)S(1)}, u32[]{:S(2)}, u32[]{:S(2)}) async-start(f32[4,8,2,32,128]{4,3,2,1,0:T(8,128)} %bitcast.1), calls=%async_computation | async-start | bytes 2097152 | tf_op jit(solution)/shard_map/all_to_all | solution.py:406
  109.7 101.6 %all-to-all-start.6 = ((f32[4,32,2,32,128]{4,3,2,1,0:T(8,128)}), f32[4,32,2,32,128]{4,3,2,1,0:T(8,128)}, u32[]{:S(2)}, u32[]{:S(2)}) async-start(f32[4,32,2,32,128]{4,3,2,1,0:T(8,128)} %bitcast.11), calls=%async_computation.6 | async-start | bytes 8388608 | tf_op jit(solution)/shard_map/all_to_all | solution.py:406
  115.7 16.0 %collective-permute-start.3 = (f32[4,4,2,32,128]{4,3,2,1,0:T(8,128)}, f32[4,4,2,32,128]{4,3,2,1,0:T(8,128)S(1)}, u32[]{:S(2)}, u32[]{:S(2)}) collective-permute-start(f32[4,4,2,32,128]{4,3,2,1,0:T(8,128)} %get-tuple-element.234), channel_id=1, source_target_pairs={{0,4},{1,5},{2,6},{3,7},{8,12},{9,13},{10,14},{11,15},{16,20},{17,... | collective-permute-start | bytes 1572872 | tf_op jit(solution)/shard_map/ppermute | solution.py:409
  119.7 22.8 %collective-permute-start = (f32[4,4,2,32,128]{4,3,2,1,0:T(8,128)}, f32[4,4,2,32,128]{4,3,2,1,0:T(8,128)S(1)}, u32[]{:S(2)}, u32[]{:S(2)}) collective-permute-start(f32[4,4,2,32,128]{4,3,2,1,0:T(8,128)} %get-tuple-element.235), channel_id=1, source_target_pairs={{0,4},{1,5},{2,6},{3,7},{8,12},{9,13},{10,14},{11,15},{16,20},{17,... | collective-permute-start | bytes 1572872 | tf_op jit(solution)/shard_map/ppermute | solution.py:409
  132.0 16.8 %collective-permute-start.4 = (f32[4,4,2,32,128]{4,3,2,1,0:T(8,128)S(1)}, f32[4,4,2,32,128]{4,3,2,1,0:T(8,128)S(1)}, u32[]{:S(2)}, u32[]{:S(2)}) collective-permute-start(f32[4,4,2,32,128]{4,3,2,1,0:T(8,128)S(1)} %get-tuple-element.134), channel_id=1, source_target_pairs={{4,8},{5,9},{6,10},{7,11},{20,24},{21,25},{22,26},{23,27}} | collective-permute-start | bytes 1572872 | tf_op jit(solution)/shard_map/ppermute | solution.py:409
  133.3 15.5 %collective-permute-start.5 = (f32[4,4,2,32,128]{4,3,2,1,0:T(8,128)S(1)}, f32[4,4,2,32,128]{4,3,2,1,0:T(8,128)S(1)}, u32[]{:S(2)}, u32[]{:S(2)}) collective-permute-start(f32[4,4,2,32,128]{4,3,2,1,0:T(8,128)S(1)} %get-tuple-element.135), channel_id=1, source_target_pairs={{4,12},{5,13},{6,14},{7,15},{20,28},{21,29},{22,30},{23,31}} | collective-permute-start | bytes 1572872 | tf_op jit(solution)/shard_map/ppermute | solution.py:409
  154.0 21.3 %collective-permute-start.6 = (f32[4,4,2,32,128]{4,3,2,1,0:T(8,128)S(1)}, f32[4,4,2,32,128]{4,3,2,1,0:T(8,128)S(1)}, u32[]{:S(2)}, u32[]{:S(2)}) collective-permute-start(f32[4,4,2,32,128]{4,3,2,1,0:T(8,128)S(1)} %get-tuple-element.139), channel_id=1, source_target_pairs={{0,4},{1,5},{2,6},{3,7},{8,12},{9,13},{10,14},{11,15},{4,0},{5,1},... | collective-permute-start | bytes 1572872 | tf_op jit(solution)/shard_map/ppermute | solution.py:409
  164.9 16.7 %collective-permute-start.1 = (f32[4,4,2,32,128]{4,3,2,1,0:T(8,128)S(1)}, f32[4,4,2,32,128]{4,3,2,1,0:T(8,128)S(1)}, u32[]{:S(2)}, u32[]{:S(2)}) collective-permute-start(f32[4,4,2,32,128]{4,3,2,1,0:T(8,128)S(1)} %get-tuple-element.132.refs_6_), channel_id=1, source_target_pairs={{4,8},{5,9},{6,10},{7,11},{20,24},{21,25},{22,26},{23,27}} | collective-permute-start | bytes 1572872 | tf_op jit(solution)/shard_map/ppermute | solution.py:409
  166.2 15.5 %collective-permute-start.2 = (f32[4,4,2,32,128]{4,3,2,1,0:T(8,128)S(1)}, f32[4,4,2,32,128]{4,3,2,1,0:T(8,128)S(1)}, u32[]{:S(2)}, u32[]{:S(2)}) collective-permute-start(f32[4,4,2,32,128]{4,3,2,1,0:T(8,128)S(1)} %get-tuple-element.133), channel_id=1, source_target_pairs={{4,12},{5,13},{6,14},{7,15},{20,28},{21,29},{22,30},{23,31}} | collective-permute-start | bytes 1572872 | tf_op jit(solution)/shard_map/ppermute | solution.py:409
  185.7 18.9 %collective-permute-start.7 = (f32[4,4,2,32,128]{4,3,2,1,0:T(8,128)S(1)}, f32[4,4,2,32,128]{4,3,2,1,0:T(8,128)S(1)}, u32[]{:S(2)}, u32[]{:S(2)}) collective-permute-start(f32[4,4,2,32,128]{4,3,2,1,0:T(8,128)S(1)} %get-tuple-element.143), channel_id=1, source_target_pairs={{0,4},{1,5},{2,6},{3,7},{8,12},{9,13},{10,14},{11,15},{4,0},{5,1},... | collective-permute-start | bytes 1572872 | tf_op jit(solution)/shard_map/ppermute | solution.py:409
  211.4 29.3 %all-to-all-start.3 = ((f32[4,2,2,32,8,128]{5,4,3,2,1,0:T(8,128)}), f32[4,2,2,32,8,128]{5,4,3,2,1,0:T(8,128)S(1)}, u32[]{:S(2)}, u32[]{:S(2)}) async-start(f32[4,2,2,32,8,128]{5,4,3,2,1,0:T(8,128)} %copy-done.24), calls=%async_computation.3 | async-start | bytes 4194304 | tf_op jit(solution)/shard_map/all_to_all | solution.py:406
  240.6 42.1 %all-to-all-start.4 = ((f32[4,2,2,32,8,128]{5,4,3,2,1,0:T(8,128)}), f32[4,2,2,32,8,128]{5,4,3,2,1,0:T(8,128)}, u32[]{:S(2)}, u32[]{:S(2)}) async-start(f32[4,2,2,32,8,128]{5,4,3,2,1,0:T(8,128)} %copy-done.23), calls=%async_computation.4 | async-start | bytes 4194304 | tf_op jit(solution)/shard_map/all_to_all | solution.py:406
  245.1 16.8 %collective-permute-start.10 = (f32[4,4,2,32,128]{4,3,2,1,0:T(8,128)}, f32[4,4,2,32,128]{4,3,2,1,0:T(8,128)S(1)}, u32[]{:S(2)}, u32[]{:S(2)}) collective-permute-start(f32[4,4,2,32,128]{4,3,2,1,0:T(8,128)} %copy-done.60), channel_id=1, source_target_pairs={{4,8},{5,9},{6,10},{7,11},{8,4},{9,5},{10,6},{11,7},{20,24},{21,25... | collective-permute-start | bytes 1572872 | tf_op jit(solution)/shard_map/ppermute | solution.py:409
  247.0 23.6 %collective-permute-start.11 = (f32[4,4,2,32,128]{4,3,2,1,0:T(8,128)}, f32[4,4,2,32,128]{4,3,2,1,0:T(8,128)S(1)}, u32[]{:S(2)}, u32[]{:S(2)}) collective-permute-start(f32[4,4,2,32,128]{4,3,2,1,0:T(8,128)} %copy-done.80), channel_id=1, source_target_pairs={{4,12},{5,13},{6,14},{7,15},{8,0},{9,1},{10,2},{11,3},{20,28},{21,... | collective-permute-start | bytes 1572872 | tf_op jit(solution)/shard_map/ppermute | solution.py:409
  282.7 76.5 %all-to-all-start.5 = ((f32[4,2,2,32,8,128]{5,4,3,2,1,0:T(8,128)}), f32[4,2,2,32,8,128]{5,4,3,2,1,0:T(8,128)}, u32[]{:S(2)}, u32[]{:S(2)}) async-start(f32[4,2,2,32,8,128]{5,4,3,2,1,0:T(8,128)} %copy-done.21), calls=%async_computation.5 | async-start | bytes 4194304 | tf_op jit(solution)/shard_map/all_to_all | solution.py:406
  287.5 16.3 %collective-permute-start.12 = (f32[4,4,2,32,128]{4,3,2,1,0:T(8,128)}, f32[4,4,2,32,128]{4,3,2,1,0:T(8,128)S(1)}, u32[]{:S(2)}, u32[]{:S(2)}) collective-permute-start(f32[4,4,2,32,128]{4,3,2,1,0:T(8,128)} %copy-done.89), channel_id=1, source_target_pairs={{0,4},{1,5},{2,6},{3,7},{8,12},{9,13},{10,14},{11,15},{4,0},{5,1},... | collective-permute-start | bytes 1572872 | tf_op jit(solution)/shard_map/ppermute | solution.py:409
  291.1 16.9 %collective-permute-start.8 = (f32[4,4,2,32,128]{4,3,2,1,0:T(8,128)}, f32[4,4,2,32,128]{4,3,2,1,0:T(8,128)S(1)}, u32[]{:S(2)}, u32[]{:S(2)}) collective-permute-start(f32[4,4,2,32,128]{4,3,2,1,0:T(8,128)} %copy-done.35), channel_id=1, source_target_pairs={{4,8},{5,9},{6,10},{7,11},{8,4},{9,5},{10,6},{11,7},{20,24},{21,25... | collective-permute-start | bytes 1572872 | tf_op jit(solution)/shard_map/ppermute | solution.py:409
  293.4 22.9 %collective-permute-start.9 = (f32[4,4,2,32,128]{4,3,2,1,0:T(8,128)}, f32[4,4,2,32,128]{4,3,2,1,0:T(8,128)S(1)}, u32[]{:S(2)}, u32[]{:S(2)}) collective-permute-start(f32[4,4,2,32,128]{4,3,2,1,0:T(8,128)} %copy-done.78), channel_id=1, source_target_pairs={{4,12},{5,13},{6,14},{7,15},{8,0},{9,1},{10,2},{11,3},{20,28},{21,... | collective-permute-start | bytes 1572872 | tf_op jit(solution)/shard_map/ppermute | solution.py:409
  321.2 14.8 %collective-permute-start.13 = (f32[4,4,2,32,128]{4,3,2,1,0:T(8,128)S(1)}, f32[4,4,2,32,128]{4,3,2,1,0:T(8,128)S(1)}, u32[]{:S(2)}, u32[]{:S(2)}) collective-permute-start(f32[4,4,2,32,128]{4,3,2,1,0:T(8,128)S(1)} %get-tuple-element.156), channel_id=1, source_target_pairs={{0,4},{1,5},{2,6},{3,7},{8,12},{9,13},{10,14},{11,15},{4,0},{5,1},... | collective-permute-start | bytes 1572872 | tf_op jit(solution)/shard_map/ppermute | solution.py:409
  324.7 16.7 %collective-permute-start.16 = (f32[4,4,2,32,128]{4,3,2,1,0:T(8,128)S(1)}, f32[4,4,2,32,128]{4,3,2,1,0:T(8,128)S(1)}, u32[]{:S(2)}, u32[]{:S(2)}) collective-permute-start(f32[4,4,2,32,128]{4,3,2,1,0:T(8,128)S(1)} %get-tuple-element.153.refs_6_), channel_id=1, source_target_pairs={{4,8},{5,9},{6,10},{7,11},{8,4},{9,5},{10,6},{11,7},{20,24},{21,25... | collective-permute-start | bytes 1572872 | tf_op jit(solution)/shard_map/ppermute | solution.py:409
  327.0 21.5 %collective-permute-start.17 = (f32[4,4,2,32,128]{4,3,2,1,0:T(8,128)S(1)}, f32[4,4,2,32,128]{4,3,2,1,0:T(8,128)S(1)}, u32[]{:S(2)}, u32[]{:S(2)}) collective-permute-start(f32[4,4,2,32,128]{4,3,2,1,0:T(8,128)S(1)} %get-tuple-element.160), channel_id=1, source_target_pairs={{4,12},{5,13},{6,14},{7,15},{8,0},{9,1},{10,2},{11,3},{20,28},{21,... | collective-permute-start | bytes 1572872 | tf_op jit(solution)/shard_map/ppermute | solution.py:409
  359.2 76.6 %all-to-all-start.8 = ((f32[4,2,2,32,8,128]{5,4,3,2,1,0:T(8,128)}), f32[4,2,2,32,8,128]{5,4,3,2,1,0:T(8,128)}, u32[]{:S(2)}, u32[]{:S(2)}) async-start(f32[4,2,2,32,8,128]{5,4,3,2,1,0:T(8,128)} %copy-done.22), calls=%async_computation.8 | async-start | bytes 4194304 | tf_op jit(solution)/shard_map/all_to_all | solution.py:406
  364.0 16.3 %collective-permute-start.18 = (f32[4,4,2,32,128]{4,3,2,1,0:T(8,128)}, f32[4,4,2,32,128]{4,3,2,1,0:T(8,128)S(1)}, u32[]{:S(2)}, u32[]{:S(2)}) collective-permute-start(f32[4,4,2,32,128]{4,3,2,1,0:T(8,128)} %copy-done.86), channel_id=1, source_target_pairs={{0,4},{1,5},{2,6},{3,7},{8,12},{9,13},{10,14},{11,15},{4,0},{5,1},... | collective-permute-start | bytes 1572872 | tf_op jit(solution)/shard_map/ppermute | solution.py:409
  367.6 16.9 %collective-permute-start.14 = (f32[4,4,2,32,128]{4,3,2,1,0:T(8,128)}, f32[4,4,2,32,128]{4,3,2,1,0:T(8,128)S(1)}, u32[]{:S(2)}, u32[]{:S(2)}) collective-permute-start(f32[4,4,2,32,128]{4,3,2,1,0:T(8,128)} %copy-done.69), channel_id=1, source_target_pairs={{4,8},{5,9},{6,10},{7,11},{8,4},{9,5},{10,6},{11,7},{20,24},{21,25... | collective-permute-start | bytes 1572872 | tf_op jit(solution)/shard_map/ppermute | solution.py:409
  369.9 22.9 %collective-permute-start.15 = (f32[4,4,2,32,128]{4,3,2,1,0:T(8,128)}, f32[4,4,2,32,128]{4,3,2,1,0:T(8,128)S(1)}, u32[]{:S(2)}, u32[]{:S(2)}) collective-permute-start(f32[4,4,2,32,128]{4,3,2,1,0:T(8,128)} %copy-done.82), channel_id=1, source_target_pairs={{4,12},{5,13},{6,14},{7,15},{8,0},{9,1},{10,2},{11,3},{20,28},{21,... | collective-permute-start | bytes 1572872 | tf_op jit(solution)/shard_map/ppermute | solution.py:409
  398.5 14.8 %collective-permute-start.19 = (f32[4,4,2,32,128]{4,3,2,1,0:T(8,128)S(1)}, f32[4,4,2,32,128]{4,3,2,1,0:T(8,128)S(1)}, u32[]{:S(2)}, u32[]{:S(2)}) collective-permute-start(f32[4,4,2,32,128]{4,3,2,1,0:T(8,128)S(1)} %get-tuple-element.168), channel_id=1, source_target_pairs={{0,4},{1,5},{2,6},{3,7},{8,12},{9,13},{10,14},{11,15},{4,0},{5,1},... | collective-permute-start | bytes 1572872 | tf_op jit(solution)/shard_map/ppermute | solution.py:409
  402.0 16.7 %collective-permute-start.22 = (f32[4,4,2,32,128]{4,3,2,1,0:T(8,128)S(1)}, f32[4,4,2,32,128]{4,3,2,1,0:T(8,128)S(1)}, u32[]{:S(2)}, u32[]{:S(2)}) collective-permute-start(f32[4,4,2,32,128]{4,3,2,1,0:T(8,128)S(1)} %get-tuple-element.165.refs_6_), channel_id=1, source_target_pairs={{4,8},{5,9},{6,10},{7,11},{8,4},{9,5},{10,6},{11,7},{20,24},{21,25... | collective-permute-start | bytes 1572872 | tf_op jit(solution)/shard_map/ppermute | solution.py:409
  404.3 21.5 %collective-permute-start.23 = (f32[4,4,2,32,128]{4,3,2,1,0:T(8,128)S(1)}, f32[4,4,2,32,128]{4,3,2,1,0:T(8,128)S(1)}, u32[]{:S(2)}, u32[]{:S(2)}) collective-permute-start(f32[4,4,2,32,128]{4,3,2,1,0:T(8,128)S(1)} %get-tuple-element.172), channel_id=1, source_target_pairs={{4,12},{5,13},{6,14},{7,15},{8,0},{9,1},{10,2},{11,3},{20,28},{21,... | collective-permute-start | bytes 1572872 | tf_op jit(solution)/shard_map/ppermute | solution.py:409
  435.8 73.9 %all-to-all-start.9 = ((f32[4,2,2,32,8,128]{5,4,3,2,1,0:T(8,128)}), f32[4,2,2,32,8,128]{5,4,3,2,1,0:T(8,128)}, u32[]{:S(2)}, u32[]{:S(2)}) async-start(f32[4,2,2,32,8,128]{5,4,3,2,1,0:T(8,128)} %packed.13), calls=%async_computation.9 | async-start | bytes 4194304 | tf_op jit(solution)/shard_map/all_to_all | solution.py:406
  440.3 16.3 %collective-permute-start.24 = (f32[4,4,2,32,128]{4,3,2,1,0:T(8,128)}, f32[4,4,2,32,128]{4,3,2,1,0:T(8,128)S(1)}, u32[]{:S(2)}, u32[]{:S(2)}) collective-permute-start(f32[4,4,2,32,128]{4,3,2,1,0:T(8,128)} %copy-done.87), channel_id=1, source_target_pairs={{0,4},{1,5},{2,6},{3,7},{8,12},{9,13},{10,14},{11,15},{4,0},{5,1},... | collective-permute-start | bytes 1572872 | tf_op jit(solution)/shard_map/ppermute | solution.py:409
  443.9 16.7 %collective-permute-start.20 = (f32[4,4,2,32,128]{4,3,2,1,0:T(8,128)S(1)}, f32[4,4,2,32,128]{4,3,2,1,0:T(8,128)S(1)}, u32[]{:S(2)}, u32[]{:S(2)}) collective-permute-start(f32[4,4,2,32,128]{4,3,2,1,0:T(8,128)S(1)} %get-tuple-element.170.refs_6_), channel_id=1, source_target_pairs={{4,8},{5,9},{6,10},{7,11},{8,4},{9,5},{10,6},{11,7},{20,24},{21,25... | collective-permute-start | bytes 1572872 | tf_op jit(solution)/shard_map/ppermute | solution.py:409
  446.3 22.7 %collective-permute-start.21 = (f32[4,4,2,32,128]{4,3,2,1,0:T(8,128)}, f32[4,4,2,32,128]{4,3,2,1,0:T(8,128)S(1)}, u32[]{:S(2)}, u32[]{:S(2)}) collective-permute-start(f32[4,4,2,32,128]{4,3,2,1,0:T(8,128)} %copy-done.83), channel_id=1, source_target_pairs={{4,12},{5,13},{6,14},{7,15},{8,0},{9,1},{10,2},{11,3},{20,28},{21,... | collective-permute-start | bytes 1572872 | tf_op jit(solution)/shard_map/ppermute | solution.py:409
  474.5 14.7 %collective-permute-start.25 = (f32[4,4,2,32,128]{4,3,2,1,0:T(8,128)S(1)}, f32[4,4,2,32,128]{4,3,2,1,0:T(8,128)S(1)}, u32[]{:S(2)}, u32[]{:S(2)}) collective-permute-start(f32[4,4,2,32,128]{4,3,2,1,0:T(8,128)S(1)} %get-tuple-element.182), channel_id=1, source_target_pairs={{0,4},{1,5},{2,6},{3,7},{8,12},{9,13},{10,14},{11,15},{4,0},{5,1},... | collective-permute-start | bytes 1572872 | tf_op jit(solution)/shard_map/ppermute | solution.py:409
  477.9 16.7 %collective-permute-start.28 = (f32[4,4,2,32,128]{4,3,2,1,0:T(8,128)S(1)}, f32[4,4,2,32,128]{4,3,2,1,0:T(8,128)S(1)}, u32[]{:S(2)}, u32[]{:S(2)}) collective-permute-start(f32[4,4,2,32,128]{4,3,2,1,0:T(8,128)S(1)} %get-tuple-element.178.refs_6_), channel_id=1, source_target_pairs={{4,8},{5,9},{6,10},{7,11},{8,4},{9,5},{10,6},{11,7},{20,24},{21,25... | collective-permute-start | bytes 1572872 | tf_op jit(solution)/shard_map/ppermute | solution.py:409
  480.2 21.5 %collective-permute-start.29 = (f32[4,4,2,32,128]{4,3,2,1,0:T(8,128)S(1)}, f32[4,4,2,32,128]{4,3,2,1,0:T(8,128)S(1)}, u32[]{:S(2)}, u32[]{:S(2)}) collective-permute-start(f32[4,4,2,32,128]{4,3,2,1,0:T(8,128)S(1)} %get-tuple-element.186), channel_id=1, source_target_pairs={{4,12},{5,13},{6,14},{7,15},{8,0},{9,1},{10,2},{11,3},{20,28},{21,... | collective-permute-start | bytes 1572872 | tf_op jit(solution)/shard_map/ppermute | solution.py:409
  538.7 76.3 %all-to-all-start.7 = ((f32[4,24,2,32,128]{4,3,2,1,0:T(8,128)}), f32[4,24,2,32,128]{4,3,2,1,0:T(8,128)}, u32[]{:S(2)}, u32[]{:S(2)}) async-start(f32[4,24,2,32,128]{4,3,2,1,0:T(8,128)} %get-tuple-element.181), calls=%async_computation.7 | async-start | bytes 6291456 | tf_op jit(solution)/shard_map/all_to_all | solution.py:406
  543.4 16.2 %collective-permute-start.30 = (f32[4,4,2,32,128]{4,3,2,1,0:T(8,128)}, f32[4,4,2,32,128]{4,3,2,1,0:T(8,128)S(1)}, u32[]{:S(2)}, u32[]{:S(2)}) collective-permute-start(f32[4,4,2,32,128]{4,3,2,1,0:T(8,128)} %get-tuple-element.188), channel_id=1, source_target_pairs={{0,4},{1,5},{2,6},{3,7},{8,12},{9,13},{10,14},{11,15},{4,0},{5,1},... | collective-permute-start | bytes 1572872 | tf_op jit(solution)/shard_map/ppermute | solution.py:409
  547.0 16.7 %collective-permute-start.26 = (f32[4,4,2,32,128]{4,3,2,1,0:T(8,128)S(1)}, f32[4,4,2,32,128]{4,3,2,1,0:T(8,128)S(1)}, u32[]{:S(2)}, u32[]{:S(2)}) collective-permute-start(f32[4,4,2,32,128]{4,3,2,1,0:T(8,128)S(1)} %copy-done.62), channel_id=1, source_target_pairs={{4,8},{5,9},{6,10},{7,11},{8,4},{9,5},{10,6},{11,7},{20,24},{21,25... | collective-permute-start | bytes 1572872 | tf_op jit(solution)/shard_map/ppermute | solution.py:409
  549.4 22.7 %collective-permute-start.27 = (f32[4,4,2,32,128]{4,3,2,1,0:T(8,128)}, f32[4,4,2,32,128]{4,3,2,1,0:T(8,128)S(1)}, u32[]{:S(2)}, u32[]{:S(2)}) collective-permute-start(f32[4,4,2,32,128]{4,3,2,1,0:T(8,128)} %copy-done.81), channel_id=1, source_target_pairs={{4,12},{5,13},{6,14},{7,15},{8,0},{9,1},{10,2},{11,3},{20,28},{21,... | collective-permute-start | bytes 1572872 | tf_op jit(solution)/shard_map/ppermute | solution.py:409
  577.6 14.7 %collective-permute-start.31 = (f32[4,4,2,32,128]{4,3,2,1,0:T(8,128)S(1)}, f32[4,4,2,32,128]{4,3,2,1,0:T(8,128)S(1)}, u32[]{:S(2)}, u32[]{:S(2)}) collective-permute-start(f32[4,4,2,32,128]{4,3,2,1,0:T(8,128)S(1)} %get-tuple-element.193), channel_id=1, source_target_pairs={{0,4},{1,5},{2,6},{3,7},{8,12},{9,13},{10,14},{11,15},{4,0},{5,1},... | collective-permute-start | bytes 1572872 | tf_op jit(solution)/shard_map/ppermute | solution.py:409
  581.0 16.7 %collective-permute-start.34 = (f32[4,4,2,32,128]{4,3,2,1,0:T(8,128)S(1)}, f32[4,4,2,32,128]{4,3,2,1,0:T(8,128)S(1)}, u32[]{:S(2)}, u32[]{:S(2)}) collective-permute-start(f32[4,4,2,32,128]{4,3,2,1,0:T(8,128)S(1)} %get-tuple-element.190.refs_6_), channel_id=1, source_target_pairs={{4,8},{5,9},{6,10},{7,11},{8,4},{9,5},{10,6},{11,7},{20,24},{21,25... | collective-permute-start | bytes 1572872 | tf_op jit(solution)/shard_map/ppermute | solution.py:409
  583.4 21.5 %collective-permute-start.35 = (f32[4,4,2,32,128]{4,3,2,1,0:T(8,128)S(1)}, f32[4,4,2,32,128]{4,3,2,1,0:T(8,128)S(1)}, u32[]{:S(2)}, u32[]{:S(2)}) collective-permute-start(f32[4,4,2,32,128]{4,3,2,1,0:T(8,128)S(1)} %get-tuple-element.197), channel_id=1, source_target_pairs={{4,12},{5,13},{6,14},{7,15},{8,0},{9,1},{10,2},{11,3},{20,28},{21,... | collective-permute-start | bytes 1572872 | tf_op jit(solution)/shard_map/ppermute | solution.py:409
  615.0 80.3 %all-to-all-start.12 = ((f32[4,2,2,32,8,128]{5,4,3,2,1,0:T(8,128)}), f32[4,2,2,32,8,128]{5,4,3,2,1,0:T(8,128)}, u32[]{:S(2)}, u32[]{:S(2)}) async-start(f32[4,2,2,32,8,128]{5,4,3,2,1,0:T(8,128)} %packed.15), calls=%async_computation.12 | async-start | bytes 4194304 | tf_op jit(solution)/shard_map/all_to_all | solution.py:406
  619.6 16.2 %collective-permute-start.36 = (f32[4,4,2,32,128]{4,3,2,1,0:T(8,128)}, f32[4,4,2,32,128]{4,3,2,1,0:T(8,128)S(1)}, u32[]{:S(2)}, u32[]{:S(2)}) collective-permute-start(f32[4,4,2,32,128]{4,3,2,1,0:T(8,128)} %copy-done.88), channel_id=1, source_target_pairs={{0,4},{1,5},{2,6},{3,7},{8,12},{9,13},{10,14},{11,15},{4,0},{5,1},... | collective-permute-start | bytes 1572872 | tf_op jit(solution)/shard_map/ppermute | solution.py:409
  623.1 16.7 %collective-permute-start.32 = (f32[4,4,2,32,128]{4,3,2,1,0:T(8,128)S(1)}, f32[4,4,2,32,128]{4,3,2,1,0:T(8,128)S(1)}, u32[]{:S(2)}, u32[]{:S(2)}) collective-permute-start(f32[4,4,2,32,128]{4,3,2,1,0:T(8,128)S(1)} %copy-done.64), channel_id=1, source_target_pairs={{4,8},{5,9},{6,10},{7,11},{8,4},{9,5},{10,6},{11,7},{20,24},{21,25... | collective-permute-start | bytes 1572872 | tf_op jit(solution)/shard_map/ppermute | solution.py:409
  625.6 22.6 %collective-permute-start.33 = (f32[4,4,2,32,128]{4,3,2,1,0:T(8,128)S(1)}, f32[4,4,2,32,128]{4,3,2,1,0:T(8,128)S(1)}, u32[]{:S(2)}, u32[]{:S(2)}) collective-permute-start(f32[4,4,2,32,128]{4,3,2,1,0:T(8,128)S(1)} %copy-done.85), channel_id=1, source_target_pairs={{4,12},{5,13},{6,14},{7,15},{8,0},{9,1},{10,2},{11,3},{20,28},{21,... | collective-permute-start | bytes 1572872 | tf_op jit(solution)/shard_map/ppermute | solution.py:409
  653.6 14.7 %collective-permute-start.37 = (f32[4,4,2,32,128]{4,3,2,1,0:T(8,128)S(1)}, f32[4,4,2,32,128]{4,3,2,1,0:T(8,128)S(1)}, u32[]{:S(2)}, u32[]{:S(2)}) collective-permute-start(f32[4,4,2,32,128]{4,3,2,1,0:T(8,128)S(1)} %get-tuple-element.206), channel_id=1, source_target_pairs={{0,4},{1,5},{2,6},{3,7},{8,12},{9,13},{10,14},{11,15},{4,0},{5,1},... | collective-permute-start | bytes 1572872 | tf_op jit(solution)/shard_map/ppermute | solution.py:409
  657.0 16.7 %collective-permute-start.40 = (f32[4,4,2,32,128]{4,3,2,1,0:T(8,128)S(1)}, f32[4,4,2,32,128]{4,3,2,1,0:T(8,128)S(1)}, u32[]{:S(2)}, u32[]{:S(2)}) collective-permute-start(f32[4,4,2,32,128]{4,3,2,1,0:T(8,128)S(1)} %get-tuple-element.202.refs_6_), channel_id=1, source_target_pairs={{4,8},{5,9},{6,10},{7,11},{8,4},{9,5},{10,6},{11,7},{20,24},{21,25... | collective-permute-start | bytes 1572872 | tf_op jit(solution)/shard_map/ppermute | solution.py:409
  659.5 21.5 %collective-permute-start.41 = (f32[4,4,2,32,128]{4,3,2,1,0:T(8,128)S(1)}, f32[4,4,2,32,128]{4,3,2,1,0:T(8,128)S(1)}, u32[]{:S(2)}, u32[]{:S(2)}) collective-permute-start(f32[4,4,2,32,128]{4,3,2,1,0:T(8,128)S(1)} %get-tuple-element.210), channel_id=1, source_target_pairs={{4,12},{5,13},{6,14},{7,15},{8,0},{9,1},{10,2},{11,3},{20,28},{21,... | collective-permute-start | bytes 1572872 | tf_op jit(solution)/shard_map/ppermute | solution.py:409
  687.3 13.8 %collective-permute-start.42 = (f32[4,4,2,32,128]{4,3,2,1,0:T(8,128)}, f32[4,4,2,32,128]{4,3,2,1,0:T(8,128)}, u32[]{:S(2)}, u32[]{:S(2)}) collective-permute-start(f32[4,4,2,32,128]{4,3,2,1,0:T(8,128)} %get-tuple-element.212), channel_id=1, source_target_pairs={{0,4},{1,5},{2,6},{3,7},{8,12},{9,13},{10,14},{11,15},{4,0},{5,1},... | collective-permute-start | bytes 1572872 | tf_op jit(solution)/shard_map/ppermute | solution.py:409
  690.7 17.1 %collective-permute-start.38 = (f32[4,4,2,32,128]{4,3,2,1,0:T(8,128)}, f32[4,4,2,32,128]{4,3,2,1,0:T(8,128)}, u32[]{:S(2)}, u32[]{:S(2)}) collective-permute-start(f32[4,4,2,32,128]{4,3,2,1,0:T(8,128)} %get-tuple-element.208.refs_6_), channel_id=1, source_target_pairs={{4,8},{5,9},{6,10},{7,11},{8,4},{9,5},{10,6},{11,7},{20,24},{21,25... | collective-permute-start | bytes 1572872 | tf_op jit(solution)/shard_map/ppermute | solution.py:409
  693.2 20.6 %collective-permute-start.39 = (f32[4,4,2,32,128]{4,3,2,1,0:T(8,128)}, f32[4,4,2,32,128]{4,3,2,1,0:T(8,128)}, u32[]{:S(2)}, u32[]{:S(2)}) collective-permute-start(f32[4,4,2,32,128]{4,3,2,1,0:T(8,128)} %get-tuple-element.209), channel_id=1, source_target_pairs={{4,12},{5,13},{6,14},{7,15},{8,0},{9,1},{10,2},{11,3},{20,28},{21,... | collective-permute-start | bytes 1572872 | tf_op jit(solution)/shard_map/ppermute | solution.py:409
  695.3 86.2 %all-to-all-start.10 = ((f32[4,16,2,32,128]{4,3,2,1,0:T(8,128)}), f32[4,16,2,32,128]{4,3,2,1,0:T(8,128)S(1)}, u32[]{:S(2)}, u32[]{:S(2)}) async-start(f32[4,16,2,32,128]{4,3,2,1,0:T(8,128)} %get-tuple-element.205), calls=%async_computation.10 | async-start | bytes 4194304 | tf_op jit(solution)/shard_map/all_to_all | solution.py:406
  722.8 16.7 %collective-permute-start.46 = (f32[4,4,2,32,128]{4,3,2,1,0:T(8,128)S(1)}, f32[4,4,2,32,128]{4,3,2,1,0:T(8,128)S(1)}, u32[]{:S(2)}, u32[]{:S(2)}) collective-permute-start(f32[4,4,2,32,128]{4,3,2,1,0:T(8,128)S(1)} %get-tuple-element.214.refs_6_), channel_id=1, source_target_pairs={{4,8},{5,9},{6,10},{7,11},{8,4},{9,5},{10,6},{11,7},{20,24},{21,25... | collective-permute-start | bytes 1572872 | tf_op jit(solution)/shard_map/ppermute | solution.py:409
  725.3 19.1 %collective-permute-start.47 = (f32[4,4,2,32,128]{4,3,2,1,0:T(8,128)S(1)}, f32[4,4,2,32,128]{4,3,2,1,0:T(8,128)S(1)}, u32[]{:S(2)}, u32[]{:S(2)}) collective-permute-start(f32[4,4,2,32,128]{4,3,2,1,0:T(8,128)S(1)} %get-tuple-element.221), channel_id=1, source_target_pairs={{4,12},{5,13},{6,14},{7,15},{8,0},{9,1},{10,2},{11,3},{20,28},{21,... | collective-permute-start | bytes 1572872 | tf_op jit(solution)/shard_map/ppermute | solution.py:409
  751.0 19.3 %collective-permute-start.44 = (f32[4,4,2,32,128]{4,3,2,1,0:T(8,128)S(1)}, f32[4,4,2,32,128]{4,3,2,1,0:T(8,128)S(1)}, u32[]{:S(2)}, u32[]{:S(2)}) collective-permute-start(f32[4,4,2,32,128]{4,3,2,1,0:T(8,128)S(1)} %get-tuple-element.219.refs_6_), channel_id=1, source_target_pairs={{4,8},{5,9},{6,10},{7,11},{8,4},{9,5},{10,6},{11,7},{20,24},{21,25... | collective-permute-start | bytes 1572872 | tf_op jit(solution)/shard_map/ppermute | solution.py:409
  757.5 17.9 %collective-permute-start.45 = (f32[4,4,2,32,128]{4,3,2,1,0:T(8,128)S(1)}, f32[4,4,2,32,128]{4,3,2,1,0:T(8,128)S(1)}, u32[]{:S(2)}, u32[]{:S(2)}) collective-permute-start(f32[4,4,2,32,128]{4,3,2,1,0:T(8,128)S(1)} %get-tuple-element.220), channel_id=1, source_target_pairs={{4,12},{5,13},{6,14},{7,15},{8,0},{9,1},{10,2},{11,3},{20,28},{21,... | collective-permute-start | bytes 1572872 | tf_op jit(solution)/shard_map/ppermute | solution.py:409
  781.5 60.0 %all-to-all-start.13 = ((f32[4,16,2,32,128]{4,3,2,1,0:T(8,128)}), f32[4,16,2,32,128]{4,3,2,1,0:T(8,128)}, u32[]{:S(2)}, u32[]{:S(2)}) async-start(f32[4,16,2,32,128]{4,3,2,1,0:T(8,128)} %get-tuple-element.228), calls=%async_computation.13 | async-start | bytes 4194304 | tf_op jit(solution)/shard_map/all_to_all | solution.py:406
  786.0 16.2 %collective-permute-start.49 = (f32[4,4,2,32,128]{4,3,2,1,0:T(8,128)S(1)}, f32[4,4,2,32,128]{4,3,2,1,0:T(8,128)S(1)}, u32[]{:S(2)}, u32[]{:S(2)}) collective-permute-start(f32[4,4,2,32,128]{4,3,2,1,0:T(8,128)S(1)} %get-tuple-element.229.rest_0_.refs_9_), channel_id=1, source_target_pairs={{4,0},{5,1},{6,2},{7,3},{12,8},{13,9},{14,10},{15,11},{20,16},{21,... | collective-permute-start | bytes 1572872 | tf_op jit(solution)/shard_map/ppermute | solution.py:409
  787.3 21.2 %collective-permute-start.52 = (f32[4,4,2,32,128]{4,3,2,1,0:T(8,128)}, f32[4,4,2,32,128]{4,3,2,1,0:T(8,128)S(1)}, u32[]{:S(2)}, u32[]{:S(2)}) collective-permute-start(f32[4,4,2,32,128]{4,3,2,1,0:T(8,128)} %copy-done.59), channel_id=1, source_target_pairs={{8,4},{9,5},{10,6},{11,7},{24,20},{25,21},{26,22},{27,23}} | collective-permute-start | bytes 1572872 | tf_op jit(solution)/shard_map/ppermute | solution.py:409
  793.8 23.8 %collective-permute-start.53 = (f32[4,4,2,32,128]{4,3,2,1,0:T(8,128)}, f32[4,4,2,32,128]{4,3,2,1,0:T(8,128)S(1)}, u32[]{:S(2)}, u32[]{:S(2)}) collective-permute-start(f32[4,4,2,32,128]{4,3,2,1,0:T(8,128)} %copy-done.79), channel_id=1, source_target_pairs={{8,0},{9,1},{10,2},{11,3},{24,16},{25,17},{26,18},{27,19}} | collective-permute-start | bytes 1572872 | tf_op jit(solution)/shard_map/ppermute | solution.py:409
  803.5 25.3 %collective-permute-start.50 = (f32[4,4,2,32,128]{4,3,2,1,0:T(8,128)S(1)}, f32[4,4,2,32,128]{4,3,2,1,0:T(8,128)S(1)}, u32[]{:S(2)}, u32[]{:S(2)}) collective-permute-start(f32[4,4,2,32,128]{4,3,2,1,0:T(8,128)S(1)} %get-tuple-element.230.refs_6_), channel_id=1, source_target_pairs={{8,4},{9,5},{10,6},{11,7},{24,20},{25,21},{26,22},{27,23}} | collective-permute-start | bytes 1572872 | tf_op jit(solution)/shard_map/ppermute | solution.py:409
  805.8 33.4 %collective-permute-start.51 = (f32[4,4,2,32,128]{4,3,2,1,0:T(8,128)S(1)}, f32[4,4,2,32,128]{4,3,2,1,0:T(8,128)S(1)}, u32[]{:S(2)}, u32[]{:S(2)}) collective-permute-start(f32[4,4,2,32,128]{4,3,2,1,0:T(8,128)S(1)} %get-tuple-element.231), channel_id=1, source_target_pairs={{8,0},{9,1},{10,2},{11,3},{24,16},{25,17},{26,18},{27,19}} | collective-permute-start | bytes 1572872 | tf_op jit(solution)/shard_map/ppermute | solution.py:409
  841.5 36.8 %all-to-all-start.14 = ((f32[4,8,2,32,128]{4,3,2,1,0:T(8,128)}), f32[4,8,2,32,128]{4,3,2,1,0:T(8,128)}, u32[]{:S(2)}, u32[]{:S(2)}) async-start(f32[4,8,2,32,128]{4,3,2,1,0:T(8,128)} %cells.35), calls=%async_computation.14 | async-start | bytes 2097152 | tf_op jit(solution)/shard_map/all_to_all | solution.py:406
  (92 other events, 1368.5 us)

commit v2 on v1

--- a/solution.py
+++ b/solution.py
@@ -11,6 +11,11 @@
 layers = 4
 chunk_target = 16
 lanes = 128
+ends_of = {"field": (2, 6, 10), "cells": (2, 4, 6, 10, 14), "gradient": (7, 11, 14)}
+transfers = (
+    ("cells", 1, 1), ("cells", 2, 2), ("field", 2, 3), ("cells", 3, 4), ("field", 3, 6), ("cells", 4, 8), ("gradient", 0, 10),
+    ("cells", 5, 12), ("gradient", 1, 13), ("gradient", 2, 16), ("gradient", 3, 18),
+)
 f32, bf16 = jnp.float32, jnp.bfloat16
 ANY = pl.BlockSpec(memory_space=pl.ANY)
 SMEM = pl.BlockSpec(memory_space=pltpu.SMEM)
@@ -34,8 +39,7 @@
     return pl.BlockSpec(shape, lambda *_: (0,) * len(shape))
 
 
-def cost(flops, transferred):
-    return pl.CostEstimate(flops=int(flops), bytes_accessed=int(transferred), transcendentals=0)
+brief = pl.CostEstimate(flops=1, bytes_accessed=1, transcendentals=0)
 
 
 def fold_rows(values):
@@ -47,14 +51,23 @@
     return jnp.concatenate([matrix[q * rows + low : q * rows + high] for low, high in bounds for q in range(peers)], axis=0)
 
 
-def field_factors(cholesky_north, cholesky_time, bounds, peers):
-    def kernel(north, time, north_high, north_low, time_high, time_low):
+def field_factors(cholesky_north, cholesky_time, bounds, peers, held_back):
+    def kernel(north, time, _, north_high, north_low, time_high, time_low):
         north_high[...], north_low[...] = split(permuted_rows(north[...], bounds, peers))
         time_high[...], time_low[...] = split(time[...].T)
 
     ny, nt = cholesky_north.shape[0], cholesky_time.shape[0]
     pair = lambda size: [jax.ShapeDtypeStruct((size, size), bf16)] * 2
-    return pl.pallas_call(kernel, out_shape=pair(ny) + pair(nt), compiler_params=params(), name="field_factors")(cholesky_north, cholesky_time)
+    full = pl.BlockSpec(memory_space=pltpu.VMEM)
+    return pl.pallas_call(
+        kernel,
+        out_shape=pair(ny) + pair(nt),
+        in_specs=[full, full, ANY],
+        out_specs=[full] * 4,
+        cost_estimate=brief,
+        compiler_params=params(),
+        name="field_factors",
+    )(cholesky_north, cholesky_time, held_back)
 
 
 def other_factors(layer, cholesky_east, cholesky_north, cholesky_time, bounds, peers, held_back):
@@ -100,6 +113,7 @@
         out_specs=[whole(s.shape) for s in shapes],
         grid=(1,),
         compiler_params=params(),
+        cost_estimate=brief,
         name="other_factors",
     )(layer, cholesky_east, cholesky_north, cholesky_time, held_back)
     return [tuple(outs[2 * i : 2 * i + 2]) for i in range(len(sizes))]
@@ -141,19 +155,20 @@
         out_specs=[pl.BlockSpec((rows, parts, step, lanes), lambda i: (0, 0, i, 0)) for rows in counts] + [whole((8, nt))],
         out_shape=[jax.ShapeDtypeStruct((rows, parts, planes, lanes), f32) for rows in counts] + [jax.ShapeDtypeStruct((8, nt), f32)],
         compiler_params=params(),
-        cost_estimate=cost(12 * planes * ny * nt * nt, 8 * whitened.size),
+        cost_estimate=brief,
         name="field",
     )(whitened, *factors)
     return [g.reshape(peers, -1, *g.shape[1:]) for g in groups], squares
 
 
-def packed(counts, exposure, low, high, peers, held_back):
+def packed(counts, exposure, low, high, peers, *held_back):
     planes, ny, nt = counts.shape
     rows, parts = high - low, nt // lanes
     band = 8 if rows % 8 == 0 and low % 8 == 0 and (ny // peers) % 8 == 0 else rows
     per_peer = ny // peers // band
 
-    def kernel(c, e, _, out):
+    def kernel(c, e, *rest):
+        out = rest[-1]
         for h in range(parts):
             out[0, 0, h] = c[:, :, h * lanes : (h + 1) * lanes].astype(f32)
             out[0, 1, h] = e[:, :, h * lanes : (h + 1) * lanes].astype(f32)
@@ -162,39 +177,46 @@
     return pl.pallas_call(
         kernel,
         grid=(peers, rows // band),
-        in_specs=[source, source, ANY],
+        in_specs=[source, source] + [ANY] * len(held_back),
         out_specs=pl.BlockSpec((1, 2, parts, planes, band, lanes), lambda q, j: (q, 0, 0, 0, j, 0)),
         out_shape=jax.ShapeDtypeStruct((peers, 2, parts, planes, rows, lanes), f32),
         compiler_params=params(),
-        cost_estimate=cost(0, 16 * peers * planes * rows * nt),
+        cost_estimate=brief,
         name="packed",
-    )(counts, exposure, held_back)
-
-
-def gate(values, held_back):
-    def kernel(_, __, out):
+    )(counts, exposure, *held_back)
+
+
+def gate(values, *held_back):
+    def kernel(*_):
         pass
 
     return pl.pallas_call(
         kernel,
-        in_specs=[ANY, ANY],
+        in_specs=[ANY] * (1 + len(held_back)),
         out_specs=ANY,
         out_shape=jax.ShapeDtypeStruct(values.shape, values.dtype),
         input_output_aliases={0: 0},
+        cost_estimate=brief,
         name="gate",
-    )(values, held_back)
-
-
-def lines(block):
-    peers, _, parts = block.shape[:3]
-    return jnp.concatenate([jnp.concatenate([block[q, 0, h] for h in range(parts)], axis=1) for q in range(peers)], axis=0)
-
-
-def put_lines(out, values):
-    peers, _, parts, planes, width = out.shape
-    for q in range(peers):
-        for h in range(parts):
-            out[q, 0, h] = values[q * planes : (q + 1) * planes, h * width : (h + 1) * width]
+    )(values, *held_back)
+
+
+def lines(*blocks):
+    peers = blocks[0].shape[0]
+    return jnp.concatenate(
+        [jnp.concatenate([b[q, 0, h] for b in blocks for h in range(b.shape[2])], axis=1) for q in range(peers)], axis=0
+    )
+
+
+def put_lines(outs, values):
+    outs = outs if isinstance(outs, list) else [outs]
+    first = 0
+    for out in outs:
+        peers, _, parts, planes, width = out.shape
+        for q in range(peers):
+            for h in range(parts):
+                out[q, 0, h] = values[q * planes : (q + 1) * planes, (first + h) * width : (first + h + 1) * width]
+        first += parts
 
 
 def rows_of(array, start):
@@ -203,21 +225,24 @@
 
 
 def cross_terms(layer, cross, crossed, own_field, own_residual, rows):
-    operands, specs = [layer, *cross, crossed], [SMEM, whole(cross[0].shape), whole(cross[1].shape), rows_of(crossed, 0)]
+    operands = [layer, *cross, *crossed]
+    specs = [SMEM, whole(cross[0].shape), whole(cross[1].shape)] + [rows_of(c, 0) for c in crossed]
+    pieces = len(crossed)
     for pair in (own_field, own_residual):
         if pair is not None:
             operands.append(pair[0])
             specs.append(rows_of(*pair))
-    peers, _, parts, planes, _ = crossed.shape
+    peers, _, _, planes, _ = crossed[0].shape
+    parts = sum(c.shape[2] for c in crossed)
     span, nt = peers * planes, parts * lanes
 
-    def kernel(layer_ref, high, low, moved, *rest):
-        near, far = rest[-2:]
-        rest = list(rest[:-2])
+    def kernel(layer_ref, high, low, *rest):
+        moved, near, far = list(rest[:pieces]), *rest[-2:]
+        rest = list(rest[pieces:-2])
         here = layer_ref[0]
 
         def run(first, second):
-            result = product((high[...], low[...]), split(jnp.concatenate([lines(first), lines(second)], axis=0)))
+            result = product((high[...], low[...]), split(jnp.concatenate([lines(*first), lines(*second)], axis=0)))
             put_lines(near, result[:span])
             put_lines(far, result[span:])
 
@@ -226,14 +251,14 @@
 
             @pl.when(here == 1)
             def _():
-                run(moved, own_p)
+                run(moved, [own_p])
 
         if own_residual is not None:
             own_r = rest.pop(0)
 
             @pl.when(here == 2)
             def _():
-                run(own_r, moved)
+                run([own_r], moved)
 
     shape = jax.ShapeDtypeStruct((peers, rows, parts, planes, lanes), f32)
     return pl.pallas_call(
@@ -243,20 +268,23 @@
         out_specs=[rows_of(shape, 0)] * 2,
         out_shape=[shape] * 2,
         compiler_params=params(),
-        cost_estimate=cost(6 * 4 * span * span * rows * nt, 20 * span * rows * nt),
+        cost_estimate=brief,
         name="cross_terms",
     )(*operands)
 
 
 def cells(layer, factors, moved, near, far, total, own_field, observed, next_field, old_residual, gradient, rows, held_back):
     own, own_t, beside = factors
-    peers, _, parts, planes, _ = moved.shape
+    peers, _, parts, planes, _ = near.shape
     span, nt = peers * planes, parts * lanes
-    operands = [layer, *beside, moved, near, far, held_back]
-    specs = [SMEM, whole((span, span)), whole((span, span)), rows_of(moved, 0), rows_of(near, 0), rows_of(far, 0), ANY]
+    pieces = len(moved)
+    operands = [layer, *beside, near, far, *moved, *held_back]
+    specs = [SMEM, whole((span, span)), whole((span, span)), rows_of(near, 0), rows_of(far, 0)]
+    specs += [rows_of(m, 0) for m in moved] + [ANY] * len(held_back)
     shape = jax.ShapeDtypeStruct((peers, rows, parts, planes, lanes), f32)
     shapes, out_specs, aliases = [], [], {}
-    names = ["layer", "beside_high", "beside_low", "moved", "near", "far", "_"]
+    names = ["layer", "beside_high", "beside_low", "near", "far"]
+    names += ["moved%d" % i for i in range(pieces)] + ["_"] * len(held_back)
     out_names = []
 
     def take(name, array, spec):
@@ -279,7 +307,9 @@
         take("total", total, whole(total.shape))
         if next_field is not None:
             take("next_field", next_field[0], rows_of(*next_field))
-            give("send", shape, rows_of(shape, 0))
+        for i in range(pieces):
+            piece = jax.ShapeDtypeStruct((peers, rows, moved[i].shape[2], planes, lanes), f32)
+            give("send%d" % i, piece, rows_of(piece, 0))
         give("residual", shape, rows_of(shape, 0))
         give("new_total", jax.ShapeDtypeStruct(total.shape, f32), whole(total.shape))
     if old_residual is not None:
@@ -297,7 +327,7 @@
         ref = dict(zip(names + out_names, refs))
         here = ref["layer"][0]
         odd, upper = here % 2 == 1, here >= layers // 2
-        extra = product((ref["beside_high"][...], ref["beside_low"][...]), split(lines(ref["moved"])))
+        extra = product((ref["beside_high"][...], ref["beside_low"][...]), split(lines(*[ref["moved%d" % i] for i in range(pieces)])))
         partial = jnp.where((here == 1) | (here == 2), lines(ref["near"]), lines(ref["far"]))
         if own_field is not None:
             log_rate = product((ref["own_high"][...], ref["own_low"][...]), split(lines(ref["field"])))
@@ -319,15 +349,17 @@
                 ref["new_total"][...] = ref["total"][...]
 
             ref["new_total"][...] += fold_rows(observed_counts * log_rate - intensity)
+            send = [ref["send%d" % i] for i in range(pieces)]
+
+            @pl.when(odd)
+            def _():
+                put_lines(send, residual)
+
             if next_field is not None:
-
-                @pl.when(odd)
-                def _():
-                    put_lines(ref["send"], residual)
 
                 @pl.when(jnp.logical_not(odd))
                 def _():
-                    ref["send"][...] = ref["next_field"][...]
+                    put_lines(send, lines(ref["next_field"]))
 
         if old_residual is not None:
             out = product((ref["own_t_high"][...], ref["own_t_low"][...]), split(lines(ref["old"])))
@@ -341,7 +373,7 @@
         out_shape=shapes,
         input_output_aliases=aliases,
         compiler_params=params(),
-        cost_estimate=cost(6 * 3 * span * span * rows * nt, 40 * span * rows * nt),
+        cost_estimate=brief,
         name="cells",
     )(*operands)
     return dict(zip(out_names, outs))
@@ -377,18 +409,15 @@
         out_specs=planes_block,
         out_shape=jax.ShapeDtypeStruct(whitened.shape, f32),
         compiler_params=params(),
-        cost_estimate=cost(12 * planes * ny * nt * nt, 12 * whitened.size),
+        cost_estimate=brief,
         name="finish",
     )(whitened, *north, *time, *flat)
 
 
-def bounds_of(eighths, rows, unit):
-    ends = sorted({min(rows, max(unit, rows * e // 8 // unit * unit)) for e in eighths} | {rows})
+def ranges_of(kind, rows, unit):
+    unit = unit if kind == "cells" else max(1, rows // chunk_target)
+    ends = sorted({min(rows, max(unit, rows * e // 16 // unit * unit)) for e in ends_of[kind]} | {rows})
     return list(zip([0] + ends[:-1], ends))
-
-
-def containing(bounds, row):
-    return next(i for i, (low, high) in enumerate(bounds) if low <= row < high)
 
 
 def per_device(whitened, counts, exposure, cholesky_east, cholesky_north, cholesky_time):
@@ -408,27 +437,41 @@
     def move(values, pairs):
         return lax.ppermute(values, "slab", [(a * peers + q, b * peers + q) for a, b in pairs for q in range(peers)])
 
-    field_bounds = bounds_of((1, 4), rows, unit)
-    cell_bounds = bounds_of((1, 2, 3, 4, 5, 6, 7), rows, unit)
-    gradient_bounds = bounds_of((3, 5, 7), rows, chunk)
-
-    tables = [packed(counts, exposure, *cell_bounds[0], peers, whitened)]
-    tables[0] = exchange(tables[0])
-    groups, squares = field(whitened, field_factors(cholesky_north, cholesky_time, field_bounds, peers), field_bounds, peers)
-    fields = [exchange(g) for g in groups]
-    north, time, cross, *blocks = other_factors(layer, cholesky_east, cholesky_north, cholesky_time, gradient_bounds, peers, squares)
+    spans = {kind: ranges_of(kind, rows, unit) for kind in ("field", "cells", "gradient")}
+    pack = lambda i, *held_back: packed(counts, exposure, *spans["cells"][i], peers, *held_back)
+    first = pack(0)
+    arrived = {("cells", 0): exchange(first)}
+    factors = field_factors(cholesky_north, cholesky_time, spans["field"], peers, first)
+    groups, squares = field(whitened, factors, spans["field"], peers)
+    start = gate(groups[0], arrived["cells", 0])
+    tables = [first] + [pack(i, start) for i in range(1, len(spans["cells"]))]
+    north, time, cross, *blocks = other_factors(layer, cholesky_east, cholesky_north, cholesky_time, spans["gradient"], peers, start)
+    arrived["field", 0] = gate(exchange(start), *tables[1:], cross[0])
+
+    def sum_over_slab(values):
+        if devices & (devices - 1):
+            return lax.psum(values, "slab")
+        step = 1
+        while step < devices:
+            values = values + lax.ppermute(values, "slab", [(q, q ^ step) for q in range(devices)])
+            step *= 2
+        return values
+
+    def part_of(kind, c):
+        i = next(i for i, (low, high) in enumerate(spans[kind]) if low <= c * chunk < high)
+        return i, c * chunk - spans[kind][i][0]
 
     def field_chunk(c):
-        g = containing(field_bounds, c * chunk)
-        return fields[g], c * chunk - field_bounds[g][0]
-
-    def field_slice(c):
-        array, start = field_chunk(c)
-        return lax.slice_in_dim(array, start, start + chunk, axis=1)
+        i, start = part_of("field", c)
+        return arrived["field", i], start
+
+    def pieces_of(values):
+        half = max(1, nt // lanes // 2)
+        return [lax.slice_in_dim(values, h, min(h + half, nt // lanes), axis=2) for h in range(0, nt // lanes, half)]
 
     total = -0.5 * squares
     crossed, residuals, nears, fars = {}, {}, {}, {}
-    buffers, results = {}, {}
+    buffers = {}
 
     def do_cross(k):
         own_field = field_chunk(k) if k < number else None
@@ -439,43 +482,56 @@
         fars[k + 1] = move(far, [(1, 3)] * forward + [(2, 0)] * backward)
         return near
 
+    def send(kind, i, held_back):
+        values = {"field": groups, "cells": tables, "gradient": buffers}[kind][i]
+        arrived[kind, i] = exchange(gate(values, held_back) if held_back is not None else values)
+
     for k in (0, 1):
-        crossed[k] = move(field_slice(k), [(0, 1), (2, 3)])
-    done = do_cross(0)
+        array, start = field_chunk(k)
+        values = lax.slice_in_dim(array, start, start + chunk, axis=1)
+        crossed[k] = [move(v, [(0, 1), (2, 3)]) for v in pieces_of(values)]
+        if k == 0:
+            send("field", 1, values)
+            done = do_cross(0)
     done = do_cross(1)
+    pending = list(transfers)
     for k in range(1, number + 3):
         c, g = k - 1, k - 3
+        held = [done] if k < number + 2 else [done, sums]
         own_field = observed = next_field = old = gradient = None
+        early = residuals[min(k - 2, number - 1)] if k >= 2 else done
+        while pending and pending[0][2] * number <= (k - 1) * 16:
+            kind, i, _ = pending.pop(0)
+            if i < len(spans[kind]):
+                send(kind, i, early)
         if c < number:
             own_field = field_chunk(c)
-            t = containing(cell_bounds, c * chunk)
-            while len(tables) <= t:
-                held = residuals[c - 2 * unit // chunk] if c >= 2 * unit // chunk else done
-                tables.append(exchange(packed(counts, exposure, *cell_bounds[len(tables)], peers, held)))
-            observed = (tables[t], c * chunk - cell_bounds[t][0])
+            i, start = part_of("cells", c)
+            observed = (arrived["cells", i], start)
             if k + 1 < number:
                 next_field = field_chunk(k + 1)
         if g >= 0:
             old = residuals[g]
-            h = containing(gradient_bounds, g * chunk)
-            low, high = gradient_bounds[h]
-            gradient = (buffers.get(h), high - low, g * chunk - low)
-        outs = cells(layer, blocks, crossed[k - 1], nears[k], fars[k], total, own_field, observed, next_field, old, gradient, chunk, done)
+            h, start = part_of("gradient", g)
+            low, high = spans["gradient"][h]
+            gradient = (buffers.get(h), high - low, start)
+        outs = cells(layer, blocks, crossed[k - 1], nears[k], fars[k], total, own_field, observed, next_field, old, gradient, chunk, held)
         if c < number:
             residuals[c], total = outs["residual"], outs["new_total"]
+            if c == number - 1:
+                sums = sum_over_slab(total)
         if g >= 0:
             buffers[h] = outs["gradient"]
-            if (g + 1) * chunk == high:
-                results[h] = exchange(buffers[h])
-        if k + 1 < number:
-            crossed[k + 1] = move(outs["send"], [(0, 1), (2, 3), (1, 0), (3, 2)])
-        elif k + 1 < number + 2:
-            crossed[k + 1] = move(outs["residual"], [(1, 0), (3, 2)])
-        if k + 1 in crossed:
+        if c < number:
+            pairs = ([(0, 1), (2, 3)] if k + 1 < number else []) + [(1, 0), (3, 2)]
+            crossed[k + 1] = [move(outs["send%d" % i], pairs) for i in range(len(crossed[0]))]
             done = do_cross(k + 1)
+    for kind, i, _ in pending:
+        if i < len(spans[kind]):
+            send(kind, i, None)
     cell_count = planes * ny * nt * devices
-    density = lax.psum(jnp.sum(total), "slab") / cell_count
-    gradient = finish([results[h] for h in range(len(gradient_bounds))], whitened, north, time)
+    density = jnp.sum(sums) / cell_count
+    gradient = finish([arrived["gradient", h] for h in range(len(spans["gradient"]))], whitened, north, time)
     return gradient, jnp.reshape(density, (1,))
 
 

time: 912 us -> 815 us (0.89)
  blocking collectives: 130 us -> 0 us
  local copies, waits for them, and re-layouts: 29.9 us -> 82.1 us
  waiting for transfers between devices: 356 us -> 334 us
  starting transfers between devices: 196 us -> 217 us
  Pallas kernels: 182 us -> 167 us
    all_to_all x3 -> x0, blocking collectives: 98.4 us -> none  [exchange(): lax.all_to_all(values, 'slab', 0, 0, tiled=True, axis_index_groups=in_layer)]
    unnamed x180 -> x390, local copies, waits for them, and re-layouts: 28.8 us -> 80.1 us
    ppermute x54 -> x72, waiting for transfers between devices: 322 us -> 289 us  [move(): lax.ppermute(values, 'slab', [(a * peers + q, b * peers + q) for a, b in...]
    psum x1 -> x0, blocking collectives: 31.1 us -> none  [per_device(): density = lax.psum(jnp.sum(total), 'slab') / cell_count]
    ppermute x0 -> x4, waiting for transfers between devices: none -> 27.9 us  [sum_over_slab(): lax.ppermute(values, 'slab', [(q, q ^ step) for q in range(devices)])]
    all_to_all x12 -> x14, waiting for transfers between devices: 34 us -> 17.4 us  [exchange(): lax.all_to_all(values, 'slab', 0, 0, tiled=True, axis_index_groups=in_layer)]
    pallas_call x18, Pallas kernels: 35.6 us -> 24.9 us  [cross_terms(): pl.pallas_call(kernel, grid=(rows,), in_specs=specs, out_specs=[rows_of(s...]
    ppermute x54 -> x72, starting transfers between devices: 144 us -> 153 us  [move(): lax.ppermute(values, 'slab', [(a * peers + q, b * peers + q) for a, b in...]
  transfers between devices with their start and end apart: 66 -> 90, of which waited for: 53 -> 42; matrix products, arithmetic and copies ran while one was open for 0% -> 0% of each run, Pallas kernels for 16% -> 18%
where the time goes in v2:
time: 815 us; the launch traced here: 806 us
  waiting for transfers between devices  334 us (41%)
  starting transfers between devices  217 us (27%)
  Pallas kernels  167 us (20%)
  local copies, waits for them, and re-layouts  82.1 us (10%)
    ppermute x72, waiting for transfers between devices, move(): lax.ppermute(values, 'slab', [(a * peers + q, b * peers + q) for a, b in...  289 us
    ppermute x72, starting transfers between devices, move(): lax.ppermute(values, 'slab', [(a * peers + q, b * peers + q) for a, b in...  153 us
    pallas_call x18, Pallas kernels, cells(): pl.pallas_call(kernel, grid=(rows,), in_specs=specs, out_specs=out_specs,...  85.1 us
    unnamed x390, local copies, waits for them, and re-layouts  80.1 us
    all_to_all x14, starting transfers between devices, exchange(): lax.all_to_all(values, 'slab', 0, 0, tiled=True, axis_index_groups=in_layer)  59.4 us
    ppermute x4, waiting for transfers between devices, sum_over_slab(): lax.ppermute(values, 'slab', [(q, q ^ step) for q in range(devices)])  27.9 us
    pallas_call x18, Pallas kernels, cross_terms(): pl.pallas_call(kernel, grid=(rows,), in_specs=specs, out_specs=[rows_of(s...  24.9 us
    pallas_call x6, Pallas kernels, packed(): pl.pallas_call(kernel, grid=(peers, rows // band), in_specs=[source, sour...  20.5 us
  transfers between devices with their start and end apart: 90, of which 42 were waited for; matrix products, arithmetic and copies ran while one was open for 0% of the time, Pallas kernels for 18%

profile of v2, /device:TPU:18, one launch (start us, length us, event | category | flops | bytes accessed | tf_op | source)
XLA Modules:
  0.0 805.7 jit_solution(13730066280470544425)
XLA Ops:
  8.3 18.2 %field.1 = (f32[32,2,32,128]{3,2,1,0:T(8,128)S(1)}, f32[64,2,32,128]{3,2,1,0:T(8,128)S(1)}, f32[64,2,32,128]{3,2,1,0:T(8,128)S(1)}, f32[96,2,32,128]{3,2,1,0:T(8,128)}, f32[8,256]{1,0:T(8,128)S(1)}) custom-call(f32[32,256,256]{2,1,0:T(8,128)} %w.3, bf16[256,256]{1,0:T(8,128)(2,1)S(1)} %get-tuple-element.137.north_high, ...), custom_call_target="tpu_custom_call" | custom-call | flops 1 | bytes 1 | tf_op jit(solution)/shard_map/field/pallas_call | solution.py:151
  80.1 5.3 collective-permute-done.1.rest_1_.refs_6_
  85.3 5.2 collective-permute-done.rest_0_.refs_5_
  98.5 5.5 collective-permute-done.5.rest_1_.refs_6_
  104.0 15.4 %collective-permute-done.4.rest_0_.refs_5_ = f32[4,4,1,32,128]{4,3,2,1,0:T(8,128)S(1)} collective-permute-done((f32[4,4,1,32,128]{4,3,2,1,0:T(8,128)S(1)}, f32[4,4,1,32,128]{4,3,2,1,0:T(8,128)S(1)}, u32[]{:S(2)}, u32[]{:S(2)}) %collective-permute-start.4) | collective-permute-done | bytes 262176 | tf_op jit(solution)/shard_map/ppermute | solution.py:438
  146.3 18.1 %collective-permute-done.6.rest_0_.refs_5_ = f32[4,4,1,32,128]{4,3,2,1,0:T(8,128)S(1)} collective-permute-done((f32[4,4,1,32,128]{4,3,2,1,0:T(8,128)}, f32[4,4,1,32,128]{4,3,2,1,0:T(8,128)S(1)}, u32[]{:S(2)}, u32[]{:S(2)}) %collective-permute-start.6) | collective-permute-done | bytes 262176 | tf_op jit(solution)/shard_map/ppermute | solution.py:438
  164.4 5.2 collective-permute-done.7.rest_1_.refs_6_
  184.7 5.7 collective-permute-start.8
  192.5 13.2 %collective-permute-done.12.rest_0_.refs_5_ = f32[4,4,1,32,128]{4,3,2,1,0:T(8,128)S(1)} collective-permute-done((f32[4,4,1,32,128]{4,3,2,1,0:T(8,128)}, f32[4,4,1,32,128]{4,3,2,1,0:T(8,128)S(1)}, u32[]{:S(2)}, u32[]{:S(2)}) %collective-permute-start.12) | collective-permute-done | bytes 262176 | tf_op jit(solution)/shard_map/ppermute | solution.py:438
  205.7 5.5 collective-permute-done.13.rest_1_.refs_6_
  212.7 5.3 cells.20
  225.3 5.4 collective-permute-start.18
  232.9 13.2 %collective-permute-done.14.rest_0_.refs_5_ = f32[4,4,1,32,128]{4,3,2,1,0:T(8,128)S(1)} collective-permute-done((f32[4,4,1,32,128]{4,3,2,1,0:T(8,128)}, f32[4,4,1,32,128]{4,3,2,1,0:T(8,128)S(1)}, u32[]{:S(2)}, u32[]{:S(2)}) %collective-permute-start.14) | collective-permute-done | bytes 262176 | tf_op jit(solution)/shard_map/ppermute | solution.py:438
  246.1 5.5 collective-permute-done.15.rest_1_.refs_6_
  257.5 5.1 cells.21
  273.1 5.2 collective-permute-start.16
  280.3 13.2 %collective-permute-done.20.rest_0_.refs_5_ = f32[4,4,1,32,128]{4,3,2,1,0:T(8,128)S(1)} collective-permute-done((f32[4,4,1,32,128]{4,3,2,1,0:T(8,128)}, f32[4,4,1,32,128]{4,3,2,1,0:T(8,128)S(1)}, u32[]{:S(2)}, u32[]{:S(2)}) %collective-permute-start.20) | collective-permute-done | bytes 262176 | tf_op jit(solution)/shard_map/ppermute | solution.py:438
  293.5 5.5 collective-permute-done.21.rest_1_.refs_6_
  304.7 5.3 collective-permute-start.26
  310.1 5.5 cells.22
  317.7 7.2 collective-permute-done.22.rest_0_.refs_5_
  324.9 5.2 collective-permute-done.23.rest_1_.refs_6_
  332.3 5.5 cells.23
  345.4 5.1 collective-permute-start.24
  352.6 13.2 %collective-permute-done.28.rest_0_.refs_5_ = f32[4,4,1,32,128]{4,3,2,1,0:T(8,128)S(1)} collective-permute-done((f32[4,4,1,32,128]{4,3,2,1,0:T(8,128)}, f32[4,4,1,32,128]{4,3,2,1,0:T(8,128)S(1)}, u32[]{:S(2)}, u32[]{:S(2)}) %collective-permute-start.28) | collective-permute-done | bytes 262176 | tf_op jit(solution)/shard_map/ppermute | solution.py:438
  365.8 5.5 collective-permute-done.29.rest_1_.refs_6_
  377.1 5.1 collective-permute-start.34
  382.3 5.2 cells.24
  389.5 7.3 collective-permute-done.30.rest_0_.refs_5_
  396.8 5.5 collective-permute-done.31.rest_1_.refs_6_
  403.8 5.4 cells.25
  419.5 5.0 collective-permute-start.32
  426.7 13.2 %collective-permute-done.36.rest_0_.refs_5_ = f32[4,4,1,32,128]{4,3,2,1,0:T(8,128)S(1)} collective-permute-done((f32[4,4,1,32,128]{4,3,2,1,0:T(8,128)}, f32[4,4,1,32,128]{4,3,2,1,0:T(8,128)S(1)}, u32[]{:S(2)}, u32[]{:S(2)}) %collective-permute-start.36) | collective-permute-done | bytes 262176 | tf_op jit(solution)/shard_map/ppermute | solution.py:438
  439.9 5.5 collective-permute-done.37.rest_1_.refs_6_
  451.2 5.0 collective-permute-start.38
  456.4 5.6 cells.26
  464.0 7.2 collective-permute-done.40.rest_0_.refs_5_
  471.2 5.3 collective-permute-done.41.rest_1_.refs_6_
  478.0 5.2 cells.27
  486.7 5.0 all-to-all-start.8
  493.9 5.0 collective-permute-start.42
  501.0 13.2 %collective-permute-done.44.rest_0_.refs_5_ = f32[4,4,1,32,128]{4,3,2,1,0:T(8,128)S(1)} collective-permute-done((f32[4,4,1,32,128]{4,3,2,1,0:T(8,128)}, f32[4,4,1,32,128]{4,3,2,1,0:T(8,128)S(1)}, u32[]{:S(2)}, u32[]{:S(2)}) %collective-permute-start.44) | collective-permute-done | bytes 262176 | tf_op jit(solution)/shard_map/ppermute | solution.py:438
  514.1 5.5 collective-permute-done.45.rest_1_.refs_6_
  525.0 5.0 collective-permute-start.50
  530.1 5.1 cells.28
  537.2 7.6 collective-permute-done.46.rest_0_.refs_5_
  544.8 5.5 collective-permute-done.47.rest_1_.refs_6_
  552.7 5.0 cells.29
  568.1 5.2 collective-permute-start.48
  575.4 12.9 %collective-permute-done.52.rest_0_.refs_5_ = f32[4,4,1,32,128]{4,3,2,1,0:T(8,128)S(1)} collective-permute-done((f32[4,4,1,32,128]{4,3,2,1,0:T(8,128)}, f32[4,4,1,32,128]{4,3,2,1,0:T(8,128)S(1)}, u32[]{:S(2)}, u32[]{:S(2)}) %collective-permute-start.52) | collective-permute-done | bytes 262176 | tf_op jit(solution)/shard_map/ppermute | solution.py:438
  588.3 5.5 collective-permute-done.53.rest_1_.refs_6_
  596.5 5.1 cells.30
  612.2 4.9 collective-permute-start.54
  619.2 13.2 %collective-permute-done.56.rest_0_.refs_5_ = f32[4,4,1,32,128]{4,3,2,1,0:T(8,128)S(1)} collective-permute-done((f32[4,4,1,32,128]{4,3,2,1,0:T(8,128)}, f32[4,4,1,32,128]{4,3,2,1,0:T(8,128)S(1)}, u32[]{:S(2)}, u32[]{:S(2)}) %collective-permute-start.56) | collective-permute-done | bytes 262176 | tf_op jit(solution)/shard_map/ppermute | solution.py:438
  632.4 5.5 collective-permute-done.57.rest_1_.refs_6_
  642.1 4.9 collective-permute-start.62
  647.1 5.1 cells.31
  654.3 7.3 collective-permute-done.58.rest_0_.refs_5_
  661.6 5.5 collective-permute-done.59.rest_1_.refs_6_
  682.7 8.5 %collective-permute-done.64.rest_0_.refs_5_ = f32[4,4,1,32,128]{4,3,2,1,0:T(8,128)S(1)} collective-permute-done((f32[4,4,1,32,128]{4,3,2,1,0:T(8,128)S(1)}, f32[4,4,1,32,128]{4,3,2,1,0:T(8,128)S(1)}, u32[]{:S(2)}, u32[]{:S(2)}) %collective-permute-start.64) | collective-permute-done | bytes 262176 | tf_op jit(solution)/shard_map/ppermute | solution.py:438
  720.6 5.2 collective-permute-done.67.rest_1_.refs_6_
  740.3 21.1 %collective-permute-done.73 = f32[8,256]{1,0:T(8,128)S(1)} collective-permute-done((f32[8,256]{1,0:T(8,128)S(1)}, f32[8,256]{1,0:T(8,128)S(1)}, u32[]{:S(2)}, u32[]{:S(2)}) %collective-permute-start.73) | collective-permute-done | bytes 8224 | tf_op jit(solution)/shard_map/ppermute | solution.py:456
  772.8 13.8 %all-to-all-done.13 = f32[4,8,2,32,128]{4,3,2,1,0:T(8,128)S(1)} async-done(((f32[4,8,2,32,128]{4,3,2,1,0:T(8,128)}), f32[4,8,2,32,128]{4,3,2,1,0:T(8,128)S(1)}, u32[]{:S(2)}, u32[]{:S(2)}) %all-to-all-start.13) | async-done | bytes 1048608 | tf_op jit(solution)/shard_map/all_to_all | solution.py:435
  786.6 17.9 %finish.1 = f32[32,256,256]{2,1,0:T(8,128)} custom-call(f32[32,256,256]{2,1,0:T(8,128)} %w.3, bf16[256,256]{1,0:T(8,128)(2,1)S(1)} %copy-done.155, bf16[256,256]{1,0:T(8,128)(2,1)S(1)} %copy-done.157, bf16[256,256]{1,0:T(8,128)(2,1)S(1)} %copy-done.159, bf16[256,256]{1,0:T(8,128)(2,1)S(1)} %copy-done.161, f32[112,2,32,128]{3,2,1,0:T(8,128)} %bitcast.5.refs_0_, ...), custom_call_target="tpu_custom_call" | custom-call | flops 1 | bytes 1 | tf_op jit(solution)/shard_map/finish/pallas_call | solution.py:405
  (572 shorter events, 313.5 us)
Async XLA Ops:
  4.4 29.4 %all-to-all-start = ((f32[4,2,2,32,8,128]{5,4,3,2,1,0:T(8,128)}), f32[4,2,2,32,8,128]{5,4,3,2,1,0:T(8,128)S(1)}, u32[]{:S(2)}, u32[]{:S(2)}) async-start(f32[4,2,2,32,8,128]{5,4,3,2,1,0:T(8,128)} %packed.6._), calls=%async_computation | async-start | bytes 4194304 | tf_op jit(solution)/shard_map/all_to_all | solution.py:435
  35.2 33.4 %all-to-all-start.1 = ((f32[4,8,2,32,128]{4,3,2,1,0:T(8,128)}), f32[4,8,2,32,128]{4,3,2,1,0:T(8,128)S(1)}, u32[]{:S(2)}, u32[]{:S(2)}) async-start(f32[4,8,2,32,128]{4,3,2,1,0:T(8,128)} %gate.13._.rest_0_), calls=%async_computation.1 | async-start | bytes 2097152 | tf_op jit(solution)/shard_map/all_to_all | solution.py:435
  71.4 51.6 %all-to-all-start.2 = ((f32[4,16,2,32,128]{4,3,2,1,0:T(8,128)}), f32[4,16,2,32,128]{4,3,2,1,0:T(8,128)S(1)}, u32[]{:S(2)}, u32[]{:S(2)}) async-start(f32[4,16,2,32,128]{4,3,2,1,0:T(8,128)} %gate.15), calls=%async_computation.2 | async-start | bytes 4194304 | tf_op jit(solution)/shard_map/all_to_all | solution.py:435
  90.8 30.5 %collective-permute-start.2 = (f32[4,4,2,32,128]{4,3,2,1,0:T(8,128)S(1)}, f32[4,4,2,32,128]{4,3,2,1,0:T(8,128)S(1)}, u32[]{:S(2)}, u32[]{:S(2)}) collective-permute-start(f32[4,4,2,32,128]{4,3,2,1,0:T(8,128)S(1)} %get-tuple-element.150), channel_id=1, source_target_pairs={{4,8},{5,9},{6,10},{7,11},{20,24},{21,25},{22,26},{23,27}} | collective-permute-start | bytes 1572872 | tf_op jit(solution)/shard_map/ppermute | solution.py:438
  92.1 30.0 %collective-permute-start.3 = (f32[4,4,2,32,128]{4,3,2,1,0:T(8,128)S(1)}, f32[4,4,2,32,128]{4,3,2,1,0:T(8,128)S(1)}, u32[]{:S(2)}, u32[]{:S(2)}) collective-permute-start(f32[4,4,2,32,128]{4,3,2,1,0:T(8,128)S(1)} %get-tuple-element.151), channel_id=1, source_target_pairs={{4,12},{5,13},{6,14},{7,15},{20,28},{21,29},{22,30},{23,31}} | collective-permute-start | bytes 1572872 | tf_op jit(solution)/shard_map/ppermute | solution.py:438
  97.2 22.2 %collective-permute-start.4 = (f32[4,4,1,32,128]{4,3,2,1,0:T(8,128)S(1)}, f32[4,4,1,32,128]{4,3,2,1,0:T(8,128)S(1)}, u32[]{:S(2)}, u32[]{:S(2)}) collective-permute-start(f32[4,4,1,32,128]{4,3,2,1,0:T(8,128)S(1)} %get-tuple-element.275), channel_id=1, source_target_pairs={{0,4},{1,5},{2,6},{3,7},{8,12},{9,13},{10,14},{11,15},{16,20},{17,... | collective-permute-start | bytes 786440 | tf_op jit(solution)/shard_map/ppermute | solution.py:438
  137.0 41.5 %all-to-all-start.3 = ((f32[4,2,2,32,8,128]{5,4,3,2,1,0:T(8,128)}), f32[4,2,2,32,8,128]{5,4,3,2,1,0:T(8,128)}, u32[]{:S(2)}, u32[]{:S(2)}) async-start(f32[4,2,2,32,8,128]{5,4,3,2,1,0:T(8,128)} %gate.16), calls=%async_computation.3 | async-start | bytes 4194304 | tf_op jit(solution)/shard_map/all_to_all | solution.py:435
  141.6 30.5 %collective-permute-start.11 = (f32[4,4,2,32,128]{4,3,2,1,0:T(8,128)}, f32[4,4,2,32,128]{4,3,2,1,0:T(8,128)S(1)}, u32[]{:S(2)}, u32[]{:S(2)}) collective-permute-start(f32[4,4,2,32,128]{4,3,2,1,0:T(8,128)} %copy-done.170), channel_id=1, source_target_pairs={{4,12},{5,13},{6,14},{7,15},{20,28},{21,29},{22,30},{23,31}} | collective-permute-start | bytes 1572872 | tf_op jit(solution)/shard_map/ppermute | solution.py:438
  142.4 29.7 %collective-permute-start.10 = (f32[4,4,2,32,128]{4,3,2,1,0:T(8,128)}, f32[4,4,2,32,128]{4,3,2,1,0:T(8,128)S(1)}, u32[]{:S(2)}, u32[]{:S(2)}) collective-permute-start(f32[4,4,2,32,128]{4,3,2,1,0:T(8,128)} %copy-done.146), channel_id=1, source_target_pairs={{4,8},{5,9},{6,10},{7,11},{20,24},{21,25},{22,26},{23,27}} | collective-permute-start | bytes 1572872 | tf_op jit(solution)/shard_map/ppermute | solution.py:438
  143.7 20.7 %collective-permute-start.6 = (f32[4,4,1,32,128]{4,3,2,1,0:T(8,128)}, f32[4,4,1,32,128]{4,3,2,1,0:T(8,128)S(1)}, u32[]{:S(2)}, u32[]{:S(2)}) collective-permute-start(f32[4,4,1,32,128]{4,3,2,1,0:T(8,128)} %copy-done.193), channel_id=1, source_target_pairs={{0,4},{1,5},{2,6},{3,7},{8,12},{9,13},{10,14},{11,15},{4,0},{5,1},... | collective-permute-start | bytes 786440 | tf_op jit(solution)/shard_map/ppermute | solution.py:438
  146.2 23.3 %collective-permute-start.7 = (f32[4,4,1,32,128]{4,3,2,1,0:T(8,128)}, f32[4,4,1,32,128]{4,3,2,1,0:T(8,128)S(1)}, u32[]{:S(2)}, u32[]{:S(2)}) collective-permute-start(f32[4,4,1,32,128]{4,3,2,1,0:T(8,128)} %copy-done.192), channel_id=1, source_target_pairs={{0,4},{1,5},{2,6},{3,7},{8,12},{9,13},{10,14},{11,15},{4,0},{5,1},... | collective-permute-start | bytes 786440 | tf_op jit(solution)/shard_map/ppermute | solution.py:438
  178.5 41.8 %all-to-all-start.4 = ((f32[4,2,2,32,8,128]{5,4,3,2,1,0:T(8,128)}), f32[4,2,2,32,8,128]{5,4,3,2,1,0:T(8,128)}, u32[]{:S(2)}, u32[]{:S(2)}) async-start(f32[4,2,2,32,8,128]{5,4,3,2,1,0:T(8,128)} %gate.17), calls=%async_computation.4 | async-start | bytes 4194304 | tf_op jit(solution)/shard_map/all_to_all | solution.py:435
  183.2 29.4 %collective-permute-start.9 = (f32[4,4,2,32,128]{4,3,2,1,0:T(8,128)}, f32[4,4,2,32,128]{4,3,2,1,0:T(8,128)S(1)}, u32[]{:S(2)}, u32[]{:S(2)}) collective-permute-start(f32[4,4,2,32,128]{4,3,2,1,0:T(8,128)} %copy-done.168), channel_id=1, source_target_pairs={{4,12},{5,13},{6,14},{7,15},{8,0},{9,1},{10,2},{11,3},{20,28},{21,... | collective-permute-start | bytes 1572872 | tf_op jit(solution)/shard_map/ppermute | solution.py:438
  184.7 27.9 %collective-permute-start.8 = (f32[4,4,2,32,128]{4,3,2,1,0:T(8,128)}, f32[4,4,2,32,128]{4,3,2,1,0:T(8,128)S(1)}, u32[]{:S(2)}, u32[]{:S(2)}) collective-permute-start(f32[4,4,2,32,128]{4,3,2,1,0:T(8,128)} %copy-done.145), channel_id=1, source_target_pairs={{4,8},{5,9},{6,10},{7,11},{8,4},{9,5},{10,6},{11,7},{20,24},{21,25... | collective-permute-start | bytes 1572872 | tf_op jit(solution)/shard_map/ppermute | solution.py:438
  190.5 20.6 %collective-permute-start.13 = (f32[4,4,1,32,128]{4,3,2,1,0:T(8,128)S(1)}, f32[4,4,1,32,128]{4,3,2,1,0:T(8,128)S(1)}, u32[]{:S(2)}, u32[]{:S(2)}) collective-permute-start(f32[4,4,1,32,128]{4,3,2,1,0:T(8,128)S(1)} %copy-done.182), channel_id=1, source_target_pairs={{0,4},{1,5},{2,6},{3,7},{8,12},{9,13},{10,14},{11,15},{4,0},{5,1},... | collective-permute-start | bytes 786440 | tf_op jit(solution)/shard_map/ppermute | solution.py:438
  220.2 44.7 %all-to-all-start.5 = ((f32[4,16,2,32,128]{4,3,2,1,0:T(8,128)}), f32[4,16,2,32,128]{4,3,2,1,0:T(8,128)S(1)}, u32[]{:S(2)}, u32[]{:S(2)}) async-start(f32[4,16,2,32,128]{4,3,2,1,0:T(8,128)} %gate.18), calls=%async_computation.5 | async-start | bytes 4194304 | tf_op jit(solution)/shard_map/all_to_all | solution.py:435
  224.0 31.4 %collective-permute-start.19 = (f32[4,4,2,32,128]{4,3,2,1,0:T(8,128)}, f32[4,4,2,32,128]{4,3,2,1,0:T(8,128)S(1)}, u32[]{:S(2)}, u32[]{:S(2)}) collective-permute-start(f32[4,4,2,32,128]{4,3,2,1,0:T(8,128)} %copy-done.169), channel_id=1, source_target_pairs={{4,12},{5,13},{6,14},{7,15},{8,0},{9,1},{10,2},{11,3},{20,28},{21,... | collective-permute-start | bytes 1572872 | tf_op jit(solution)/shard_map/ppermute | solution.py:438
  225.3 30.1 %collective-permute-start.18 = (f32[4,4,2,32,128]{4,3,2,1,0:T(8,128)}, f32[4,4,2,32,128]{4,3,2,1,0:T(8,128)S(1)}, u32[]{:S(2)}, u32[]{:S(2)}) collective-permute-start(f32[4,4,2,32,128]{4,3,2,1,0:T(8,128)} %copy-done.153), channel_id=1, source_target_pairs={{4,8},{5,9},{6,10},{7,11},{8,4},{9,5},{10,6},{11,7},{20,24},{21,25... | collective-permute-start | bytes 1572872 | tf_op jit(solution)/shard_map/ppermute | solution.py:438
  230.8 15.3 %collective-permute-start.14 = (f32[4,4,1,32,128]{4,3,2,1,0:T(8,128)}, f32[4,4,1,32,128]{4,3,2,1,0:T(8,128)S(1)}, u32[]{:S(2)}, u32[]{:S(2)}) collective-permute-start(f32[4,4,1,32,128]{4,3,2,1,0:T(8,128)} %copy-done.190), channel_id=1, source_target_pairs={{0,4},{1,5},{2,6},{3,7},{8,12},{9,13},{10,14},{11,15},{4,0},{5,1},... | collective-permute-start | bytes 786440 | tf_op jit(solution)/shard_map/ppermute | solution.py:438
  230.9 20.7 %collective-permute-start.15 = (f32[4,4,1,32,128]{4,3,2,1,0:T(8,128)}, f32[4,4,1,32,128]{4,3,2,1,0:T(8,128)S(1)}, u32[]{:S(2)}, u32[]{:S(2)}) collective-permute-start(f32[4,4,1,32,128]{4,3,2,1,0:T(8,128)} %copy-done.183), channel_id=1, source_target_pairs={{0,4},{1,5},{2,6},{3,7},{8,12},{9,13},{10,14},{11,15},{4,0},{5,1},... | collective-permute-start | bytes 786440 | tf_op jit(solution)/shard_map/ppermute | solution.py:438
  266.2 73.8 %all-to-all-start.6 = ((f32[4,2,2,32,16,128]{5,4,3,2,1,0:T(8,128)}), f32[4,2,2,32,16,128]{5,4,3,2,1,0:T(8,128)}, u32[]{:S(2)}, u32[]{:S(2)}) async-start(f32[4,2,2,32,16,128]{5,4,3,2,1,0:T(8,128)} %gate.19), calls=%async_computation.6 | async-start | bytes 8388608 | tf_op jit(solution)/shard_map/all_to_all | solution.py:435
  271.1 39.0 %collective-permute-start.17 = (f32[4,4,2,32,128]{4,3,2,1,0:T(8,128)}, f32[4,4,2,32,128]{4,3,2,1,0:T(8,128)S(1)}, u32[]{:S(2)}, u32[]{:S(2)}) collective-permute-start(f32[4,4,2,32,128]{4,3,2,1,0:T(8,128)} %copy-done.163), channel_id=1, source_target_pairs={{4,12},{5,13},{6,14},{7,15},{8,0},{9,1},{10,2},{11,3},{20,28},{21,... | collective-permute-start | bytes 1572872 | tf_op jit(solution)/shard_map/ppermute | solution.py:438
  273.1 37.0 %collective-permute-start.16 = (f32[4,4,2,32,128]{4,3,2,1,0:T(8,128)}, f32[4,4,2,32,128]{4,3,2,1,0:T(8,128)S(1)}, u32[]{:S(2)}, u32[]{:S(2)}) collective-permute-start(f32[4,4,2,32,128]{4,3,2,1,0:T(8,128)} %copy-done.141), channel_id=1, source_target_pairs={{4,8},{5,9},{6,10},{7,11},{8,4},{9,5},{10,6},{11,7},{20,24},{21,25... | collective-permute-start | bytes 1572872 | tf_op jit(solution)/shard_map/ppermute | solution.py:438
  278.3 20.7 %collective-permute-start.21 = (f32[4,4,1,32,128]{4,3,2,1,0:T(8,128)}, f32[4,4,1,32,128]{4,3,2,1,0:T(8,128)S(1)}, u32[]{:S(2)}, u32[]{:S(2)}) collective-permute-start(f32[4,4,1,32,128]{4,3,2,1,0:T(8,128)} %copy-done.175), channel_id=1, source_target_pairs={{0,4},{1,5},{2,6},{3,7},{8,12},{9,13},{10,14},{11,15},{4,0},{5,1},... | collective-permute-start | bytes 786440 | tf_op jit(solution)/shard_map/ppermute | solution.py:438
  303.1 29.2 %collective-permute-start.27 = (f32[4,4,2,32,128]{4,3,2,1,0:T(8,128)S(1)}, f32[4,4,2,32,128]{4,3,2,1,0:T(8,128)S(1)}, u32[]{:S(2)}, u32[]{:S(2)}) collective-permute-start(f32[4,4,2,32,128]{4,3,2,1,0:T(8,128)S(1)} %get-tuple-element.191), channel_id=1, source_target_pairs={{4,12},{5,13},{6,14},{7,15},{8,0},{9,1},{10,2},{11,3},{20,28},{21,... | collective-permute-start | bytes 1572872 | tf_op jit(solution)/shard_map/ppermute | solution.py:438
  304.7 27.6 %collective-permute-start.26 = (f32[4,4,2,32,128]{4,3,2,1,0:T(8,128)S(1)}, f32[4,4,2,32,128]{4,3,2,1,0:T(8,128)S(1)}, u32[]{:S(2)}, u32[]{:S(2)}) collective-permute-start(f32[4,4,2,32,128]{4,3,2,1,0:T(8,128)S(1)} %get-tuple-element.182.refs_7_), channel_id=1, source_target_pairs={{4,8},{5,9},{6,10},{7,11},{8,4},{9,5},{10,6},{11,7},{20,24},{21,25... | collective-permute-start | bytes 1572872 | tf_op jit(solution)/shard_map/ppermute | solution.py:438
  340.1 71.3 %all-to-all-start.7 = ((f32[4,24,2,32,128]{4,3,2,1,0:T(8,128)}), f32[4,24,2,32,128]{4,3,2,1,0:T(8,128)S(1)}, u32[]{:S(2)}, u32[]{:S(2)}) async-start(f32[4,24,2,32,128]{4,3,2,1,0:T(8,128)} %gate.20), calls=%async_computation.7 | async-start | bytes 6291456 | tf_op jit(solution)/shard_map/all_to_all | solution.py:435
  343.8 38.4 %collective-permute-start.25 = (f32[4,4,2,32,128]{4,3,2,1,0:T(8,128)}, f32[4,4,2,32,128]{4,3,2,1,0:T(8,128)S(1)}, u32[]{:S(2)}, u32[]{:S(2)}) collective-permute-start(f32[4,4,2,32,128]{4,3,2,1,0:T(8,128)} %copy-done.162), channel_id=1, source_target_pairs={{4,12},{5,13},{6,14},{7,15},{8,0},{9,1},{10,2},{11,3},{20,28},{21,... | collective-permute-start | bytes 1572872 | tf_op jit(solution)/shard_map/ppermute | solution.py:438
  345.4 36.8 %collective-permute-start.24 = (f32[4,4,2,32,128]{4,3,2,1,0:T(8,128)}, f32[4,4,2,32,128]{4,3,2,1,0:T(8,128)S(1)}, u32[]{:S(2)}, u32[]{:S(2)}) collective-permute-start(f32[4,4,2,32,128]{4,3,2,1,0:T(8,128)} %copy-done.140), channel_id=1, source_target_pairs={{4,8},{5,9},{6,10},{7,11},{8,4},{9,5},{10,6},{11,7},{20,24},{21,25... | collective-permute-start | bytes 1572872 | tf_op jit(solution)/shard_map/ppermute | solution.py:438
  350.5 15.3 %collective-permute-start.28 = (f32[4,4,1,32,128]{4,3,2,1,0:T(8,128)}, f32[4,4,1,32,128]{4,3,2,1,0:T(8,128)S(1)}, u32[]{:S(2)}, u32[]{:S(2)}) collective-permute-start(f32[4,4,1,32,128]{4,3,2,1,0:T(8,128)} %copy-done.176), channel_id=1, source_target_pairs={{0,4},{1,5},{2,6},{3,7},{8,12},{9,13},{10,14},{11,15},{4,0},{5,1},... | collective-permute-start | bytes 786440 | tf_op jit(solution)/shard_map/ppermute | solution.py:438
  350.6 20.7 %collective-permute-start.29 = (f32[4,4,1,32,128]{4,3,2,1,0:T(8,128)}, f32[4,4,1,32,128]{4,3,2,1,0:T(8,128)S(1)}, u32[]{:S(2)}, u32[]{:S(2)}) collective-permute-start(f32[4,4,1,32,128]{4,3,2,1,0:T(8,128)} %copy-done.171), channel_id=1, source_target_pairs={{0,4},{1,5},{2,6},{3,7},{8,12},{9,13},{10,14},{11,15},{4,0},{5,1},... | collective-permute-start | bytes 786440 | tf_op jit(solution)/shard_map/ppermute | solution.py:438
  375.4 28.3 %collective-permute-start.35 = (f32[4,4,2,32,128]{4,3,2,1,0:T(8,128)S(1)}, f32[4,4,2,32,128]{4,3,2,1,0:T(8,128)S(1)}, u32[]{:S(2)}, u32[]{:S(2)}) collective-permute-start(f32[4,4,2,32,128]{4,3,2,1,0:T(8,128)S(1)} %get-tuple-element.205), channel_id=1, source_target_pairs={{4,12},{5,13},{6,14},{7,15},{8,0},{9,1},{10,2},{11,3},{20,28},{21,... | collective-permute-start | bytes 1572872 | tf_op jit(solution)/shard_map/ppermute | solution.py:438
  377.1 26.6 %collective-permute-start.34 = (f32[4,4,2,32,128]{4,3,2,1,0:T(8,128)S(1)}, f32[4,4,2,32,128]{4,3,2,1,0:T(8,128)S(1)}, u32[]{:S(2)}, u32[]{:S(2)}) collective-permute-start(f32[4,4,2,32,128]{4,3,2,1,0:T(8,128)S(1)} %get-tuple-element.197.refs_7_), channel_id=1, source_target_pairs={{4,8},{5,9},{6,10},{7,11},{8,4},{9,5},{10,6},{11,7},{20,24},{21,25... | collective-permute-start | bytes 1572872 | tf_op jit(solution)/shard_map/ppermute | solution.py:438
  413.0 73.7 %all-to-all-start.9 = ((f32[4,2,2,32,16,128]{5,4,3,2,1,0:T(8,128)}), f32[4,2,2,32,16,128]{5,4,3,2,1,0:T(8,128)}, u32[]{:S(2)}, u32[]{:S(2)}) async-start(f32[4,2,2,32,16,128]{5,4,3,2,1,0:T(8,128)} %gate.22), calls=%async_computation.9 | async-start | bytes 8388608 | tf_op jit(solution)/shard_map/all_to_all | solution.py:435
  417.9 38.4 %collective-permute-start.33 = (f32[4,4,2,32,128]{4,3,2,1,0:T(8,128)}, f32[4,4,2,32,128]{4,3,2,1,0:T(8,128)S(1)}, u32[]{:S(2)}, u32[]{:S(2)}) collective-permute-start(f32[4,4,2,32,128]{4,3,2,1,0:T(8,128)} %copy-done.165), channel_id=1, source_target_pairs={{4,12},{5,13},{6,14},{7,15},{8,0},{9,1},{10,2},{11,3},{20,28},{21,... | collective-permute-start | bytes 1572872 | tf_op jit(solution)/shard_map/ppermute | solution.py:438
  419.5 36.7 %collective-permute-start.32 = (f32[4,4,2,32,128]{4,3,2,1,0:T(8,128)}, f32[4,4,2,32,128]{4,3,2,1,0:T(8,128)S(1)}, u32[]{:S(2)}, u32[]{:S(2)}) collective-permute-start(f32[4,4,2,32,128]{4,3,2,1,0:T(8,128)} %copy-done.142), channel_id=1, source_target_pairs={{4,8},{5,9},{6,10},{7,11},{8,4},{9,5},{10,6},{11,7},{20,24},{21,25... | collective-permute-start | bytes 1572872 | tf_op jit(solution)/shard_map/ppermute | solution.py:438
  424.7 20.7 %collective-permute-start.37 = (f32[4,4,1,32,128]{4,3,2,1,0:T(8,128)}, f32[4,4,1,32,128]{4,3,2,1,0:T(8,128)S(1)}, u32[]{:S(2)}, u32[]{:S(2)}) collective-permute-start(f32[4,4,1,32,128]{4,3,2,1,0:T(8,128)} %copy-done.177), channel_id=1, source_target_pairs={{0,4},{1,5},{2,6},{3,7},{8,12},{9,13},{10,14},{11,15},{4,0},{5,1},... | collective-permute-start | bytes 786440 | tf_op jit(solution)/shard_map/ppermute | solution.py:438
  449.5 28.4 %collective-permute-start.39 = (f32[4,4,2,32,128]{4,3,2,1,0:T(8,128)S(1)}, f32[4,4,2,32,128]{4,3,2,1,0:T(8,128)S(1)}, u32[]{:S(2)}, u32[]{:S(2)}) collective-permute-start(f32[4,4,2,32,128]{4,3,2,1,0:T(8,128)S(1)} %get-tuple-element.216), channel_id=1, source_target_pairs={{4,12},{5,13},{6,14},{7,15},{8,0},{9,1},{10,2},{11,3},{20,28},{21,... | collective-permute-start | bytes 1572872 | tf_op jit(solution)/shard_map/ppermute | solution.py:438
  451.2 26.7 %collective-permute-start.38 = (f32[4,4,2,32,128]{4,3,2,1,0:T(8,128)S(1)}, f32[4,4,2,32,128]{4,3,2,1,0:T(8,128)S(1)}, u32[]{:S(2)}, u32[]{:S(2)}) collective-permute-start(f32[4,4,2,32,128]{4,3,2,1,0:T(8,128)S(1)} %get-tuple-element.211.refs_7_), channel_id=1, source_target_pairs={{4,8},{5,9},{6,10},{7,11},{8,4},{9,5},{10,6},{11,7},{20,24},{21,25... | collective-permute-start | bytes 1572872 | tf_op jit(solution)/shard_map/ppermute | solution.py:438
  486.7 74.6 %all-to-all-start.8 = ((f32[4,28,2,32,128]{4,3,2,1,0:T(8,128)}), f32[4,28,2,32,128]{4,3,2,1,0:T(8,128)}, u32[]{:S(2)}, u32[]{:S(2)}) async-start(f32[4,28,2,32,128]{4,3,2,1,0:T(8,128)} %gate.21), calls=%async_computation.8 | async-start | bytes 7340032 | tf_op jit(solution)/shard_map/all_to_all | solution.py:435
  491.7 38.2 %collective-permute-start.43 = (f32[4,4,2,32,128]{4,3,2,1,0:T(8,128)}, f32[4,4,2,32,128]{4,3,2,1,0:T(8,128)S(1)}, u32[]{:S(2)}, u32[]{:S(2)}) collective-permute-start(f32[4,4,2,32,128]{4,3,2,1,0:T(8,128)} %copy-done.164), channel_id=1, source_target_pairs={{4,12},{5,13},{6,14},{7,15},{8,0},{9,1},{10,2},{11,3},{20,28},{21,... | collective-permute-start | bytes 1572872 | tf_op jit(solution)/shard_map/ppermute | solution.py:438
  493.9 36.1 %collective-permute-start.42 = (f32[4,4,2,32,128]{4,3,2,1,0:T(8,128)}, f32[4,4,2,32,128]{4,3,2,1,0:T(8,128)S(1)}, u32[]{:S(2)}, u32[]{:S(2)}) collective-permute-start(f32[4,4,2,32,128]{4,3,2,1,0:T(8,128)} %copy-done.152), channel_id=1, source_target_pairs={{4,8},{5,9},{6,10},{7,11},{8,4},{9,5},{10,6},{11,7},{20,24},{21,25... | collective-permute-start | bytes 1572872 | tf_op jit(solution)/shard_map/ppermute | solution.py:438
  499.0 20.7 %collective-permute-start.45 = (f32[4,4,1,32,128]{4,3,2,1,0:T(8,128)}, f32[4,4,1,32,128]{4,3,2,1,0:T(8,128)S(1)}, u32[]{:S(2)}, u32[]{:S(2)}) collective-permute-start(f32[4,4,1,32,128]{4,3,2,1,0:T(8,128)} %copy-done.174), channel_id=1, source_target_pairs={{0,4},{1,5},{2,6},{3,7},{8,12},{9,13},{10,14},{11,15},{4,0},{5,1},... | collective-permute-start | bytes 786440 | tf_op jit(solution)/shard_map/ppermute | solution.py:438
  523.1 29.6 %collective-permute-start.51 = (f32[4,4,2,32,128]{4,3,2,1,0:T(8,128)}, f32[4,4,2,32,128]{4,3,2,1,0:T(8,128)S(1)}, u32[]{:S(2)}, u32[]{:S(2)}) collective-permute-start(f32[4,4,2,32,128]{4,3,2,1,0:T(8,128)} %get-tuple-element.234), channel_id=1, source_target_pairs={{4,12},{5,13},{6,14},{7,15},{8,0},{9,1},{10,2},{11,3},{20,28},{21,... | collective-permute-start | bytes 1572872 | tf_op jit(solution)/shard_map/ppermute | solution.py:438
  525.0 27.7 %collective-permute-start.50 = (f32[4,4,2,32,128]{4,3,2,1,0:T(8,128)S(1)}, f32[4,4,2,32,128]{4,3,2,1,0:T(8,128)S(1)}, u32[]{:S(2)}, u32[]{:S(2)}) collective-permute-start(f32[4,4,2,32,128]{4,3,2,1,0:T(8,128)S(1)} %get-tuple-element.226.refs_7_), channel_id=1, source_target_pairs={{4,8},{5,9},{6,10},{7,11},{8,4},{9,5},{10,6},{11,7},{20,24},{21,25... | collective-permute-start | bytes 1572872 | tf_op jit(solution)/shard_map/ppermute | solution.py:438
  561.3 43.9 %all-to-all-start.11 = ((f32[4,2,2,32,8,128]{5,4,3,2,1,0:T(8,128)}), f32[4,2,2,32,8,128]{5,4,3,2,1,0:T(8,128)}, u32[]{:S(2)}, u32[]{:S(2)}) async-start(f32[4,2,2,32,8,128]{5,4,3,2,1,0:T(8,128)} %gate.24), calls=%async_computation.11 | async-start | bytes 4194304 | tf_op jit(solution)/shard_map/all_to_all | solution.py:435
  566.0 30.4 %collective-permute-start.49 = (f32[4,4,2,32,128]{4,3,2,1,0:T(8,128)}, f32[4,4,2,32,128]{4,3,2,1,0:T(8,128)S(1)}, u32[]{:S(2)}, u32[]{:S(2)}) collective-permute-start(f32[4,4,2,32,128]{4,3,2,1,0:T(8,128)} %copy-done.167), channel_id=1, source_target_pairs={{4,12},{5,13},{6,14},{7,15},{8,0},{9,1},{10,2},{11,3},{20,28},{21,... | collective-permute-start | bytes 1572872 | tf_op jit(solution)/shard_map/ppermute | solution.py:438
  568.1 28.3 %collective-permute-start.48 = (f32[4,4,2,32,128]{4,3,2,1,0:T(8,128)}, f32[4,4,2,32,128]{4,3,2,1,0:T(8,128)S(1)}, u32[]{:S(2)}, u32[]{:S(2)}) collective-permute-start(f32[4,4,2,32,128]{4,3,2,1,0:T(8,128)} %copy-done.144), channel_id=1, source_target_pairs={{4,8},{5,9},{6,10},{7,11},{8,4},{9,5},{10,6},{11,7},{20,24},{21,25... | collective-permute-start | bytes 1572872 | tf_op jit(solution)/shard_map/ppermute | solution.py:438
  573.4 20.5 %collective-permute-start.53 = (f32[4,4,1,32,128]{4,3,2,1,0:T(8,128)}, f32[4,4,1,32,128]{4,3,2,1,0:T(8,128)S(1)}, u32[]{:S(2)}, u32[]{:S(2)}) collective-permute-start(f32[4,4,1,32,128]{4,3,2,1,0:T(8,128)} %copy-done.178), channel_id=1, source_target_pairs={{0,4},{1,5},{2,6},{3,7},{8,12},{9,13},{10,14},{11,15},{4,0},{5,1},... | collective-permute-start | bytes 786440 | tf_op jit(solution)/shard_map/ppermute | solution.py:438
  605.2 100.7 %all-to-all-start.10 = ((f32[4,16,2,32,128]{4,3,2,1,0:T(8,128)}), f32[4,16,2,32,128]{4,3,2,1,0:T(8,128)}, u32[]{:S(2)}, u32[]{:S(2)}) async-start(f32[4,16,2,32,128]{4,3,2,1,0:T(8,128)} %gate.23), calls=%async_computation.10 | async-start | bytes 4194304 | tf_op jit(solution)/shard_map/all_to_all | solution.py:435
  609.9 37.1 %collective-permute-start.55 = (f32[4,4,2,32,128]{4,3,2,1,0:T(8,128)}, f32[4,4,2,32,128]{4,3,2,1,0:T(8,128)S(1)}, u32[]{:S(2)}, u32[]{:S(2)}) collective-permute-start(f32[4,4,2,32,128]{4,3,2,1,0:T(8,128)} %copy-done.166), channel_id=1, source_target_pairs={{4,12},{5,13},{6,14},{7,15},{8,0},{9,1},{10,2},{11,3},{20,28},{21,... | collective-permute-start | bytes 1572872 | tf_op jit(solution)/shard_map/ppermute | solution.py:438
  612.2 34.9 %collective-permute-start.54 = (f32[4,4,2,32,128]{4,3,2,1,0:T(8,128)}, f32[4,4,2,32,128]{4,3,2,1,0:T(8,128)S(1)}, u32[]{:S(2)}, u32[]{:S(2)}) collective-permute-start(f32[4,4,2,32,128]{4,3,2,1,0:T(8,128)} %copy-done.143), channel_id=1, source_target_pairs={{4,8},{5,9},{6,10},{7,11},{8,4},{9,5},{10,6},{11,7},{20,24},{21,25... | collective-permute-start | bytes 1572872 | tf_op jit(solution)/shard_map/ppermute | solution.py:438
  617.2 20.7 %collective-permute-start.57 = (f32[4,4,1,32,128]{4,3,2,1,0:T(8,128)}, f32[4,4,1,32,128]{4,3,2,1,0:T(8,128)S(1)}, u32[]{:S(2)}, u32[]{:S(2)}) collective-permute-start(f32[4,4,1,32,128]{4,3,2,1,0:T(8,128)} %copy-done.185), channel_id=1, source_target_pairs={{0,4},{1,5},{2,6},{3,7},{8,12},{9,13},{10,14},{11,15},{4,0},{5,1},... | collective-permute-start | bytes 786440 | tf_op jit(solution)/shard_map/ppermute | solution.py:438
  640.4 34.9 %collective-permute-start.63 = (f32[4,4,2,32,128]{4,3,2,1,0:T(8,128)S(1)}, f32[4,4,2,32,128]{4,3,2,1,0:T(8,128)S(1)}, u32[]{:S(2)}, u32[]{:S(2)}) collective-permute-start(f32[4,4,2,32,128]{4,3,2,1,0:T(8,128)S(1)} %get-tuple-element.255), channel_id=1, source_target_pairs={{4,12},{5,13},{6,14},{7,15},{8,0},{9,1},{10,2},{11,3},{20,28},{21,... | collective-permute-start | bytes 1572872 | tf_op jit(solution)/shard_map/ppermute | solution.py:438
  642.1 33.2 %collective-permute-start.62 = (f32[4,4,2,32,128]{4,3,2,1,0:T(8,128)S(1)}, f32[4,4,2,32,128]{4,3,2,1,0:T(8,128)S(1)}, u32[]{:S(2)}, u32[]{:S(2)}) collective-permute-start(f32[4,4,2,32,128]{4,3,2,1,0:T(8,128)S(1)} %get-tuple-element.248.refs_7_), channel_id=1, source_target_pairs={{4,8},{5,9},{6,10},{7,11},{8,4},{9,5},{10,6},{11,7},{20,24},{21,25... | collective-permute-start | bytes 1572872 | tf_op jit(solution)/shard_map/ppermute | solution.py:438
  668.5 29.1 %collective-permute-start.61 = (f32[4,4,2,32,128]{4,3,2,1,0:T(8,128)S(1)}, f32[4,4,2,32,128]{4,3,2,1,0:T(8,128)S(1)}, u32[]{:S(2)}, u32[]{:S(2)}) collective-permute-start(f32[4,4,2,32,128]{4,3,2,1,0:T(8,128)S(1)} %get-tuple-element.254), channel_id=1, source_target_pairs={{4,12},{5,13},{6,14},{7,15},{8,0},{9,1},{10,2},{11,3},{20,28},{21,... | collective-permute-start | bytes 1572872 | tf_op jit(solution)/shard_map/ppermute | solution.py:438
  670.4 27.3 %collective-permute-start.60 = (f32[4,4,2,32,128]{4,3,2,1,0:T(8,128)S(1)}, f32[4,4,2,32,128]{4,3,2,1,0:T(8,128)S(1)}, u32[]{:S(2)}, u32[]{:S(2)}) collective-permute-start(f32[4,4,2,32,128]{4,3,2,1,0:T(8,128)S(1)} %get-tuple-element.253.refs_7_), channel_id=1, source_target_pairs={{4,8},{5,9},{6,10},{7,11},{8,4},{9,5},{10,6},{11,7},{20,24},{21,25... | collective-permute-start | bytes 1572872 | tf_op jit(solution)/shard_map/ppermute | solution.py:438
  705.9 62.6 %all-to-all-start.12 = ((f32[4,12,2,32,128]{4,3,2,1,0:T(8,128)}), f32[4,12,2,32,128]{4,3,2,1,0:T(8,128)S(1)}, u32[]{:S(2)}, u32[]{:S(2)}) async-start(f32[4,12,2,32,128]{4,3,2,1,0:T(8,128)} %gate.25), calls=%async_computation.12 | async-start | bytes 3145728 | tf_op jit(solution)/shard_map/all_to_all | solution.py:435
  712.2 49.9 %collective-permute-start.74 = (f32[4,4,2,32,128]{4,3,2,1,0:T(8,128)}, f32[4,4,2,32,128]{4,3,2,1,0:T(8,128)S(1)}, u32[]{:S(2)}, u32[]{:S(2)}) collective-permute-start(f32[4,4,2,32,128]{4,3,2,1,0:T(8,128)} %get-tuple-element.261.refs_7_), channel_id=1, source_target_pairs={{8,4},{9,5},{10,6},{11,7},{24,20},{25,21},{26,22},{27,23}} | collective-permute-start | bytes 1572872 | tf_op jit(solution)/shard_map/ppermute | solution.py:438
  715.7 46.4 %collective-permute-start.75 = (f32[4,4,2,32,128]{4,3,2,1,0:T(8,128)}, f32[4,4,2,32,128]{4,3,2,1,0:T(8,128)S(1)}, u32[]{:S(2)}, u32[]{:S(2)}) collective-permute-start(f32[4,4,2,32,128]{4,3,2,1,0:T(8,128)} %get-tuple-element.271), channel_id=1, source_target_pairs={{8,0},{9,1},{10,2},{11,3},{24,16},{25,17},{26,18},{27,19}} | collective-permute-start | bytes 1572872 | tf_op jit(solution)/shard_map/ppermute | solution.py:438
  727.1 39.1 %collective-permute-start.69 = (f32[4,4,2,32,128]{4,3,2,1,0:T(8,128)S(1)}, f32[4,4,2,32,128]{4,3,2,1,0:T(8,128)S(1)}, u32[]{:S(2)}, u32[]{:S(2)}) collective-permute-start(f32[4,4,2,32,128]{4,3,2,1,0:T(8,128)S(1)} %get-tuple-element.269), channel_id=1, source_target_pairs={{8,0},{9,1},{10,2},{11,3},{24,16},{25,17},{26,18},{27,19}} | collective-permute-start | bytes 1572872 | tf_op jit(solution)/shard_map/ppermute | solution.py:438
  728.5 37.8 %collective-permute-start.68 = (f32[4,4,2,32,128]{4,3,2,1,0:T(8,128)S(1)}, f32[4,4,2,32,128]{4,3,2,1,0:T(8,128)S(1)}, u32[]{:S(2)}, u32[]{:S(2)}) collective-permute-start(f32[4,4,2,32,128]{4,3,2,1,0:T(8,128)S(1)} %get-tuple-element.268.refs_7_), channel_id=1, source_target_pairs={{8,4},{9,5},{10,6},{11,7},{24,20},{25,21},{26,22},{27,23}} | collective-permute-start | bytes 1572872 | tf_op jit(solution)/shard_map/ppermute | solution.py:438
  738.3 23.1 %collective-permute-start.73 = (f32[8,256]{1,0:T(8,128)S(1)}, f32[8,256]{1,0:T(8,128)S(1)}, u32[]{:S(2)}, u32[]{:S(2)}) collective-permute-start(f32[8,256]{1,0:T(8,128)S(1)} %add.15), channel_id=1, source_target_pairs={{0,8},{1,9},{2,10},{3,11},{4,12},{5,13},{6,14},{7,15},{8,0},{9,1},... | collective-permute-start | bytes 24584 | tf_op jit(solution)/shard_map/ppermute | solution.py:456
  768.5 18.1 %all-to-all-start.13 = ((f32[4,8,2,32,128]{4,3,2,1,0:T(8,128)}), f32[4,8,2,32,128]{4,3,2,1,0:T(8,128)S(1)}, u32[]{:S(2)}, u32[]{:S(2)}) async-start(f32[4,8,2,32,128]{4,3,2,1,0:T(8,128)} %cells.35), calls=%async_computation.13 | async-start | bytes 2097152 | tf_op jit(solution)/shard_map/all_to_all | solution.py:435
  (221 other events, 1796.3 us)

commit v3 on v2

--- a/solution.py
+++ b/solution.py
@@ -11,10 +11,9 @@
 layers = 4
 chunk_target = 16
 lanes = 128
-ends_of = {"field": (2, 6, 10), "cells": (2, 4, 6, 10, 14), "gradient": (7, 11, 14)}
+ends_of = {"field": (2, 10), "cells": (2, 6, 10), "gradient": (7, 11, 14)}
 transfers = (
-    ("cells", 1, 1), ("cells", 2, 2), ("field", 2, 3), ("cells", 3, 4), ("field", 3, 6), ("cells", 4, 8), ("gradient", 0, 10),
-    ("cells", 5, 12), ("gradient", 1, 13), ("gradient", 2, 16), ("gradient", 3, 18),
+    ("cells", 1, 1), ("cells", 2, 3), ("field", 2, 5), ("cells", 3, 7), ("gradient", 0, 11), ("gradient", 1, 14), ("gradient", 2, 17), ("gradient", 3, 19),
 )
 f32, bf16 = jnp.float32, jnp.bfloat16
 ANY = pl.BlockSpec(memory_space=pl.ANY)
@@ -40,6 +39,7 @@
 
 
 brief = pl.CostEstimate(flops=1, bytes_accessed=1, transcendentals=0)
+step_long = pl.CostEstimate(flops=1, bytes_accessed=60_000_000, transcendentals=0)
 
 
 def fold_rows(values):
@@ -73,39 +73,42 @@
 def other_factors(layer, cholesky_east, cholesky_north, cholesky_time, bounds, peers, held_back):
     nx = cholesky_east.shape[0]
     span, half = nx // layers, nx // 2
+    most = bounds[-1][0] * peers
 
     def kernel(layer_ref, east, north, time, _, *outs):
         def put(place, values):
             outs[2 * place][...], outs[2 * place + 1][...] = split(values)
 
         here = layer_ref[0]
-        put(0, permuted_rows(north[...], bounds, peers).T)
-        put(1, time[...])
+        turned = permuted_rows(north[...], bounds, peers).T
+        put(0, turned[:, :most])
+        put(1, turned[:, most:])
+        put(2, time[...])
 
         @pl.when(here == 1)
         def _():
-            put(2, field_scale * east[half:, :half])
+            put(3, field_scale * east[half:, :half])
 
         @pl.when(here != 1)
         def _():
             cross = (field_scale * east[half:, :half]).T
-            put(2, jnp.concatenate([cross[span:], cross[:span]], axis=0))
+            put(3, jnp.concatenate([cross[span:], cross[:span]], axis=0))
 
         for z in range(layers):
 
             @pl.when(here == z)
             def _(z=z):
                 own = field_scale * east[z * span : (z + 1) * span, z * span : (z + 1) * span]
-                put(3, own)
-                put(4, own.T)
+                put(4, own)
+                put(5, own.T)
                 if z % 2:
-                    put(5, field_scale * east[z * span : (z + 1) * span, (z - 1) * span : z * span])
+                    put(6, field_scale * east[z * span : (z + 1) * span, (z - 1) * span : z * span])
                 else:
-                    put(5, (field_scale * east[(z + 1) * span : (z + 2) * span, z * span : (z + 1) * span]).T)
+                    put(6, (field_scale * east[(z + 1) * span : (z + 2) * span, z * span : (z + 1) * span]).T)
 
     ny, nt = cholesky_north.shape[0], cholesky_time.shape[0]
-    sizes = (ny, nt, half, span, span, span)
-    shapes = [jax.ShapeDtypeStruct((size, size), bf16) for size in sizes for _ in range(2)]
+    sizes = [(ny, most), (ny, ny - most)] + [(size, size) for size in (nt, half, span, span, span)]
+    shapes = [jax.ShapeDtypeStruct(size, bf16) for size in sizes for _ in range(2)]
     outs = pl.pallas_call(
         kernel,
         out_shape=shapes,
@@ -224,7 +227,7 @@
     return pl.BlockSpec((peers, 1, *rest), lambda y: (0, start + y, 0, 0, 0))
 
 
-def cross_terms(layer, cross, crossed, own_field, own_residual, rows):
+def cross_terms(layer, cross, crossed, own_field, own_residual, rows, *held_back):
     operands = [layer, *cross, *crossed]
     specs = [SMEM, whole(cross[0].shape), whole(cross[1].shape)] + [rows_of(c, 0) for c in crossed]
     pieces = len(crossed)
@@ -232,6 +235,8 @@
         if pair is not None:
             operands.append(pair[0])
             specs.append(rows_of(*pair))
+    operands += held_back
+    specs += [ANY] * len(held_back)
     peers, _, _, planes, _ = crossed[0].shape
     parts = sum(c.shape[2] for c in crossed)
     span, nt = peers * planes, parts * lanes
@@ -373,14 +378,14 @@
         out_shape=shapes,
         input_output_aliases=aliases,
         compiler_params=params(),
-        cost_estimate=brief,
+        cost_estimate=step_long,
         name="cells",
     )(*operands)
     return dict(zip(out_names, outs))
 
 
-def finish(groups, whitened, north, time):
-    planes, ny, nt = whitened.shape
+def finish(groups, partial, north, time, sign):
+    planes, ny, nt = partial.shape
     step = 8
     flat = [g.reshape(-1, *g.shape[2:]) for g in groups]
     counts = [g.shape[0] for g in flat]
@@ -396,7 +401,7 @@
             values = jnp.concatenate(
                 [jnp.concatenate([line(ref, rows, h) for h in range(parts)], axis=1) for ref, rows in zip(refs[:-1], counts)], axis=0
             )
-            out[x] = product(north_pair, split(product(split(values), time_pair))) - w[x]
+            out[x] = product(north_pair, split(product(split(values), time_pair))) + sign * w[x]
             return carry
 
         lax.fori_loop(0, step, one, 0, unroll=2)
@@ -405,13 +410,15 @@
     return pl.pallas_call(
         kernel,
         grid=(planes // step,),
-        in_specs=[planes_block] + [whole(f.shape) for f in (*north, *time)] + [pl.BlockSpec((rows, parts, step, lanes), lambda i: (0, 0, i, 0)) for rows in counts],
+        in_specs=[planes_block]
+        + [whole(f.shape) for f in (*north, *time)]
+        + [pl.BlockSpec((rows, parts, step, lanes), lambda i: (0, 0, i, 0)) for rows in counts],
         out_specs=planes_block,
-        out_shape=jax.ShapeDtypeStruct(whitened.shape, f32),
+        out_shape=jax.ShapeDtypeStruct(partial.shape, f32),
         compiler_params=params(),
         cost_estimate=brief,
         name="finish",
-    )(whitened, *north, *time, *flat)
+    )(partial, *north, *time, *flat)
 
 
 def ranges_of(kind, rows, unit):
@@ -444,18 +451,18 @@
     factors = field_factors(cholesky_north, cholesky_time, spans["field"], peers, first)
     groups, squares = field(whitened, factors, spans["field"], peers)
     start = gate(groups[0], arrived["cells", 0])
-    tables = [first] + [pack(i, start) for i in range(1, len(spans["cells"]))]
-    north, time, cross, *blocks = other_factors(layer, cholesky_east, cholesky_north, cholesky_time, spans["gradient"], peers, start)
+    tables = [first, pack(1, start)]
+    north, north_last, time, cross, *blocks = other_factors(layer, cholesky_east, cholesky_north, cholesky_time, spans["gradient"], peers, start)
     arrived["field", 0] = gate(exchange(start), *tables[1:], cross[0])
 
-    def sum_over_slab(values):
+    def sums_over_slab(values):
         if devices & (devices - 1):
-            return lax.psum(values, "slab")
+            yield lax.psum(values, "slab")
         step = 1
-        while step < devices:
+        while step < devices and not devices & (devices - 1):
             values = values + lax.ppermute(values, "slab", [(q, q ^ step) for q in range(devices)])
+            yield values
             step *= 2
-        return values
 
     def part_of(kind, c):
         i = next(i for i, (low, high) in enumerate(spans[kind]) if low <= c * chunk < high)
@@ -465,73 +472,80 @@
         i, start = part_of("field", c)
         return arrived["field", i], start
 
-    def pieces_of(values):
-        half = max(1, nt // lanes // 2)
-        return [lax.slice_in_dim(values, h, min(h + half, nt // lanes), axis=2) for h in range(0, nt // lanes, half)]
-
     total = -0.5 * squares
     crossed, residuals, nears, fars = {}, {}, {}, {}
     buffers = {}
-
-    def do_cross(k):
+    latest = [arrived["field", 0]]
+
+    def do_cross(k, *held_back):
         own_field = field_chunk(k) if k < number else None
-        own_residual = (residuals[k - 2], 0) if k >= 2 else None
-        near, far = cross_terms(layer, cross, crossed[k], own_field, own_residual, chunk)
-        forward, backward = k < number, k >= 2
+        own_residual = (residuals[k - 3], 0) if k >= 3 else None
+        near, far = cross_terms(layer, cross, crossed[k - 1], own_field, own_residual, chunk, *held_back)
+        forward, backward = k < number, k >= 3
         nears[k + 1] = move(near, [(1, 2)] * forward + [(2, 1)] * backward)
         fars[k + 1] = move(far, [(1, 3)] * forward + [(2, 0)] * backward)
         return near
 
     def send(kind, i, held_back):
         values = {"field": groups, "cells": tables, "gradient": buffers}[kind][i]
-        arrived[kind, i] = exchange(gate(values, held_back) if held_back is not None else values)
-
-    for k in (0, 1):
-        array, start = field_chunk(k)
+        latest[0] = arrived[kind, i] = exchange(gate(values, *latest, *([] if held_back is None else [held_back])))
+
+    def start_field(k):
+        array, start = field_chunk(k + 1)
         values = lax.slice_in_dim(array, start, start + chunk, axis=1)
-        crossed[k] = [move(v, [(0, 1), (2, 3)]) for v in pieces_of(values)]
-        if k == 0:
-            send("field", 1, values)
-            done = do_cross(0)
-    done = do_cross(1)
+        crossed[k] = [move(values, [(0, 1), (2, 3)])]
+        return values
+
+    start_field(-1)
+    send("field", 1, start_field(0))
+    near = do_cross(0)
+    tables += [pack(i, near) for i in range(2, len(spans["cells"]))]
+    start_field(1)
+    done = do_cross(1, nears[1], *tables[2:])
     pending = list(transfers)
-    for k in range(1, number + 3):
-        c, g = k - 1, k - 3
-        held = [done] if k < number + 2 else [done, sums]
+    for k in range(1, number + 4):
+        c, g = k - 1, k - 4
         own_field = observed = next_field = old = gradient = None
-        early = residuals[min(k - 2, number - 1)] if k >= 2 else done
         while pending and pending[0][2] * number <= (k - 1) * 16:
             kind, i, _ = pending.pop(0)
             if i < len(spans[kind]):
-                send(kind, i, early)
+                send(kind, i, residuals[min(k - 2, number - 1)] if k >= 2 else done)
         if c < number:
             own_field = field_chunk(c)
             i, start = part_of("cells", c)
             observed = (arrived["cells", i], start)
-            if k + 1 < number:
-                next_field = field_chunk(k + 1)
+            if k + 2 < number:
+                next_field = field_chunk(k + 2)
         if g >= 0:
             old = residuals[g]
             h, start = part_of("gradient", g)
             low, high = spans["gradient"][h]
             gradient = (buffers.get(h), high - low, start)
-        outs = cells(layer, blocks, crossed[k - 1], nears[k], fars[k], total, own_field, observed, next_field, old, gradient, chunk, held)
+        held = [done] if k < number + 3 else []
+        if k == number + 1:
+            sum_steps = sums_over_slab(total)
+        if k > number:
+            held.append(next(sum_steps))
+        outs = cells(layer, blocks, crossed[k - 2], nears[k], fars[k], total, own_field, observed, next_field, old, gradient, chunk, held)
         if c < number:
             residuals[c], total = outs["residual"], outs["new_total"]
-            if c == number - 1:
-                sums = sum_over_slab(total)
         if g >= 0:
             buffers[h] = outs["gradient"]
         if c < number:
-            pairs = ([(0, 1), (2, 3)] if k + 1 < number else []) + [(1, 0), (3, 2)]
+            pairs = ([(0, 1), (2, 3)] if k + 2 < number else []) + [(1, 0), (3, 2)]
             crossed[k + 1] = [move(outs["send%d" % i], pairs) for i in range(len(crossed[0]))]
+        if k + 1 <= number + 2:
             done = do_cross(k + 1)
     for kind, i, _ in pending:
         if i < len(spans[kind]):
             send(kind, i, None)
+    for sums in sum_steps:
+        pass
     cell_count = planes * ny * nt * devices
     density = jnp.sum(sums) / cell_count
-    gradient = finish([arrived["gradient", h] for h in range(len(spans["gradient"]))], whitened, north, time)
+    *most, last = [arrived["gradient", h] for h in range(len(spans["gradient"]))]
+    gradient = finish(most, whitened, north, time, -1.0) if most else whitened
+    gradient = finish([last], gradient, north_last, time, 1.0 if most else -1.0)
     return gradient, jnp.reshape(density, (1,))
 
 

time: 815 us -> 718 us (0.88)
  waiting for transfers between devices: 334 us -> 264 us
  starting transfers between devices: 217 us -> 178 us
  Pallas kernels: 167 us -> 194 us
  local copies, waits for them, and re-layouts: 82.1 us -> 68.6 us
    ppermute x72 -> x57, waiting for transfers between devices: 289 us -> 240 us  [move(): lax.ppermute(values, 'slab', [(a * peers + q, b * peers + q) for a, b in...]
    ppermute x72 -> x57, starting transfers between devices: 153 us -> 124 us  [move(): lax.ppermute(values, 'slab', [(a * peers + q, b * peers + q) for a, b in...]
    ppermute x4, waiting for transfers between devices: 27.9 us -> 7.26 us  [sums_over_slab(): lax.ppermute(values, 'slab', [(q, q ^ step) for q in range(devices)])]
    pallas_call x1 -> x2, Pallas kernels: 17.9 us -> 34.3 us  [finish(): pl.pallas_call(kernel, grid=(planes // step,), in_specs=[planes_block] +...]
    unnamed x390 -> x278, local copies, waits for them, and re-layouts: 80.1 us -> 65.3 us
    all_to_all x14 -> x11, starting transfers between devices: 59.4 us -> 48.2 us  [exchange(): lax.all_to_all(values, 'slab', 0, 0, tiled=True, axis_index_groups=in_layer)]
    pallas_call x18 -> x19, Pallas kernels: 24.9 us -> 35.1 us  [cross_terms(): pl.pallas_call(kernel, grid=(rows,), in_specs=specs, out_specs=[rows_of(s...]
    pallas_call x6 -> x4, Pallas kernels: 20.5 us -> 22.6 us  [packed(): pl.pallas_call(kernel, grid=(peers, rows // band), in_specs=[source, sour...]
  transfers between devices with their start and end apart: 90 -> 72, of which waited for: 42 -> 39; matrix products, arithmetic and copies ran while one was open for 0% -> 0% of each run, Pallas kernels for 18% -> 23%
where the time goes in v3:
time: 718 us; the launch traced here: 710 us
  waiting for transfers between devices  264 us (37%)
  Pallas kernels  194 us (27%)
  starting transfers between devices  178 us (25%)
  local copies, waits for them, and re-layouts  68.6 us (10%)
    ppermute x57, waiting for transfers between devices, move(): lax.ppermute(values, 'slab', [(a * peers + q, b * peers + q) for a, b in...  240 us
    ppermute x57, starting transfers between devices, move(): lax.ppermute(values, 'slab', [(a * peers + q, b * peers + q) for a, b in...  124 us
    pallas_call x19, Pallas kernels, cells(): pl.pallas_call(kernel, grid=(rows,), in_specs=specs, out_specs=out_specs,...  83.8 us
    unnamed x278, local copies, waits for them, and re-layouts  65.3 us
    all_to_all x11, starting transfers between devices, exchange(): lax.all_to_all(values, 'slab', 0, 0, tiled=True, axis_index_groups=in_layer)  48.2 us
    pallas_call x19, Pallas kernels, cross_terms(): pl.pallas_call(kernel, grid=(rows,), in_specs=specs, out_specs=[rows_of(s...  35.1 us
    pallas_call x2, Pallas kernels, finish(): pl.pallas_call(kernel, grid=(planes // step,), in_specs=[planes_block] +...  34.3 us
    pallas_call x4, Pallas kernels, packed(): pl.pallas_call(kernel, grid=(peers, rows // band), in_specs=[source, sour...  22.6 us
  transfers between devices with their start and end apart: 72, of which 39 were waited for; matrix products, arithmetic and copies ran while one was open for 0% of the time, Pallas kernels for 23%

profile of v3, /device:TPU:18, one launch (start us, length us, event | category | flops | bytes accessed | tf_op | source)
XLA Modules:
  0.0 709.7 jit_solution(10290513141720213009)
XLA Ops:
  0.6 3.8 packed.4._
  4.4 3.7 all-to-all-start
  8.3 18.0 %field.1 = (f32[32,2,32,128]{3,2,1,0:T(8,128)S(1)}, f32[128,2,32,128]{3,2,1,0:T(8,128)}, f32[96,2,32,128]{3,2,1,0:T(8,128)S(1)}, f32[8,256]{1,0:T(8,128)S(1)}) custom-call(f32[32,256,256]{2,1,0:T(8,128)} %w.3, bf16[256,256]{1,0:T(8,128)(2,1)S(1)} %get-tuple-element.123.north_high, bf16[256,256]{1,0:T(8,128)(2,1)S(1)} %get-tuple-element.124.north_low, ...), custom_call_target="tpu_custom_call" | custom-call | flops 1 | bytes 1 | tf_op jit(solution)/shard_map/field/pallas_call | solution.py:154
  29.0 4.8 all-to-all-done.__1_.refs_10_
  40.0 4.9 packed.5.__1_.__0_
  56.3 5.0 all-to-all-start.2
  66.1 10.9 %collective-permute-done.rest_0_.refs_5_ = f32[4,4,2,32,128]{4,3,2,1,0:T(8,128)S(1)} collective-permute-done((f32[4,4,2,32,128]{4,3,2,1,0:T(8,128)S(1)}, f32[4,4,2,32,128]{4,3,2,1,0:T(8,128)S(1)}, u32[]{:S(2)}, u32[]{:S(2)}) %collective-permute-start) | collective-permute-done | bytes 524320 | tf_op jit(solution)/shard_map/ppermute | solution.py:445
  79.3 9.2 %packed.7.rest_4_.__0_ = f32[4,2,2,32,24,128]{5,4,3,2,1,0:T(8,128)} custom-call(s32[32,256,256]{2,1,0:T(8,128)} %c.7, s32[32,256,256]{2,1,0:T(8,128)} %e.7, f32[4,4,2,32,128]{4,3,2,1,0:T(8,128)S(1)} %get-tuple-element.136.rest_0_), custom_call_target="tpu_custom_call" | custom-call | flops 1 | bytes 1 | tf_op jit(solution)/shard_map/packed/pallas_call | solution.py:180
  88.5 4.8 packed.6.rest_3_.__0_
  98.1 11.4 %all-to-all-done.2.refs_12_.rest_1_.__1_.refs_9_ = f32[4,32,2,32,128]{4,3,2,1,0:T(8,128)} async-done(((f32[4,32,2,32,128]{4,3,2,1,0:T(8,128)}), f32[4,32,2,32,128]{4,3,2,1,0:T(8,128)}, u32[]{:S(2)}, u32[]{:S(2)}) %all-to-all-start.2) | async-done | bytes 4194336 | tf_op jit(solution)/shard_map/all_to_all | solution.py:442
  111.6 3.8 cells.19
  117.0 4.8 all-to-all-start.3
  128.6 10.1 %collective-permute-done.9.rest_0_.refs_5_ = f32[4,4,2,32,128]{4,3,2,1,0:T(8,128)S(1)} collective-permute-done((f32[4,4,2,32,128]{4,3,2,1,0:T(8,128)S(1)}, f32[4,4,2,32,128]{4,3,2,1,0:T(8,128)S(1)}, u32[]{:S(2)}, u32[]{:S(2)}) %collective-permute-start.9) | collective-permute-done | bytes 524320 | tf_op jit(solution)/shard_map/ppermute | solution.py:445
  142.7 18.1 %collective-permute-done.4.rest_0_.refs_5_ = f32[4,4,2,32,128]{4,3,2,1,0:T(8,128)S(1)} collective-permute-done((f32[4,4,2,32,128]{4,3,2,1,0:T(8,128)}, f32[4,4,2,32,128]{4,3,2,1,0:T(8,128)S(1)}, u32[]{:S(2)}, u32[]{:S(2)}) %collective-permute-start.4) | collective-permute-done | bytes 524320 | tf_op jit(solution)/shard_map/ppermute | solution.py:445
  164.6 3.9 cells.20
  175.0 3.9 cells.21
  180.5 5.0 all-to-all-start.4
  185.6 6.8 collective-permute-start.10
  195.7 9.4 %collective-permute-done.10.rest_0_.refs_5_ = f32[4,4,2,32,128]{4,3,2,1,0:T(8,128)S(1)} collective-permute-done((f32[4,4,2,32,128]{4,3,2,1,0:T(8,128)}, f32[4,4,2,32,128]{4,3,2,1,0:T(8,128)S(1)}, u32[]{:S(2)}, u32[]{:S(2)}) %collective-permute-start.10) | collective-permute-done | bytes 524320 | tf_op jit(solution)/shard_map/ppermute | solution.py:445
  212.2 5.8 collective-permute-done.6.refs_4_
  218.0 5.5 cells.22
  224.3 6.1 collective-permute-done.18.rest_0_.refs_5_
  234.1 5.6 collective-permute-done.17.refs_4_
  239.8 5.5 cells.23
  248.9 3.7 all-to-all-start.5
  252.7 3.7 collective-permute-start.13
  258.6 5.1 collective-permute-start.21
  263.7 5.6 collective-permute-done.13.rest_0_.refs_5_
  277.1 13.8 %collective-permute-done.19.rest_0_.refs_5_ = f32[4,4,2,32,128]{4,3,2,1,0:T(8,128)S(1)} collective-permute-done((f32[4,4,2,32,128]{4,3,2,1,0:T(8,128)}, f32[4,4,2,32,128]{4,3,2,1,0:T(8,128)S(1)}, u32[]{:S(2)}, u32[]{:S(2)}) %collective-permute-start.19) | collective-permute-done | bytes 524320 | tf_op jit(solution)/shard_map/ppermute | solution.py:445
  294.7 5.8 cells.24
  304.0 5.5 cells.25
  312.7 5.3 all-to-all-start.6
  325.5 9.3 %collective-permute-done.27.rest_0_.refs_5_ = f32[4,4,2,32,128]{4,3,2,1,0:T(8,128)S(1)} collective-permute-done((f32[4,4,2,32,128]{4,3,2,1,0:T(8,128)}, f32[4,4,2,32,128]{4,3,2,1,0:T(8,128)S(1)}, u32[]{:S(2)}, u32[]{:S(2)}) %collective-permute-start.27) | collective-permute-done | bytes 524320 | tf_op jit(solution)/shard_map/ppermute | solution.py:445
  341.2 6.4 collective-permute-done.26.refs_4_
  347.6 5.6 cells.26
  361.9 8.2 %collective-permute-done.30.refs_4_ = f32[4,4,2,32,128]{4,3,2,1,0:T(8,128)S(1)} collective-permute-done((f32[4,4,2,32,128]{4,3,2,1,0:T(8,128)S(1)}, f32[4,4,2,32,128]{4,3,2,1,0:T(8,128)S(1)}, u32[]{:S(2)}, u32[]{:S(2)}) %collective-permute-start.30) | collective-permute-done | bytes 524320 | tf_op jit(solution)/shard_map/ppermute | solution.py:445
  370.1 5.6 cells.27
  387.4 13.9 %collective-permute-done.33.rest_0_.refs_5_ = f32[4,4,2,32,128]{4,3,2,1,0:T(8,128)S(1)} collective-permute-done((f32[4,4,2,32,128]{4,3,2,1,0:T(8,128)S(1)}, f32[4,4,2,32,128]{4,3,2,1,0:T(8,128)S(1)}, u32[]{:S(2)}, u32[]{:S(2)}) %collective-permute-start.33) | collective-permute-done | bytes 524320 | tf_op jit(solution)/shard_map/ppermute | solution.py:445
  402.7 5.7 cells.28
  417.3 4.8 cells.29
  425.0 5.1 all-to-all-start.7
  437.5 9.3 %collective-permute-done.39.rest_0_.refs_5_ = f32[4,4,2,32,128]{4,3,2,1,0:T(8,128)S(1)} collective-permute-done((f32[4,4,2,32,128]{4,3,2,1,0:T(8,128)}, f32[4,4,2,32,128]{4,3,2,1,0:T(8,128)S(1)}, u32[]{:S(2)}, u32[]{:S(2)}) %collective-permute-start.39) | collective-permute-done | bytes 524320 | tf_op jit(solution)/shard_map/ppermute | solution.py:445
  450.7 8.4 %collective-permute-done.38.refs_4_ = f32[4,4,2,32,128]{4,3,2,1,0:T(8,128)S(1)} collective-permute-done((f32[4,4,2,32,128]{4,3,2,1,0:T(8,128)}, f32[4,4,2,32,128]{4,3,2,1,0:T(8,128)S(1)}, u32[]{:S(2)}, u32[]{:S(2)}) %collective-permute-start.38) | collective-permute-done | bytes 524320 | tf_op jit(solution)/shard_map/ppermute | solution.py:445
  459.1 5.0 cells.30
  484.5 9.1 %collective-permute-done.42.refs_4_ = f32[4,4,2,32,128]{4,3,2,1,0:T(8,128)S(1)} collective-permute-done((f32[4,4,2,32,128]{4,3,2,1,0:T(8,128)S(1)}, f32[4,4,2,32,128]{4,3,2,1,0:T(8,128)S(1)}, u32[]{:S(2)}, u32[]{:S(2)}) %collective-permute-start.42) | collective-permute-done | bytes 524320 | tf_op jit(solution)/shard_map/ppermute | solution.py:445
  493.7 4.9 cells.31
  500.2 6.7 collective-permute-done.35.refs_3_
  507.0 7.0 collective-permute-done.36.refs_4_
  514.0 4.7 cells.32
  521.7 4.7 all-to-all-start.8
  535.2 7.8 %collective-permute-done.48.rest_0_.refs_5_ = f32[4,4,2,32,128]{4,3,2,1,0:T(8,128)S(1)} collective-permute-done((f32[4,4,2,32,128]{4,3,2,1,0:T(8,128)}, f32[4,4,2,32,128]{4,3,2,1,0:T(8,128)S(1)}, u32[]{:S(2)}, u32[]{:S(2)}) %collective-permute-start.48) | collective-permute-done | bytes 524320 | tf_op jit(solution)/shard_map/ppermute | solution.py:445
  548.9 7.3 %collective-permute-done.47.refs_4_ = f32[4,4,2,32,128]{4,3,2,1,0:T(8,128)S(1)} collective-permute-done((f32[4,4,2,32,128]{4,3,2,1,0:T(8,128)}, f32[4,4,2,32,128]{4,3,2,1,0:T(8,128)S(1)}, u32[]{:S(2)}, u32[]{:S(2)}) %collective-permute-start.47) | collective-permute-done | bytes 524320 | tf_op jit(solution)/shard_map/ppermute | solution.py:445
  556.2 4.8 cells.33
  563.7 5.4 collective-permute-start.44
  570.4 8.2 %collective-permute-done.51.refs_4_ = f32[4,4,2,32,128]{4,3,2,1,0:T(8,128)S(1)} collective-permute-done((f32[4,4,2,32,128]{4,3,2,1,0:T(8,128)S(1)}, f32[4,4,2,32,128]{4,3,2,1,0:T(8,128)S(1)}, u32[]{:S(2)}, u32[]{:S(2)}) %collective-permute-start.51) | collective-permute-done | bytes 524320 | tf_op jit(solution)/shard_map/ppermute | solution.py:445
  578.6 4.7 cells.34
  589.9 10.4 %collective-permute-done.45.refs_4_ = f32[4,4,2,32,128]{4,3,2,1,0:T(8,128)S(1)} collective-permute-done((f32[4,4,2,32,128]{4,3,2,1,0:T(8,128)S(1)}, f32[4,4,2,32,128]{4,3,2,1,0:T(8,128)S(1)}, u32[]{:S(2)}, u32[]{:S(2)}) %collective-permute-start.45) | collective-permute-done | bytes 524320 | tf_op jit(solution)/shard_map/ppermute | solution.py:445
  602.7 3.7 all-to-all-start.9
  607.7 6.5 collective-permute-start.58
  615.6 7.2 %collective-permute-done.53.rest_0_.refs_5_ = f32[4,4,2,32,128]{4,3,2,1,0:T(8,128)S(1)} collective-permute-done((f32[4,4,2,32,128]{4,3,2,1,0:T(8,128)}, f32[4,4,2,32,128]{4,3,2,1,0:T(8,128)S(1)}, u32[]{:S(2)}, u32[]{:S(2)}) %collective-permute-start.53) | collective-permute-done | bytes 524320 | tf_op jit(solution)/shard_map/ppermute | solution.py:445
  641.2 7.9 %collective-permute-done.54.refs_3_ = f32[4,4,2,32,128]{4,3,2,1,0:T(8,128)S(1)} collective-permute-done((f32[4,4,2,32,128]{4,3,2,1,0:T(8,128)S(1)}, f32[4,4,2,32,128]{4,3,2,1,0:T(8,128)S(1)}, u32[]{:S(2)}, u32[]{:S(2)}) %collective-permute-start.54) | collective-permute-done | bytes 524320 | tf_op jit(solution)/shard_map/ppermute | solution.py:445
  649.0 10.5 %collective-permute-done.55.refs_4_ = f32[4,4,2,32,128]{4,3,2,1,0:T(8,128)S(1)} collective-permute-done((f32[4,4,2,32,128]{4,3,2,1,0:T(8,128)S(1)}, f32[4,4,2,32,128]{4,3,2,1,0:T(8,128)S(1)}, u32[]{:S(2)}, u32[]{:S(2)}) %collective-permute-start.55) | collective-permute-done | bytes 524320 | tf_op jit(solution)/shard_map/ppermute | solution.py:445
  674.3 17.2 %finish.2.w = f32[32,256,256]{2,1,0:T(8,128)} custom-call(f32[32,256,256]{2,1,0:T(8,128)} %w.3, bf16[256,224]{1,0:T(8,128)(2,1)S(1)} %copy-done.108, bf16[256,224]{1,0:T(8,128)(2,1)S(1)} %copy-done.110, bf16[256,256]{1,0:T(8,128)(2,1)S(1)} %copy-done.83, bf16[256,256]{1,0:T(8,128)(2,1)S(1)} %copy-done.85, f32[112,2,32,128]{3,2,1,0:T(8,128)} %bitcast.4.refs_0_, ...), custom_call_target="tpu_custom_call" | custom-call | flops 1 | bytes 1 | tf_op jit(solution)/shard_map/finish/pallas_call | solution.py:410
  691.6 17.1 %finish.3 = f32[32,256,256]{2,1,0:T(8,128)} custom-call(f32[32,256,256]{2,1,0:T(8,128)} %finish.2.w, bf16[256,32]{1,0:T(8,128)(2,1)S(1)} %copy-done.112, bf16[256,32]{1,0:T(8,128)(2,1)S(1)} %copy-done.114, bf16[256,256]{1,0:T(8,128)(2,1)S(1)} %copy-done.83, bf16[256,256]{1,0:T(8,128)(2,1)S(1)} %copy-done.85, f32[32,2,32,128]{3,2,1,0:T(8,128)S(1)} %bitcast.12), custom_call_target="tpu_custom_call" | custom-call | flops 1 | bytes 1 | tf_op jit(solution)/shard_map/finish/pallas_call | solution.py:410
  (423 shorter events, 242.9 us)
Async XLA Ops:
  4.4 29.4 %all-to-all-start = ((f32[4,2,2,32,8,128]{5,4,3,2,1,0:T(8,128)}), f32[4,2,2,32,8,128]{5,4,3,2,1,0:T(8,128)S(1)}, u32[]{:S(2)}, u32[]{:S(2)}) async-start(f32[4,2,2,32,8,128]{5,4,3,2,1,0:T(8,128)} %packed.4._), calls=%async_computation | async-start | bytes 4194304 | tf_op jit(solution)/shard_map/all_to_all | solution.py:442
  35.2 18.0 %all-to-all-start.1 = ((f32[4,8,2,32,128]{4,3,2,1,0:T(8,128)}), f32[4,8,2,32,128]{4,3,2,1,0:T(8,128)S(1)}, u32[]{:S(2)}, u32[]{:S(2)}) async-start(f32[4,8,2,32,128]{4,3,2,1,0:T(8,128)} %gate.11._.rest_0_), calls=%async_computation.1 | async-start | bytes 2097152 | tf_op jit(solution)/shard_map/all_to_all | solution.py:442
  56.3 53.2 %all-to-all-start.2 = ((f32[4,32,2,32,128]{4,3,2,1,0:T(8,128)}), f32[4,32,2,32,128]{4,3,2,1,0:T(8,128)}, u32[]{:S(2)}, u32[]{:S(2)}) async-start(f32[4,32,2,32,128]{4,3,2,1,0:T(8,128)} %gate.13), calls=%async_computation.2 | async-start | bytes 8388608 | tf_op jit(solution)/shard_map/all_to_all | solution.py:442
  64.8 30.6 %collective-permute-start.3 = (f32[4,4,2,32,128]{4,3,2,1,0:T(8,128)}, f32[4,4,2,32,128]{4,3,2,1,0:T(8,128)S(1)}, u32[]{:S(2)}, u32[]{:S(2)}) collective-permute-start(f32[4,4,2,32,128]{4,3,2,1,0:T(8,128)} %get-tuple-element.244.__2_), channel_id=1, source_target_pairs={{0,4},{1,5},{2,6},{3,7},{8,12},{9,13},{10,14},{11,15},{16,20},{17,... | collective-permute-start | bytes 1572872 | tf_op jit(solution)/shard_map/ppermute | solution.py:445
  77.3 18.1 %collective-permute-start.1 = (f32[4,4,2,32,128]{4,3,2,1,0:T(8,128)S(1)}, f32[4,4,2,32,128]{4,3,2,1,0:T(8,128)S(1)}, u32[]{:S(2)}, u32[]{:S(2)}) collective-permute-start(f32[4,4,2,32,128]{4,3,2,1,0:T(8,128)S(1)} %get-tuple-element.136.rest_0_), channel_id=1, source_target_pairs={{4,8},{5,9},{6,10},{7,11},{20,24},{21,25},{22,26},{23,27}} | collective-permute-start | bytes 1572872 | tf_op jit(solution)/shard_map/ppermute | solution.py:445
  78.6 18.7 %collective-permute-start.2 = (f32[4,4,2,32,128]{4,3,2,1,0:T(8,128)S(1)}, f32[4,4,2,32,128]{4,3,2,1,0:T(8,128)S(1)}, u32[]{:S(2)}, u32[]{:S(2)}) collective-permute-start(f32[4,4,2,32,128]{4,3,2,1,0:T(8,128)S(1)} %get-tuple-element.137), channel_id=1, source_target_pairs={{4,12},{5,13},{6,14},{7,15},{20,28},{21,29},{22,30},{23,31}} | collective-permute-start | bytes 1572872 | tf_op jit(solution)/shard_map/ppermute | solution.py:445
  117.0 54.8 %all-to-all-start.3 = ((f32[4,2,2,32,16,128]{5,4,3,2,1,0:T(8,128)}), f32[4,2,2,32,16,128]{5,4,3,2,1,0:T(8,128)}, u32[]{:S(2)}, u32[]{:S(2)}) async-start(f32[4,2,2,32,16,128]{5,4,3,2,1,0:T(8,128)} %gate.14), calls=%async_computation.3 | async-start | bytes 8388608 | tf_op jit(solution)/shard_map/all_to_all | solution.py:442
  126.5 38.1 %collective-permute-start.7 = (f32[4,4,2,32,128]{4,3,2,1,0:T(8,128)}, f32[4,4,2,32,128]{4,3,2,1,0:T(8,128)S(1)}, u32[]{:S(2)}, u32[]{:S(2)}) collective-permute-start(f32[4,4,2,32,128]{4,3,2,1,0:T(8,128)} %copy-done.94), channel_id=1, source_target_pairs={{4,8},{5,9},{6,10},{7,11},{20,24},{21,25},{22,26},{23,27}} | collective-permute-start | bytes 1572872 | tf_op jit(solution)/shard_map/ppermute | solution.py:445
  127.8 33.0 %collective-permute-start.4 = (f32[4,4,2,32,128]{4,3,2,1,0:T(8,128)}, f32[4,4,2,32,128]{4,3,2,1,0:T(8,128)S(1)}, u32[]{:S(2)}, u32[]{:S(2)}) collective-permute-start(f32[4,4,2,32,128]{4,3,2,1,0:T(8,128)} %copy-done.137), channel_id=1, source_target_pairs={{0,4},{1,5},{2,6},{3,7},{8,12},{9,13},{10,14},{11,15},{4,0},{5,1},... | collective-permute-start | bytes 1572872 | tf_op jit(solution)/shard_map/ppermute | solution.py:445
  127.9 36.7 %collective-permute-start.8 = (f32[4,4,2,32,128]{4,3,2,1,0:T(8,128)}, f32[4,4,2,32,128]{4,3,2,1,0:T(8,128)S(1)}, u32[]{:S(2)}, u32[]{:S(2)}) collective-permute-start(f32[4,4,2,32,128]{4,3,2,1,0:T(8,128)} %copy-done.126), channel_id=1, source_target_pairs={{4,12},{5,13},{6,14},{7,15},{20,28},{21,29},{22,30},{23,31}} | collective-permute-start | bytes 1572872 | tf_op jit(solution)/shard_map/ppermute | solution.py:445
  140.7 29.5 %collective-permute-start.11 = (f32[4,4,2,32,128]{4,3,2,1,0:T(8,128)S(1)}, f32[4,4,2,32,128]{4,3,2,1,0:T(8,128)S(1)}, u32[]{:S(2)}, u32[]{:S(2)}) collective-permute-start(f32[4,4,2,32,128]{4,3,2,1,0:T(8,128)S(1)} %get-tuple-element.148.refs_6_), channel_id=1, source_target_pairs={{4,8},{5,9},{6,10},{7,11},{20,24},{21,25},{22,26},{23,27}} | collective-permute-start | bytes 1572872 | tf_op jit(solution)/shard_map/ppermute | solution.py:445
  142.0 29.0 %collective-permute-start.12 = (f32[4,4,2,32,128]{4,3,2,1,0:T(8,128)S(1)}, f32[4,4,2,32,128]{4,3,2,1,0:T(8,128)S(1)}, u32[]{:S(2)}, u32[]{:S(2)}) collective-permute-start(f32[4,4,2,32,128]{4,3,2,1,0:T(8,128)S(1)} %get-tuple-element.153), channel_id=1, source_target_pairs={{4,12},{5,13},{6,14},{7,15},{20,28},{21,29},{22,30},{23,31}} | collective-permute-start | bytes 1572872 | tf_op jit(solution)/shard_map/ppermute | solution.py:445
  180.5 68.4 %all-to-all-start.4 = ((f32[4,2,2,32,16,128]{5,4,3,2,1,0:T(8,128)}), f32[4,2,2,32,16,128]{5,4,3,2,1,0:T(8,128)}, u32[]{:S(2)}, u32[]{:S(2)}) async-start(f32[4,2,2,32,16,128]{5,4,3,2,1,0:T(8,128)} %gate.15), calls=%async_computation.4 | async-start | bytes 8388608 | tf_op jit(solution)/shard_map/all_to_all | solution.py:442
  185.6 19.5 %collective-permute-start.10 = (f32[4,4,2,32,128]{4,3,2,1,0:T(8,128)}, f32[4,4,2,32,128]{4,3,2,1,0:T(8,128)S(1)}, u32[]{:S(2)}, u32[]{:S(2)}) collective-permute-start(f32[4,4,2,32,128]{4,3,2,1,0:T(8,128)} %copy-done.136), channel_id=1, source_target_pairs={{0,4},{1,5},{2,6},{3,7},{8,12},{9,13},{10,14},{11,15},{4,0},{5,1},... | collective-permute-start | bytes 1572872 | tf_op jit(solution)/shard_map/ppermute | solution.py:445
  192.4 19.7 %collective-permute-start.5 = (f32[4,4,2,32,128]{4,3,2,1,0:T(8,128)S(1)}, f32[4,4,2,32,128]{4,3,2,1,0:T(8,128)S(1)}, u32[]{:S(2)}, u32[]{:S(2)}) collective-permute-start(f32[4,4,2,32,128]{4,3,2,1,0:T(8,128)S(1)} %copy-done.91), channel_id=1, source_target_pairs={{4,8},{5,9},{6,10},{7,11},{8,4},{9,5},{10,6},{11,7},{20,24},{21,25... | collective-permute-start | bytes 1572872 | tf_op jit(solution)/shard_map/ppermute | solution.py:445
  194.3 23.6 %collective-permute-start.6 = (f32[4,4,2,32,128]{4,3,2,1,0:T(8,128)}, f32[4,4,2,32,128]{4,3,2,1,0:T(8,128)S(1)}, u32[]{:S(2)}, u32[]{:S(2)}) collective-permute-start(f32[4,4,2,32,128]{4,3,2,1,0:T(8,128)} %copy-done.120), channel_id=1, source_target_pairs={{4,12},{5,13},{6,14},{7,15},{8,0},{9,1},{10,2},{11,3},{20,28},{21,... | collective-permute-start | bytes 1572872 | tf_op jit(solution)/shard_map/ppermute | solution.py:445
  207.9 22.4 %collective-permute-start.18 = (f32[4,4,2,32,128]{4,3,2,1,0:T(8,128)S(1)}, f32[4,4,2,32,128]{4,3,2,1,0:T(8,128)S(1)}, u32[]{:S(2)}, u32[]{:S(2)}) collective-permute-start(f32[4,4,2,32,128]{4,3,2,1,0:T(8,128)S(1)} %copy-done.129), channel_id=1, source_target_pairs={{0,4},{1,5},{2,6},{3,7},{8,12},{9,13},{10,14},{11,15},{4,0},{5,1},... | collective-permute-start | bytes 1572872 | tf_op jit(solution)/shard_map/ppermute | solution.py:445
  208.9 25.2 %collective-permute-start.16 = (f32[4,4,2,32,128]{4,3,2,1,0:T(8,128)S(1)}, f32[4,4,2,32,128]{4,3,2,1,0:T(8,128)S(1)}, u32[]{:S(2)}, u32[]{:S(2)}) collective-permute-start(f32[4,4,2,32,128]{4,3,2,1,0:T(8,128)S(1)} %get-tuple-element.152.refs_6_), channel_id=1, source_target_pairs={{4,8},{5,9},{6,10},{7,11},{8,4},{9,5},{10,6},{11,7},{20,24},{21,25... | collective-permute-start | bytes 1572872 | tf_op jit(solution)/shard_map/ppermute | solution.py:445
  210.8 28.9 %collective-permute-start.17 = (f32[4,4,2,32,128]{4,3,2,1,0:T(8,128)S(1)}, f32[4,4,2,32,128]{4,3,2,1,0:T(8,128)S(1)}, u32[]{:S(2)}, u32[]{:S(2)}) collective-permute-start(f32[4,4,2,32,128]{4,3,2,1,0:T(8,128)S(1)} %get-tuple-element.162), channel_id=1, source_target_pairs={{4,12},{5,13},{6,14},{7,15},{8,0},{9,1},{10,2},{11,3},{20,28},{21,... | collective-permute-start | bytes 1572872 | tf_op jit(solution)/shard_map/ppermute | solution.py:445
  248.9 62.2 %all-to-all-start.5 = ((f32[4,24,2,32,128]{4,3,2,1,0:T(8,128)}), f32[4,24,2,32,128]{4,3,2,1,0:T(8,128)S(1)}, u32[]{:S(2)}, u32[]{:S(2)}) async-start(f32[4,24,2,32,128]{4,3,2,1,0:T(8,128)} %gate.16), calls=%async_computation.5 | async-start | bytes 6291456 | tf_op jit(solution)/shard_map/all_to_all | solution.py:442
  252.7 16.7 %collective-permute-start.13 = (f32[4,4,2,32,128]{4,3,2,1,0:T(8,128)}, f32[4,4,2,32,128]{4,3,2,1,0:T(8,128)S(1)}, u32[]{:S(2)}, u32[]{:S(2)}) collective-permute-start(f32[4,4,2,32,128]{4,3,2,1,0:T(8,128)} %copy-done.130), channel_id=1, source_target_pairs={{0,4},{1,5},{2,6},{3,7},{8,12},{9,13},{10,14},{11,15},{4,0},{5,1},... | collective-permute-start | bytes 1572872 | tf_op jit(solution)/shard_map/ppermute | solution.py:445
  256.3 38.3 %collective-permute-start.20 = (f32[4,4,2,32,128]{4,3,2,1,0:T(8,128)}, f32[4,4,2,32,128]{4,3,2,1,0:T(8,128)S(1)}, u32[]{:S(2)}, u32[]{:S(2)}) collective-permute-start(f32[4,4,2,32,128]{4,3,2,1,0:T(8,128)} %copy-done.93), channel_id=1, source_target_pairs={{4,8},{5,9},{6,10},{7,11},{8,4},{9,5},{10,6},{11,7},{20,24},{21,25... | collective-permute-start | bytes 1572872 | tf_op jit(solution)/shard_map/ppermute | solution.py:445
  258.6 32.3 %collective-permute-start.19 = (f32[4,4,2,32,128]{4,3,2,1,0:T(8,128)}, f32[4,4,2,32,128]{4,3,2,1,0:T(8,128)S(1)}, u32[]{:S(2)}, u32[]{:S(2)}) collective-permute-start(f32[4,4,2,32,128]{4,3,2,1,0:T(8,128)} %copy-done.133), channel_id=1, source_target_pairs={{0,4},{1,5},{2,6},{3,7},{8,12},{9,13},{10,14},{11,15},{4,0},{5,1},... | collective-permute-start | bytes 1572872 | tf_op jit(solution)/shard_map/ppermute | solution.py:445
  258.6 36.0 %collective-permute-start.21 = (f32[4,4,2,32,128]{4,3,2,1,0:T(8,128)}, f32[4,4,2,32,128]{4,3,2,1,0:T(8,128)S(1)}, u32[]{:S(2)}, u32[]{:S(2)}) collective-permute-start(f32[4,4,2,32,128]{4,3,2,1,0:T(8,128)} %copy-done.122), channel_id=1, source_target_pairs={{4,12},{5,13},{6,14},{7,15},{8,0},{9,1},{10,2},{11,3},{20,28},{21,... | collective-permute-start | bytes 1572872 | tf_op jit(solution)/shard_map/ppermute | solution.py:445
  273.2 28.1 %collective-permute-start.14 = (f32[4,4,2,32,128]{4,3,2,1,0:T(8,128)S(1)}, f32[4,4,2,32,128]{4,3,2,1,0:T(8,128)S(1)}, u32[]{:S(2)}, u32[]{:S(2)}) collective-permute-start(f32[4,4,2,32,128]{4,3,2,1,0:T(8,128)S(1)} %get-tuple-element.160.refs_6_), channel_id=1, source_target_pairs={{4,8},{5,9},{6,10},{7,11},{8,4},{9,5},{10,6},{11,7},{20,24},{21,25... | collective-permute-start | bytes 1572872 | tf_op jit(solution)/shard_map/ppermute | solution.py:445
  275.6 28.4 %collective-permute-start.15 = (f32[4,4,2,32,128]{4,3,2,1,0:T(8,128)S(1)}, f32[4,4,2,32,128]{4,3,2,1,0:T(8,128)S(1)}, u32[]{:S(2)}, u32[]{:S(2)}) collective-permute-start(f32[4,4,2,32,128]{4,3,2,1,0:T(8,128)S(1)} %get-tuple-element.161), channel_id=1, source_target_pairs={{4,12},{5,13},{6,14},{7,15},{8,0},{9,1},{10,2},{11,3},{20,28},{21,... | collective-permute-start | bytes 1572872 | tf_op jit(solution)/shard_map/ppermute | solution.py:445
  312.7 102.4 %all-to-all-start.6 = ((f32[4,2,2,32,24,128]{5,4,3,2,1,0:T(8,128)}), f32[4,2,2,32,24,128]{5,4,3,2,1,0:T(8,128)}, u32[]{:S(2)}, u32[]{:S(2)}) async-start(f32[4,2,2,32,24,128]{5,4,3,2,1,0:T(8,128)} %gate.17), calls=%async_computation.6 | async-start | bytes 12582912 | tf_op jit(solution)/shard_map/all_to_all | solution.py:442
  318.1 16.7 %collective-permute-start.27 = (f32[4,4,2,32,128]{4,3,2,1,0:T(8,128)}, f32[4,4,2,32,128]{4,3,2,1,0:T(8,128)S(1)}, u32[]{:S(2)}, u32[]{:S(2)}) collective-permute-start(f32[4,4,2,32,128]{4,3,2,1,0:T(8,128)} %get-tuple-element.181), channel_id=1, source_target_pairs={{0,4},{1,5},{2,6},{3,7},{8,12},{9,13},{10,14},{11,15},{4,0},{5,1},... | collective-permute-start | bytes 1572872 | tf_op jit(solution)/shard_map/ppermute | solution.py:445
  321.8 19.4 %collective-permute-start.25 = (f32[4,4,2,32,128]{4,3,2,1,0:T(8,128)S(1)}, f32[4,4,2,32,128]{4,3,2,1,0:T(8,128)S(1)}, u32[]{:S(2)}, u32[]{:S(2)}) collective-permute-start(f32[4,4,2,32,128]{4,3,2,1,0:T(8,128)S(1)} %copy-done.87), channel_id=1, source_target_pairs={{4,8},{5,9},{6,10},{7,11},{8,4},{9,5},{10,6},{11,7},{20,24},{21,25... | collective-permute-start | bytes 1572872 | tf_op jit(solution)/shard_map/ppermute | solution.py:445
  324.1 23.5 %collective-permute-start.26 = (f32[4,4,2,32,128]{4,3,2,1,0:T(8,128)S(1)}, f32[4,4,2,32,128]{4,3,2,1,0:T(8,128)S(1)}, u32[]{:S(2)}, u32[]{:S(2)}) collective-permute-start(f32[4,4,2,32,128]{4,3,2,1,0:T(8,128)S(1)} %copy-done.116), channel_id=1, source_target_pairs={{4,12},{5,13},{6,14},{7,15},{8,0},{9,1},{10,2},{11,3},{20,28},{21,... | collective-permute-start | bytes 1572872 | tf_op jit(solution)/shard_map/ppermute | solution.py:445
  325.4 31.4 %collective-permute-start.22 = (f32[4,4,2,32,128]{4,3,2,1,0:T(8,128)}, f32[4,4,2,32,128]{4,3,2,1,0:T(8,128)S(1)}, u32[]{:S(2)}, u32[]{:S(2)}) collective-permute-start(f32[4,4,2,32,128]{4,3,2,1,0:T(8,128)} %copy-done.123), channel_id=1, source_target_pairs={{0,4},{1,5},{2,6},{3,7},{8,12},{9,13},{10,14},{11,15},{4,0},{5,1},... | collective-permute-start | bytes 1572872 | tf_op jit(solution)/shard_map/ppermute | solution.py:445
  337.6 24.3 %collective-permute-start.29 = (f32[4,4,2,32,128]{4,3,2,1,0:T(8,128)S(1)}, f32[4,4,2,32,128]{4,3,2,1,0:T(8,128)S(1)}, u32[]{:S(2)}, u32[]{:S(2)}) collective-permute-start(f32[4,4,2,32,128]{4,3,2,1,0:T(8,128)S(1)} %get-tuple-element.183.refs_6_), channel_id=1, source_target_pairs={{4,8},{5,9},{6,10},{7,11},{8,4},{9,5},{10,6},{11,7},{20,24},{21,25... | collective-permute-start | bytes 1572872 | tf_op jit(solution)/shard_map/ppermute | solution.py:445
  339.9 30.2 %collective-permute-start.30 = (f32[4,4,2,32,128]{4,3,2,1,0:T(8,128)S(1)}, f32[4,4,2,32,128]{4,3,2,1,0:T(8,128)S(1)}, u32[]{:S(2)}, u32[]{:S(2)}) collective-permute-start(f32[4,4,2,32,128]{4,3,2,1,0:T(8,128)S(1)} %get-tuple-element.190), channel_id=1, source_target_pairs={{4,12},{5,13},{6,14},{7,15},{8,0},{9,1},{10,2},{11,3},{20,28},{21,... | collective-permute-start | bytes 1572872 | tf_op jit(solution)/shard_map/ppermute | solution.py:445
  353.2 27.9 %collective-permute-start.28 = (f32[4,4,2,32,128]{4,3,2,1,0:T(8,128)S(1)}, f32[4,4,2,32,128]{4,3,2,1,0:T(8,128)S(1)}, u32[]{:S(2)}, u32[]{:S(2)}) collective-permute-start(f32[4,4,2,32,128]{4,3,2,1,0:T(8,128)S(1)} %get-tuple-element.187), channel_id=1, source_target_pairs={{0,4},{1,5},{2,6},{3,7},{8,12},{9,13},{10,14},{11,15},{4,0},{5,1},... | collective-permute-start | bytes 1572872 | tf_op jit(solution)/shard_map/ppermute | solution.py:445
  359.7 43.0 %collective-permute-start.23 = (f32[4,4,2,32,128]{4,3,2,1,0:T(8,128)S(1)}, f32[4,4,2,32,128]{4,3,2,1,0:T(8,128)S(1)}, u32[]{:S(2)}, u32[]{:S(2)}) collective-permute-start(f32[4,4,2,32,128]{4,3,2,1,0:T(8,128)S(1)} %get-tuple-element.178.refs_6_), channel_id=1, source_target_pairs={{4,8},{5,9},{6,10},{7,11},{8,4},{9,5},{10,6},{11,7},{20,24},{21,25... | collective-permute-start | bytes 1572872 | tf_op jit(solution)/shard_map/ppermute | solution.py:445
  375.7 25.5 %collective-permute-start.33 = (f32[4,4,2,32,128]{4,3,2,1,0:T(8,128)S(1)}, f32[4,4,2,32,128]{4,3,2,1,0:T(8,128)S(1)}, u32[]{:S(2)}, u32[]{:S(2)}) collective-permute-start(f32[4,4,2,32,128]{4,3,2,1,0:T(8,128)S(1)} %get-tuple-element.197), channel_id=1, source_target_pairs={{0,4},{1,5},{2,6},{3,7},{8,12},{9,13},{10,14},{11,15},{4,0},{5,1},... | collective-permute-start | bytes 1572872 | tf_op jit(solution)/shard_map/ppermute | solution.py:445
  379.3 23.4 %collective-permute-start.24 = (f32[4,4,2,32,128]{4,3,2,1,0:T(8,128)S(1)}, f32[4,4,2,32,128]{4,3,2,1,0:T(8,128)S(1)}, u32[]{:S(2)}, u32[]{:S(2)}) collective-permute-start(f32[4,4,2,32,128]{4,3,2,1,0:T(8,128)S(1)} %get-tuple-element.179), channel_id=1, source_target_pairs={{4,12},{5,13},{6,14},{7,15},{8,0},{9,1},{10,2},{11,3},{20,28},{21,... | collective-permute-start | bytes 1572872 | tf_op jit(solution)/shard_map/ppermute | solution.py:445
  382.5 27.7 %collective-permute-start.31 = (f32[4,4,2,32,128]{4,3,2,1,0:T(8,128)S(1)}, f32[4,4,2,32,128]{4,3,2,1,0:T(8,128)S(1)}, u32[]{:S(2)}, u32[]{:S(2)}) collective-permute-start(f32[4,4,2,32,128]{4,3,2,1,0:T(8,128)S(1)} %get-tuple-element.189.refs_6_), channel_id=1, source_target_pairs={{4,8},{5,9},{6,10},{7,11},{8,4},{9,5},{10,6},{11,7},{20,24},{21,25... | collective-permute-start | bytes 1572872 | tf_op jit(solution)/shard_map/ppermute | solution.py:445
  386.0 28.3 %collective-permute-start.32 = (f32[4,4,2,32,128]{4,3,2,1,0:T(8,128)S(1)}, f32[4,4,2,32,128]{4,3,2,1,0:T(8,128)S(1)}, u32[]{:S(2)}, u32[]{:S(2)}) collective-permute-start(f32[4,4,2,32,128]{4,3,2,1,0:T(8,128)S(1)} %get-tuple-element.196), channel_id=1, source_target_pairs={{4,12},{5,13},{6,14},{7,15},{8,0},{9,1},{10,2},{11,3},{20,28},{21,... | collective-permute-start | bytes 1572872 | tf_op jit(solution)/shard_map/ppermute | solution.py:445
  425.0 96.6 %all-to-all-start.7 = ((f32[4,28,2,32,128]{4,3,2,1,0:T(8,128)}), f32[4,28,2,32,128]{4,3,2,1,0:T(8,128)}, u32[]{:S(2)}, u32[]{:S(2)}) async-start(f32[4,28,2,32,128]{4,3,2,1,0:T(8,128)} %gate.18), calls=%async_computation.7 | async-start | bytes 7340032 | tf_op jit(solution)/shard_map/all_to_all | solution.py:442
  430.1 16.6 %collective-permute-start.39 = (f32[4,4,2,32,128]{4,3,2,1,0:T(8,128)}, f32[4,4,2,32,128]{4,3,2,1,0:T(8,128)S(1)}, u32[]{:S(2)}, u32[]{:S(2)}) collective-permute-start(f32[4,4,2,32,128]{4,3,2,1,0:T(8,128)} %copy-done.134), channel_id=1, source_target_pairs={{0,4},{1,5},{2,6},{3,7},{8,12},{9,13},{10,14},{11,15},{4,0},{5,1},... | collective-permute-start | bytes 1572872 | tf_op jit(solution)/shard_map/ppermute | solution.py:445
  433.8 16.9 %collective-permute-start.37 = (f32[4,4,2,32,128]{4,3,2,1,0:T(8,128)}, f32[4,4,2,32,128]{4,3,2,1,0:T(8,128)S(1)}, u32[]{:S(2)}, u32[]{:S(2)}) collective-permute-start(f32[4,4,2,32,128]{4,3,2,1,0:T(8,128)} %copy-done.92), channel_id=1, source_target_pairs={{4,8},{5,9},{6,10},{7,11},{8,4},{9,5},{10,6},{11,7},{20,24},{21,25... | collective-permute-start | bytes 1572872 | tf_op jit(solution)/shard_map/ppermute | solution.py:445
  436.1 23.0 %collective-permute-start.38 = (f32[4,4,2,32,128]{4,3,2,1,0:T(8,128)}, f32[4,4,2,32,128]{4,3,2,1,0:T(8,128)S(1)}, u32[]{:S(2)}, u32[]{:S(2)}) collective-permute-start(f32[4,4,2,32,128]{4,3,2,1,0:T(8,128)} %copy-done.121), channel_id=1, source_target_pairs={{4,12},{5,13},{6,14},{7,15},{8,0},{9,1},{10,2},{11,3},{20,28},{21,... | collective-permute-start | bytes 1572872 | tf_op jit(solution)/shard_map/ppermute | solution.py:445
  437.4 34.2 %collective-permute-start.34 = (f32[4,4,2,32,128]{4,3,2,1,0:T(8,128)}, f32[4,4,2,32,128]{4,3,2,1,0:T(8,128)S(1)}, u32[]{:S(2)}, u32[]{:S(2)}) collective-permute-start(f32[4,4,2,32,128]{4,3,2,1,0:T(8,128)} %copy-done.125), channel_id=1, source_target_pairs={{0,4},{1,5},{2,6},{3,7},{8,12},{9,13},{10,14},{11,15},{4,0},{5,1},... | collective-permute-start | bytes 1572872 | tf_op jit(solution)/shard_map/ppermute | solution.py:445
  467.8 16.7 %collective-permute-start.41 = (f32[4,4,2,32,128]{4,3,2,1,0:T(8,128)S(1)}, f32[4,4,2,32,128]{4,3,2,1,0:T(8,128)S(1)}, u32[]{:S(2)}, u32[]{:S(2)}) collective-permute-start(f32[4,4,2,32,128]{4,3,2,1,0:T(8,128)S(1)} %get-tuple-element.208.refs_6_), channel_id=1, source_target_pairs={{4,8},{5,9},{6,10},{7,11},{8,4},{9,5},{10,6},{11,7},{20,24},{21,25... | collective-permute-start | bytes 1572872 | tf_op jit(solution)/shard_map/ppermute | solution.py:445
  470.1 23.6 %collective-permute-start.42 = (f32[4,4,2,32,128]{4,3,2,1,0:T(8,128)S(1)}, f32[4,4,2,32,128]{4,3,2,1,0:T(8,128)S(1)}, u32[]{:S(2)}, u32[]{:S(2)}) collective-permute-start(f32[4,4,2,32,128]{4,3,2,1,0:T(8,128)S(1)} %copy-done.132), channel_id=1, source_target_pairs={{4,12},{5,13},{6,14},{7,15},{8,0},{9,1},{10,2},{11,3},{20,28},{21,... | collective-permute-start | bytes 1572872 | tf_op jit(solution)/shard_map/ppermute | solution.py:445
  473.0 34.0 %collective-permute-start.35 = (f32[4,4,2,32,128]{4,3,2,1,0:T(8,128)S(1)}, f32[4,4,2,32,128]{4,3,2,1,0:T(8,128)S(1)}, u32[]{:S(2)}, u32[]{:S(2)}) collective-permute-start(f32[4,4,2,32,128]{4,3,2,1,0:T(8,128)S(1)} %get-tuple-element.203.refs_6_), channel_id=1, source_target_pairs={{4,8},{5,9},{6,10},{7,11},{8,4},{9,5},{10,6},{11,7},{20,24},{21,25... | collective-permute-start | bytes 1572872 | tf_op jit(solution)/shard_map/ppermute | solution.py:445
  476.6 37.4 %collective-permute-start.36 = (f32[4,4,2,32,128]{4,3,2,1,0:T(8,128)S(1)}, f32[4,4,2,32,128]{4,3,2,1,0:T(8,128)S(1)}, u32[]{:S(2)}, u32[]{:S(2)}) collective-permute-start(f32[4,4,2,32,128]{4,3,2,1,0:T(8,128)S(1)} %get-tuple-element.204), channel_id=1, source_target_pairs={{4,12},{5,13},{6,14},{7,15},{8,0},{9,1},{10,2},{11,3},{20,28},{21,... | collective-permute-start | bytes 1572872 | tf_op jit(solution)/shard_map/ppermute | solution.py:445
  521.7 81.0 %all-to-all-start.8 = ((f32[4,16,2,32,128]{4,3,2,1,0:T(8,128)}), f32[4,16,2,32,128]{4,3,2,1,0:T(8,128)}, u32[]{:S(2)}, u32[]{:S(2)}) async-start(f32[4,16,2,32,128]{4,3,2,1,0:T(8,128)} %gate.19), calls=%async_computation.8 | async-start | bytes 4194304 | tf_op jit(solution)/shard_map/all_to_all | solution.py:442
  526.4 16.6 %collective-permute-start.48 = (f32[4,4,2,32,128]{4,3,2,1,0:T(8,128)}, f32[4,4,2,32,128]{4,3,2,1,0:T(8,128)S(1)}, u32[]{:S(2)}, u32[]{:S(2)}) collective-permute-start(f32[4,4,2,32,128]{4,3,2,1,0:T(8,128)} %copy-done.135), channel_id=1, source_target_pairs={{0,4},{1,5},{2,6},{3,7},{8,12},{9,13},{10,14},{11,15},{4,0},{5,1},... | collective-permute-start | bytes 1572872 | tf_op jit(solution)/shard_map/ppermute | solution.py:445
  530.0 18.8 %collective-permute-start.46 = (f32[4,4,2,32,128]{4,3,2,1,0:T(8,128)}, f32[4,4,2,32,128]{4,3,2,1,0:T(8,128)S(1)}, u32[]{:S(2)}, u32[]{:S(2)}) collective-permute-start(f32[4,4,2,32,128]{4,3,2,1,0:T(8,128)} %copy-done.106), channel_id=1, source_target_pairs={{4,8},{5,9},{6,10},{7,11},{8,4},{9,5},{10,6},{11,7},{20,24},{21,25... | collective-permute-start | bytes 1572872 | tf_op jit(solution)/shard_map/ppermute | solution.py:445
  532.6 23.7 %collective-permute-start.47 = (f32[4,4,2,32,128]{4,3,2,1,0:T(8,128)}, f32[4,4,2,32,128]{4,3,2,1,0:T(8,128)S(1)}, u32[]{:S(2)}, u32[]{:S(2)}) collective-permute-start(f32[4,4,2,32,128]{4,3,2,1,0:T(8,128)} %copy-done.117), channel_id=1, source_target_pairs={{4,12},{5,13},{6,14},{7,15},{8,0},{9,1},{10,2},{11,3},{20,28},{21,... | collective-permute-start | bytes 1572872 | tf_op jit(solution)/shard_map/ppermute | solution.py:445
  533.9 28.5 %collective-permute-start.43 = (f32[4,4,2,32,128]{4,3,2,1,0:T(8,128)}, f32[4,4,2,32,128]{4,3,2,1,0:T(8,128)S(1)}, u32[]{:S(2)}, u32[]{:S(2)}) collective-permute-start(f32[4,4,2,32,128]{4,3,2,1,0:T(8,128)} %copy-done.124), channel_id=1, source_target_pairs={{4,0},{5,1},{6,2},{7,3},{12,8},{13,9},{14,10},{15,11},{20,16},{21,... | collective-permute-start | bytes 1572872 | tf_op jit(solution)/shard_map/ppermute | solution.py:445
  545.5 25.0 %collective-permute-start.50 = (f32[4,4,2,32,128]{4,3,2,1,0:T(8,128)S(1)}, f32[4,4,2,32,128]{4,3,2,1,0:T(8,128)S(1)}, u32[]{:S(2)}, u32[]{:S(2)}) collective-permute-start(f32[4,4,2,32,128]{4,3,2,1,0:T(8,128)S(1)} %get-tuple-element.227.refs_6_), channel_id=1, source_target_pairs={{4,8},{5,9},{6,10},{7,11},{8,4},{9,5},{10,6},{11,7},{20,24},{21,25... | collective-permute-start | bytes 1572872 | tf_op jit(solution)/shard_map/ppermute | solution.py:445
  547.5 31.2 %collective-permute-start.51 = (f32[4,4,2,32,128]{4,3,2,1,0:T(8,128)S(1)}, f32[4,4,2,32,128]{4,3,2,1,0:T(8,128)S(1)}, u32[]{:S(2)}, u32[]{:S(2)}) collective-permute-start(f32[4,4,2,32,128]{4,3,2,1,0:T(8,128)S(1)} %get-tuple-element.232), channel_id=1, source_target_pairs={{4,12},{5,13},{6,14},{7,15},{8,0},{9,1},{10,2},{11,3},{20,28},{21,... | collective-permute-start | bytes 1572872 | tf_op jit(solution)/shard_map/ppermute | solution.py:445
  561.1 23.1 %collective-permute-start.49 = (f32[4,4,2,32,128]{4,3,2,1,0:T(8,128)S(1)}, f32[4,4,2,32,128]{4,3,2,1,0:T(8,128)S(1)}, u32[]{:S(2)}, u32[]{:S(2)}) collective-permute-start(f32[4,4,2,32,128]{4,3,2,1,0:T(8,128)S(1)} %get-tuple-element.229), channel_id=1, source_target_pairs={{4,0},{5,1},{6,2},{7,3},{12,8},{13,9},{14,10},{15,11},{20,16},{21,... | collective-permute-start | bytes 1572872 | tf_op jit(solution)/shard_map/ppermute | solution.py:445
  563.7 26.1 %collective-permute-start.44 = (f32[4,4,2,32,128]{4,3,2,1,0:T(8,128)S(1)}, f32[4,4,2,32,128]{4,3,2,1,0:T(8,128)S(1)}, u32[]{:S(2)}, u32[]{:S(2)}) collective-permute-start(f32[4,4,2,32,128]{4,3,2,1,0:T(8,128)S(1)} %get-tuple-element.222.refs_6_), channel_id=1, source_target_pairs={{8,4},{9,5},{10,6},{11,7},{24,20},{25,21},{26,22},{27,23}} | collective-permute-start | bytes 1572872 | tf_op jit(solution)/shard_map/ppermute | solution.py:445
  569.1 31.1 %collective-permute-start.45 = (f32[4,4,2,32,128]{4,3,2,1,0:T(8,128)S(1)}, f32[4,4,2,32,128]{4,3,2,1,0:T(8,128)S(1)}, u32[]{:S(2)}, u32[]{:S(2)}) collective-permute-start(f32[4,4,2,32,128]{4,3,2,1,0:T(8,128)S(1)} %get-tuple-element.223), channel_id=1, source_target_pairs={{8,0},{9,1},{10,2},{11,3},{24,16},{25,17},{26,18},{27,19}} | collective-permute-start | bytes 1572872 | tf_op jit(solution)/shard_map/ppermute | solution.py:445
  602.7 59.2 %all-to-all-start.9 = ((f32[4,12,2,32,128]{4,3,2,1,0:T(8,128)}), f32[4,12,2,32,128]{4,3,2,1,0:T(8,128)S(1)}, u32[]{:S(2)}, u32[]{:S(2)}) async-start(f32[4,12,2,32,128]{4,3,2,1,0:T(8,128)} %gate.20), calls=%async_computation.9 | async-start | bytes 3145728 | tf_op jit(solution)/shard_map/all_to_all | solution.py:442
  607.7 28.8 %collective-permute-start.58 = (f32[4,4,2,32,128]{4,3,2,1,0:T(8,128)S(1)}, f32[4,4,2,32,128]{4,3,2,1,0:T(8,128)S(1)}, u32[]{:S(2)}, u32[]{:S(2)}) collective-permute-start(f32[4,4,2,32,128]{4,3,2,1,0:T(8,128)S(1)} %copy-done.89), channel_id=1, source_target_pairs={{8,4},{9,5},{10,6},{11,7},{24,20},{25,21},{26,22},{27,23}} | collective-permute-start | bytes 1572872 | tf_op jit(solution)/shard_map/ppermute | solution.py:445
  614.3 23.5 %collective-permute-start.59 = (f32[4,4,2,32,128]{4,3,2,1,0:T(8,128)S(1)}, f32[4,4,2,32,128]{4,3,2,1,0:T(8,128)S(1)}, u32[]{:S(2)}, u32[]{:S(2)}) collective-permute-start(f32[4,4,2,32,128]{4,3,2,1,0:T(8,128)S(1)} %copy-done.119), channel_id=1, source_target_pairs={{8,0},{9,1},{10,2},{11,3},{24,16},{25,17},{26,18},{27,19}} | collective-permute-start | bytes 1572872 | tf_op jit(solution)/shard_map/ppermute | solution.py:445
  624.1 24.9 %collective-permute-start.54 = (f32[4,4,2,32,128]{4,3,2,1,0:T(8,128)S(1)}, f32[4,4,2,32,128]{4,3,2,1,0:T(8,128)S(1)}, u32[]{:S(2)}, u32[]{:S(2)}) collective-permute-start(f32[4,4,2,32,128]{4,3,2,1,0:T(8,128)S(1)} %get-tuple-element.241.refs_6_), channel_id=1, source_target_pairs={{8,4},{9,5},{10,6},{11,7},{24,20},{25,21},{26,22},{27,23}} | collective-permute-start | bytes 1572872 | tf_op jit(solution)/shard_map/ppermute | solution.py:445
  626.6 32.9 %collective-permute-start.55 = (f32[4,4,2,32,128]{4,3,2,1,0:T(8,128)S(1)}, f32[4,4,2,32,128]{4,3,2,1,0:T(8,128)S(1)}, u32[]{:S(2)}, u32[]{:S(2)}) collective-permute-start(f32[4,4,2,32,128]{4,3,2,1,0:T(8,128)S(1)} %get-tuple-element.242), channel_id=1, source_target_pairs={{8,0},{9,1},{10,2},{11,3},{24,16},{25,17},{26,18},{27,19}} | collective-permute-start | bytes 1572872 | tf_op jit(solution)/shard_map/ppermute | solution.py:445
  663.0 28.5 %all-to-all-start.10 = ((f32[4,8,2,32,128]{4,3,2,1,0:T(8,128)}), f32[4,8,2,32,128]{4,3,2,1,0:T(8,128)S(1)}, u32[]{:S(2)}, u32[]{:S(2)}) async-start(f32[4,8,2,32,128]{4,3,2,1,0:T(8,128)} %gate.21), calls=%async_computation.10 | async-start | bytes 2097152 | tf_op jit(solution)/shard_map/all_to_all | solution.py:442
  (147 other events, 1351.2 us)

commit v4 on v3

--- a/solution.py
+++ b/solution.py
@@ -11,9 +11,9 @@
 layers = 4
 chunk_target = 16
 lanes = 128
-ends_of = {"field": (2, 10), "cells": (2, 6, 10), "gradient": (7, 11, 14)}
+ends_of = {"field": (2,), "cells": (2, 6), "gradient": (9, 14)}
 transfers = (
-    ("cells", 1, 1), ("cells", 2, 3), ("field", 2, 5), ("cells", 3, 7), ("gradient", 0, 11), ("gradient", 1, 14), ("gradient", 2, 17), ("gradient", 3, 19),
+    ("cells", 1, 1), ("cells", 2, 3), ("gradient", 0, 13), ("gradient", 1, 18), ("gradient", 2, 19),
 )
 f32, bf16 = jnp.float32, jnp.bfloat16
 ANY = pl.BlockSpec(memory_space=pl.ANY)
@@ -149,7 +149,7 @@
                 start += rows
             return total + fold_rows(values * values)
 
-        squares[...] += lax.fori_loop(0, step, one, jnp.zeros((8, nt), f32), unroll=2)
+        squares[...] += lax.fori_loop(0, step, one, jnp.zeros((8, nt), f32), unroll=8)
 
     *groups, squares = pl.pallas_call(
         kernel,
@@ -391,20 +391,30 @@
     counts = [g.shape[0] for g in flat]
     parts = nt // lanes
 
+    def pick(refs, x):
+        line = lambda ref, rows, h: ref.reshape(rows * parts * step, lanes)[pl.ds(h * step + x, rows, stride=parts * step), :]
+        return jnp.concatenate(
+            [jnp.concatenate([line(ref, rows, h) for h in range(parts)], axis=1) for ref, rows in zip(refs[:-1], counts)], axis=0
+        )
+
     def kernel(w, north_high, north_low, time_high, time_low, *refs):
         out = refs[-1]
         north_pair = (north_high[...], north_low[...])
         time_pair = (time_high[...], time_low[...])
 
+        if sum(counts) * 2 < ny:
+            taken = [pick(refs, x) for x in range(step)]
+            timed_high, timed_low = split(product(split(jnp.concatenate(taken, axis=0)), time_pair))
+            for x in range(step):
+                at = slice(x * sum(counts), (x + 1) * sum(counts))
+                out[x] = product(north_pair, (timed_high[at], timed_low[at])) + sign * w[x]
+            return
+
         def one(x, carry):
-            line = lambda ref, rows, h: ref.reshape(rows * parts * step, lanes)[pl.ds(h * step + x, rows, stride=parts * step), :]
-            values = jnp.concatenate(
-                [jnp.concatenate([line(ref, rows, h) for h in range(parts)], axis=1) for ref, rows in zip(refs[:-1], counts)], axis=0
-            )
-            out[x] = product(north_pair, split(product(split(values), time_pair))) + sign * w[x]
+            out[x] = product(north_pair, split(product(split(pick(refs, x)), time_pair))) + sign * w[x]
             return carry
 
-        lax.fori_loop(0, step, one, 0, unroll=2)
+        lax.fori_loop(0, step, one, 0, unroll=8)
 
     planes_block = pl.BlockSpec((step, ny, nt), lambda i: (i, 0, 0))
     return pl.pallas_call(

time: 718 us -> 683 us (0.951)
  local copies, waits for them, and re-layouts: 68.6 us -> 33.6 us
    ppermute x57, waiting for transfers between devices: 240 us -> 180 us  [move(): lax.ppermute(values, 'slab', [(a * peers + q, b * peers + q) for a, b in...]
    all_to_all x11 -> x8, waiting for transfers between devices: 17.5 us -> 76.8 us  [exchange(): lax.all_to_all(values, 'slab', 0, 0, tiled=True, axis_index_groups=in_layer)]
    unnamed x278 -> x122, local copies, waits for them, and re-layouts: 65.3 us -> 30.4 us
    pallas_call x2, Pallas kernels: 34.3 us -> 23 us  [finish(): pl.pallas_call(kernel, grid=(planes // step,), in_specs=[planes_block] +...]
    pallas_call x19, Pallas kernels: 35.1 us -> 45.9 us  [cross_terms(): pl.pallas_call(kernel, grid=(rows,), in_specs=specs, out_specs=[rows_of(s...]
    all_to_all x11 -> x8, starting transfers between devices: 48.2 us -> 37.9 us  [exchange(): lax.all_to_all(values, 'slab', 0, 0, tiled=True, axis_index_groups=in_layer)]
    ppermute x57, starting transfers between devices: 124 us -> 132 us  [move(): lax.ppermute(values, 'slab', [(a * peers + q, b * peers + q) for a, b in...]
    pallas_call x4 -> x3, Pallas kernels: 22.6 us -> 23.4 us  [packed(): pl.pallas_call(kernel, grid=(peers, rows // band), in_specs=[source, sour...]
  transfers between devices with their start and end apart: 72 -> 69, of which waited for: 39 -> 33; matrix products, arithmetic and copies ran while one was open for 0% -> 0% of each run, Pallas kernels for 23% -> 25%
where the time goes in v4:
time: 683 us; the launch traced here: 674 us
  waiting for transfers between devices  269 us (39%)
  Pallas kernels  192 us (28%)
  starting transfers between devices  175 us (26%)
  local copies, waits for them, and re-layouts  33.6 us (5%)
    ppermute x57, waiting for transfers between devices, move(): lax.ppermute(values, 'slab', [(a * peers + q, b * peers + q) for a, b in...  180 us
    ppermute x57, starting transfers between devices, move(): lax.ppermute(values, 'slab', [(a * peers + q, b * peers + q) for a, b in...  132 us
    pallas_call x19, Pallas kernels, cells(): pl.pallas_call(kernel, grid=(rows,), in_specs=specs, out_specs=out_specs,...  86.9 us
    all_to_all x8, waiting for transfers between devices, exchange(): lax.all_to_all(values, 'slab', 0, 0, tiled=True, axis_index_groups=in_layer)  76.8 us
    pallas_call x19, Pallas kernels, cross_terms(): pl.pallas_call(kernel, grid=(rows,), in_specs=specs, out_specs=[rows_of(s...  45.9 us
    all_to_all x8, starting transfers between devices, exchange(): lax.all_to_all(values, 'slab', 0, 0, tiled=True, axis_index_groups=in_layer)  37.9 us
    unnamed x122, local copies, waits for them, and re-layouts  30.4 us
    pallas_call x3, Pallas kernels, packed(): pl.pallas_call(kernel, grid=(peers, rows // band), in_specs=[source, sour...  23.4 us
  transfers between devices with their start and end apart: 69, of which 33 were waited for; matrix products, arithmetic and copies ran while one was open for 0% of the time, Pallas kernels for 25%

profile of v4, /device:TPU:18, one launch (start us, length us, event | category | flops | bytes accessed | tf_op | source)
XLA Modules:
  0.0 674.1 jit_solution(2140302384687201828)
XLA Ops:
  0.6 3.8 packed.3._
  4.5 4.4 all-to-all-start
  9.1 12.5 %field.1 = (f32[32,2,32,128]{3,2,1,0:T(8,128)S(1)}, f32[224,2,32,128]{3,2,1,0:T(8,128)}, f32[8,256]{1,0:T(8,128)S(1)}) custom-call(f32[32,256,256]{2,1,0:T(8,128)} %w.3, bf16[256,256]{1,0:T(8,128)(2,1)S(1)} %get-tuple-element.122.north_high, bf16[256,256]{1,0:T(8,128)(2,1)S(1)} %get-tuple-element.123.north_low, ...), custom_call_target="tpu_custom_call" | custom-call | flops 1 | bytes 1 | tf_op jit(solution)/shard_map/field/pallas_call | solution.py:154
  22.6 12.1 %all-to-all-done.__1_.refs_10_ = f32[4,2,2,32,8,128]{5,4,3,2,1,0:T(8,128)} async-done(((f32[4,2,2,32,8,128]{5,4,3,2,1,0:T(8,128)}), f32[4,2,2,32,8,128]{5,4,3,2,1,0:T(8,128)}, u32[]{:S(2)}, u32[]{:S(2)}) %all-to-all-start) | async-done | bytes 2097184 | tf_op jit(solution)/shard_map/all_to_all | solution.py:452
  39.5 4.9 packed.4.__1_.__0_
  55.7 5.6 all-to-all-start.2
  66.2 10.9 %collective-permute-done.3.rest_0_.refs_5_ = f32[4,4,2,32,128]{4,3,2,1,0:T(8,128)S(1)} collective-permute-done((f32[4,4,2,32,128]{4,3,2,1,0:T(8,128)S(1)}, f32[4,4,2,32,128]{4,3,2,1,0:T(8,128)S(1)}, u32[]{:S(2)}, u32[]{:S(2)}) %collective-permute-start.3) | collective-permute-done | bytes 524320 | tf_op jit(solution)/shard_map/ppermute | solution.py:455
  79.4 14.7 %packed.5.rest_3_.__0_ = f32[4,2,2,32,40,128]{5,4,3,2,1,0:T(8,128)} custom-call(s32[32,256,256]{2,1,0:T(8,128)} %c.5, s32[32,256,256]{2,1,0:T(8,128)} %e.5, f32[4,4,2,32,128]{4,3,2,1,0:T(8,128)S(1)} %get-tuple-element.138.rest_0_), custom_call_target="tpu_custom_call" | custom-call | flops 1 | bytes 1 | tf_op jit(solution)/shard_map/packed/pallas_call | solution.py:180
  96.5 46.8 %all-to-all-done.2.rest_1_.refs_12_.__1_.refs_9_ = f32[4,56,2,32,128]{4,3,2,1,0:T(8,128)} async-done(((f32[4,56,2,32,128]{4,3,2,1,0:T(8,128)}), f32[4,56,2,32,128]{4,3,2,1,0:T(8,128)}, u32[]{:S(2)}, u32[]{:S(2)}) %all-to-all-start.2) | async-done | bytes 7340064 | tf_op jit(solution)/shard_map/all_to_all | solution.py:452
  149.3 4.8 all-to-all-start.3
  160.9 10.1 %collective-permute-done.rest_0_.refs_5_ = f32[4,4,2,32,128]{4,3,2,1,0:T(8,128)S(1)} collective-permute-done((f32[4,4,2,32,128]{4,3,2,1,0:T(8,128)S(1)}, f32[4,4,2,32,128]{4,3,2,1,0:T(8,128)S(1)}, u32[]{:S(2)}, u32[]{:S(2)}) %collective-permute-start) | collective-permute-done | bytes 524320 | tf_op jit(solution)/shard_map/ppermute | solution.py:455
  175.3 17.8 %collective-permute-done.7.rest_0_.refs_5_ = f32[4,4,2,32,128]{4,3,2,1,0:T(8,128)S(1)} collective-permute-done((f32[4,4,2,32,128]{4,3,2,1,0:T(8,128)}, f32[4,4,2,32,128]{4,3,2,1,0:T(8,128)S(1)}, u32[]{:S(2)}, u32[]{:S(2)}) %collective-permute-start.7) | collective-permute-done | bytes 524320 | tf_op jit(solution)/shard_map/ppermute | solution.py:455
  196.8 3.9 cells.20
  207.4 3.9 cells.21
  212.9 6.1 all-to-all-start.4
  219.0 7.8 %collective-permute-start.15 = (f32[4,4,2,32,128]{4,3,2,1,0:T(8,128)}, f32[4,4,2,32,128]{4,3,2,1,0:T(8,128)S(1)}, u32[]{:S(2)}, u32[]{:S(2)}) collective-permute-start(f32[4,4,2,32,128]{4,3,2,1,0:T(8,128)} %copy-done.58), channel_id=1, source_target_pairs={{0,4},{1,5},{2,6},{3,7},{8,12},{9,13},{10,14},{11,15},{4,0},{5,1},... | collective-permute-start | bytes 1572872 | tf_op jit(solution)/shard_map/ppermute | solution.py:455
  230.2 9.6 %collective-permute-done.15.rest_0_.refs_5_ = f32[4,4,2,32,128]{4,3,2,1,0:T(8,128)S(1)} collective-permute-done((f32[4,4,2,32,128]{4,3,2,1,0:T(8,128)}, f32[4,4,2,32,128]{4,3,2,1,0:T(8,128)S(1)}, u32[]{:S(2)}, u32[]{:S(2)}) %collective-permute-start.15) | collective-permute-done | bytes 524320 | tf_op jit(solution)/shard_map/ppermute | solution.py:455
  246.0 6.3 collective-permute-done.14.refs_4_
  252.3 5.5 cells.22
  257.8 3.9 collective-permute-start.16
  268.0 6.8 %collective-permute-done.18.refs_4_ = f32[4,4,2,32,128]{4,3,2,1,0:T(8,128)S(1)} collective-permute-done((f32[4,4,2,32,128]{4,3,2,1,0:T(8,128)S(1)}, f32[4,4,2,32,128]{4,3,2,1,0:T(8,128)S(1)}, u32[]{:S(2)}, u32[]{:S(2)}) %collective-permute-start.18) | collective-permute-done | bytes 524320 | tf_op jit(solution)/shard_map/ppermute | solution.py:455
  274.8 5.5 cells.23
  280.2 3.9 collective-permute-start.24
  291.1 6.2 collective-permute-done.12.refs_4_
  297.3 5.5 cells.24
  302.8 3.9 collective-permute-start.19
  320.6 14.0 %all-to-all-done.4.refs_10_.__1_ = f32[4,2,2,32,40,128]{5,4,3,2,1,0:T(8,128)} async-done(((f32[4,2,2,32,40,128]{5,4,3,2,1,0:T(8,128)}), f32[4,2,2,32,40,128]{5,4,3,2,1,0:T(8,128)}, u32[]{:S(2)}, u32[]{:S(2)}) %all-to-all-start.4) | async-done | bytes 10485792 | tf_op jit(solution)/shard_map/all_to_all | solution.py:452
  336.8 5.5 cells.25
  342.2 7.7 %collective-permute-start.25 = (f32[4,4,2,32,128]{4,3,2,1,0:T(8,128)S(1)}, f32[4,4,2,32,128]{4,3,2,1,0:T(8,128)S(1)}, u32[]{:S(2)}, u32[]{:S(2)}) collective-permute-start(f32[4,4,2,32,128]{4,3,2,1,0:T(8,128)S(1)} %get-tuple-element.179), channel_id=1, source_target_pairs={{0,4},{1,5},{2,6},{3,7},{8,12},{9,13},{10,14},{11,15},{4,0},{5,1},... | collective-permute-start | bytes 1572872 | tf_op jit(solution)/shard_map/ppermute | solution.py:455
  356.1 5.7 cells.26
  364.7 3.9 collective-permute-start.31
  370.0 8.5 %collective-permute-done.21.refs_4_ = f32[4,4,2,32,128]{4,3,2,1,0:T(8,128)S(1)} collective-permute-done((f32[4,4,2,32,128]{4,3,2,1,0:T(8,128)S(1)}, f32[4,4,2,32,128]{4,3,2,1,0:T(8,128)S(1)}, u32[]{:S(2)}, u32[]{:S(2)}) %collective-permute-start.21) | collective-permute-done | bytes 524320 | tf_op jit(solution)/shard_map/ppermute | solution.py:455
  378.4 5.6 cells.27
  384.0 3.9 collective-permute-start.28
  394.0 6.9 %collective-permute-done.32.refs_4_ = f32[4,4,2,32,128]{4,3,2,1,0:T(8,128)S(1)} collective-permute-done((f32[4,4,2,32,128]{4,3,2,1,0:T(8,128)S(1)}, f32[4,4,2,32,128]{4,3,2,1,0:T(8,128)S(1)}, u32[]{:S(2)}, u32[]{:S(2)}) %collective-permute-start.32) | collective-permute-done | bytes 524320 | tf_op jit(solution)/shard_map/ppermute | solution.py:455
  400.9 5.5 cells.28
  406.4 3.9 collective-permute-start.34
  415.1 8.4 %collective-permute-done.36.refs_4_ = f32[4,4,2,32,128]{4,3,2,1,0:T(8,128)S(1)} collective-permute-done((f32[4,4,2,32,128]{4,3,2,1,0:T(8,128)S(1)}, f32[4,4,2,32,128]{4,3,2,1,0:T(8,128)S(1)}, u32[]{:S(2)}, u32[]{:S(2)}) %collective-permute-start.36) | collective-permute-done | bytes 524320 | tf_op jit(solution)/shard_map/ppermute | solution.py:455
  423.4 5.5 cells.29
  428.9 3.9 collective-permute-start.39
  437.2 3.8 collective-permute-start.37
  442.3 9.8 %collective-permute-done.39.rest_0_.refs_5_ = f32[4,4,2,32,128]{4,3,2,1,0:T(8,128)S(1)} collective-permute-done((f32[4,4,2,32,128]{4,3,2,1,0:T(8,128)S(1)}, f32[4,4,2,32,128]{4,3,2,1,0:T(8,128)S(1)}, u32[]{:S(2)}, u32[]{:S(2)}) %collective-permute-start.39) | collective-permute-done | bytes 524320 | tf_op jit(solution)/shard_map/ppermute | solution.py:455
  455.0 5.7 cells.30
  460.8 6.3 collective-permute-done.38.refs_4_
  467.1 5.5 cells.31
  474.2 5.1 all-to-all-start.5
  486.6 9.3 %collective-permute-done.42.rest_0_.refs_5_ = f32[4,4,2,32,128]{4,3,2,1,0:T(8,128)S(1)} collective-permute-done((f32[4,4,2,32,128]{4,3,2,1,0:T(8,128)}, f32[4,4,2,32,128]{4,3,2,1,0:T(8,128)S(1)}, u32[]{:S(2)}, u32[]{:S(2)}) %collective-permute-start.42) | collective-permute-done | bytes 524320 | tf_op jit(solution)/shard_map/ppermute | solution.py:455
  502.3 6.4 collective-permute-done.41.refs_4_
  508.8 5.4 cells.32
  520.3 4.7 collective-permute-start.50
  526.4 4.9 collective-permute-done.47.refs_4_
  531.3 5.3 cells.33
  539.2 5.5 collective-permute-start.44
  546.0 7.7 %collective-permute-done.51.refs_4_ = f32[4,4,2,32,128]{4,3,2,1,0:T(8,128)S(1)} collective-permute-done((f32[4,4,2,32,128]{4,3,2,1,0:T(8,128)S(1)}, f32[4,4,2,32,128]{4,3,2,1,0:T(8,128)S(1)}, u32[]{:S(2)}, u32[]{:S(2)}) %collective-permute-start.51) | collective-permute-done | bytes 524320 | tf_op jit(solution)/shard_map/ppermute | solution.py:455
  553.8 5.3 cells.34
  565.0 10.4 %collective-permute-done.45.refs_4_ = f32[4,4,2,32,128]{4,3,2,1,0:T(8,128)S(1)} collective-permute-done((f32[4,4,2,32,128]{4,3,2,1,0:T(8,128)S(1)}, f32[4,4,2,32,128]{4,3,2,1,0:T(8,128)S(1)}, u32[]{:S(2)}, u32[]{:S(2)}) %collective-permute-start.45) | collective-permute-done | bytes 524320 | tf_op jit(solution)/shard_map/ppermute | solution.py:455
  580.0 4.7 all-to-all-start.6
  586.0 6.5 collective-permute-start.58
  593.9 7.2 %collective-permute-done.53.rest_0_.refs_5_ = f32[4,4,2,32,128]{4,3,2,1,0:T(8,128)S(1)} collective-permute-done((f32[4,4,2,32,128]{4,3,2,1,0:T(8,128)}, f32[4,4,2,32,128]{4,3,2,1,0:T(8,128)S(1)}, u32[]{:S(2)}, u32[]{:S(2)}) %collective-permute-start.53) | collective-permute-done | bytes 524320 | tf_op jit(solution)/shard_map/ppermute | solution.py:455
  609.1 7.0 %collective-permute-done.56 = f32[8,256]{1,0:T(8,128)S(1)} collective-permute-done((f32[8,256]{1,0:T(8,128)S(1)}, f32[8,256]{1,0:T(8,128)S(1)}, u32[]{:S(2)}, u32[]{:S(2)}) %collective-permute-start.56) | collective-permute-done | bytes 8224 | tf_op jit(solution)/shard_map/ppermute | solution.py:473
  621.1 6.1 collective-permute-done.54.refs_3_
  627.2 10.7 %collective-permute-done.55.refs_4_ = f32[4,4,2,32,128]{4,3,2,1,0:T(8,128)S(1)} collective-permute-done((f32[4,4,2,32,128]{4,3,2,1,0:T(8,128)S(1)}, f32[4,4,2,32,128]{4,3,2,1,0:T(8,128)S(1)}, u32[]{:S(2)}, u32[]{:S(2)}) %collective-permute-start.55) | collective-permute-done | bytes 524320 | tf_op jit(solution)/shard_map/ppermute | solution.py:455
  650.0 13.4 %finish.2.w = f32[32,256,256]{2,1,0:T(8,128)} custom-call(f32[32,256,256]{2,1,0:T(8,128)} %w.3, bf16[256,224]{1,0:T(8,128)(2,1)S(1)} %get-tuple-element.127.north_high, bf16[256,224]{1,0:T(8,128)(2,1)S(1)} %copy-done.43, bf16[256,256]{1,0:T(8,128)(2,1)S(1)} %get-tuple-element.129.time_high, bf16[256,256]{1,0:T(8,128)(2,1)S(1)} %get-tuple-element.130.time_low, ...), custom_call_target="tpu_custom_call" | custom-call | flops 1 | bytes 1 | tf_op jit(solution)/shard_map/finish/pallas_call | solution.py:420
  663.4 9.6 %finish.3 = f32[32,256,256]{2,1,0:T(8,128)} custom-call(f32[32,256,256]{2,1,0:T(8,128)} %finish.2.w, bf16[256,32]{1,0:T(8,128)(2,1)S(1)} %get-tuple-element.236.north_high, bf16[256,32]{1,0:T(8,128)(2,1)S(1)} %copy-done.45, bf16[256,256]{1,0:T(8,128)(2,1)S(1)} %get-tuple-element.129.time_high, bf16[256,256]{1,0:T(8,128)(2,1)S(1)} %get-tuple-element.130.time_low, ...), custom_call_target="tpu_custom_call" | custom-call | flops 1 | bytes 1 | tf_op jit(solution)/shard_map/finish/pallas_call | solution.py:420
  (257 shorter events, 187.8 us)
Async XLA Ops:
  4.5 30.2 %all-to-all-start = ((f32[4,2,2,32,8,128]{5,4,3,2,1,0:T(8,128)}), f32[4,2,2,32,8,128]{5,4,3,2,1,0:T(8,128)}, u32[]{:S(2)}, u32[]{:S(2)}) async-start(f32[4,2,2,32,8,128]{5,4,3,2,1,0:T(8,128)} %packed.3._), calls=%async_computation | async-start | bytes 4194304 | tf_op jit(solution)/shard_map/all_to_all | solution.py:452
  34.7 18.0 %all-to-all-start.1 = ((f32[4,8,2,32,128]{4,3,2,1,0:T(8,128)}), f32[4,8,2,32,128]{4,3,2,1,0:T(8,128)S(1)}, u32[]{:S(2)}, u32[]{:S(2)}) async-start(f32[4,8,2,32,128]{4,3,2,1,0:T(8,128)} %gate.8._.rest_0_), calls=%async_computation.1 | async-start | bytes 2097152 | tf_op jit(solution)/shard_map/all_to_all | solution.py:452
  55.7 87.6 %all-to-all-start.2 = ((f32[4,56,2,32,128]{4,3,2,1,0:T(8,128)}), f32[4,56,2,32,128]{4,3,2,1,0:T(8,128)}, u32[]{:S(2)}, u32[]{:S(2)}) async-start(f32[4,56,2,32,128]{4,3,2,1,0:T(8,128)} %gate.10), calls=%async_computation.2 | async-start | bytes 14680064 | tf_op jit(solution)/shard_map/all_to_all | solution.py:452
  61.4 15.7 %collective-permute-start.3 = (f32[4,4,2,32,128]{4,3,2,1,0:T(8,128)S(1)}, f32[4,4,2,32,128]{4,3,2,1,0:T(8,128)S(1)}, u32[]{:S(2)}, u32[]{:S(2)}) collective-permute-start(f32[4,4,2,32,128]{4,3,2,1,0:T(8,128)S(1)} %get-tuple-element.242), channel_id=1, source_target_pairs={{0,4},{1,5},{2,6},{3,7},{8,12},{9,13},{10,14},{11,15},{16,20},{17,... | collective-permute-start | bytes 1572872 | tf_op jit(solution)/shard_map/ppermute | solution.py:455
  64.9 29.2 %collective-permute-start.6 = (f32[4,4,2,32,128]{4,3,2,1,0:T(8,128)}, f32[4,4,2,32,128]{4,3,2,1,0:T(8,128)S(1)}, u32[]{:S(2)}, u32[]{:S(2)}) collective-permute-start(f32[4,4,2,32,128]{4,3,2,1,0:T(8,128)} %get-tuple-element.243.__2_), channel_id=1, source_target_pairs={{0,4},{1,5},{2,6},{3,7},{8,12},{9,13},{10,14},{11,15},{16,20},{17,... | collective-permute-start | bytes 1572872 | tf_op jit(solution)/shard_map/ppermute | solution.py:455
  77.4 16.8 %collective-permute-start.4 = (f32[4,4,2,32,128]{4,3,2,1,0:T(8,128)S(1)}, f32[4,4,2,32,128]{4,3,2,1,0:T(8,128)S(1)}, u32[]{:S(2)}, u32[]{:S(2)}) collective-permute-start(f32[4,4,2,32,128]{4,3,2,1,0:T(8,128)S(1)} %get-tuple-element.138.rest_0_), channel_id=1, source_target_pairs={{4,8},{5,9},{6,10},{7,11},{20,24},{21,25},{22,26},{23,27}} | collective-permute-start | bytes 1572872 | tf_op jit(solution)/shard_map/ppermute | solution.py:455
  78.7 17.8 %collective-permute-start.5 = (f32[4,4,2,32,128]{4,3,2,1,0:T(8,128)S(1)}, f32[4,4,2,32,128]{4,3,2,1,0:T(8,128)S(1)}, u32[]{:S(2)}, u32[]{:S(2)}) collective-permute-start(f32[4,4,2,32,128]{4,3,2,1,0:T(8,128)S(1)} %get-tuple-element.139), channel_id=1, source_target_pairs={{4,12},{5,13},{6,14},{7,15},{20,28},{21,29},{22,30},{23,31}} | collective-permute-start | bytes 1572872 | tf_op jit(solution)/shard_map/ppermute | solution.py:455
  149.3 53.9 %all-to-all-start.3 = ((f32[4,2,2,32,16,128]{5,4,3,2,1,0:T(8,128)}), f32[4,2,2,32,16,128]{5,4,3,2,1,0:T(8,128)}, u32[]{:S(2)}, u32[]{:S(2)}) async-start(f32[4,2,2,32,16,128]{5,4,3,2,1,0:T(8,128)} %gate.11), calls=%async_computation.3 | async-start | bytes 8388608 | tf_op jit(solution)/shard_map/all_to_all | solution.py:452
  158.8 37.9 %collective-permute-start.8 = (f32[4,4,2,32,128]{4,3,2,1,0:T(8,128)}, f32[4,4,2,32,128]{4,3,2,1,0:T(8,128)S(1)}, u32[]{:S(2)}, u32[]{:S(2)}) collective-permute-start(f32[4,4,2,32,128]{4,3,2,1,0:T(8,128)} %get-tuple-element.140.refs_6_), channel_id=1, source_target_pairs={{4,8},{5,9},{6,10},{7,11},{20,24},{21,25},{22,26},{23,27}} | collective-permute-start | bytes 1572872 | tf_op jit(solution)/shard_map/ppermute | solution.py:455
  160.1 33.0 %collective-permute-start.7 = (f32[4,4,2,32,128]{4,3,2,1,0:T(8,128)}, f32[4,4,2,32,128]{4,3,2,1,0:T(8,128)S(1)}, u32[]{:S(2)}, u32[]{:S(2)}) collective-permute-start(f32[4,4,2,32,128]{4,3,2,1,0:T(8,128)} %copy-done.60), channel_id=1, source_target_pairs={{0,4},{1,5},{2,6},{3,7},{8,12},{9,13},{10,14},{11,15},{4,0},{5,1},... | collective-permute-start | bytes 1572872 | tf_op jit(solution)/shard_map/ppermute | solution.py:455
  160.2 36.6 %collective-permute-start.9 = (f32[4,4,2,32,128]{4,3,2,1,0:T(8,128)}, f32[4,4,2,32,128]{4,3,2,1,0:T(8,128)S(1)}, u32[]{:S(2)}, u32[]{:S(2)}) collective-permute-start(f32[4,4,2,32,128]{4,3,2,1,0:T(8,128)} %copy-done.55), channel_id=1, source_target_pairs={{4,12},{5,13},{6,14},{7,15},{20,28},{21,29},{22,30},{23,31}} | collective-permute-start | bytes 1572872 | tf_op jit(solution)/shard_map/ppermute | solution.py:455
  173.2 28.4 %collective-permute-start.1 = (f32[4,4,2,32,128]{4,3,2,1,0:T(8,128)S(1)}, f32[4,4,2,32,128]{4,3,2,1,0:T(8,128)S(1)}, u32[]{:S(2)}, u32[]{:S(2)}) collective-permute-start(f32[4,4,2,32,128]{4,3,2,1,0:T(8,128)S(1)} %get-tuple-element.136.refs_6_), channel_id=1, source_target_pairs={{4,8},{5,9},{6,10},{7,11},{20,24},{21,25},{22,26},{23,27}} | collective-permute-start | bytes 1572872 | tf_op jit(solution)/shard_map/ppermute | solution.py:455
  174.6 27.8 %collective-permute-start.2 = (f32[4,4,2,32,128]{4,3,2,1,0:T(8,128)S(1)}, f32[4,4,2,32,128]{4,3,2,1,0:T(8,128)S(1)}, u32[]{:S(2)}, u32[]{:S(2)}) collective-permute-start(f32[4,4,2,32,128]{4,3,2,1,0:T(8,128)S(1)} %get-tuple-element.137), channel_id=1, source_target_pairs={{4,12},{5,13},{6,14},{7,15},{20,28},{21,29},{22,30},{23,31}} | collective-permute-start | bytes 1572872 | tf_op jit(solution)/shard_map/ppermute | solution.py:455
  212.9 121.8 %all-to-all-start.4 = ((f32[4,2,2,32,40,128]{5,4,3,2,1,0:T(8,128)}), f32[4,2,2,32,40,128]{5,4,3,2,1,0:T(8,128)}, u32[]{:S(2)}, u32[]{:S(2)}) async-start(f32[4,2,2,32,40,128]{5,4,3,2,1,0:T(8,128)} %gate.12), calls=%async_computation.4 | async-start | bytes 20971520 | tf_op jit(solution)/shard_map/all_to_all | solution.py:452
  219.0 20.8 %collective-permute-start.15 = (f32[4,4,2,32,128]{4,3,2,1,0:T(8,128)}, f32[4,4,2,32,128]{4,3,2,1,0:T(8,128)S(1)}, u32[]{:S(2)}, u32[]{:S(2)}) collective-permute-start(f32[4,4,2,32,128]{4,3,2,1,0:T(8,128)} %copy-done.58), channel_id=1, source_target_pairs={{0,4},{1,5},{2,6},{3,7},{8,12},{9,13},{10,14},{11,15},{4,0},{5,1},... | collective-permute-start | bytes 1572872 | tf_op jit(solution)/shard_map/ppermute | solution.py:455
  226.8 19.1 %collective-permute-start.13 = (f32[4,4,2,32,128]{4,3,2,1,0:T(8,128)S(1)}, f32[4,4,2,32,128]{4,3,2,1,0:T(8,128)S(1)}, u32[]{:S(2)}, u32[]{:S(2)}) collective-permute-start(f32[4,4,2,32,128]{4,3,2,1,0:T(8,128)S(1)} %copy-done.35), channel_id=1, source_target_pairs={{4,8},{5,9},{6,10},{7,11},{8,4},{9,5},{10,6},{11,7},{20,24},{21,25... | collective-permute-start | bytes 1572872 | tf_op jit(solution)/shard_map/ppermute | solution.py:455
  228.8 23.5 %collective-permute-start.14 = (f32[4,4,2,32,128]{4,3,2,1,0:T(8,128)S(1)}, f32[4,4,2,32,128]{4,3,2,1,0:T(8,128)S(1)}, u32[]{:S(2)}, u32[]{:S(2)}) collective-permute-start(f32[4,4,2,32,128]{4,3,2,1,0:T(8,128)S(1)} %copy-done.51), channel_id=1, source_target_pairs={{4,12},{5,13},{6,14},{7,15},{8,0},{9,1},{10,2},{11,3},{20,28},{21,... | collective-permute-start | bytes 1572872 | tf_op jit(solution)/shard_map/ppermute | solution.py:455
  230.1 31.8 %collective-permute-start.10 = (f32[4,4,2,32,128]{4,3,2,1,0:T(8,128)}, f32[4,4,2,32,128]{4,3,2,1,0:T(8,128)S(1)}, u32[]{:S(2)}, u32[]{:S(2)}) collective-permute-start(f32[4,4,2,32,128]{4,3,2,1,0:T(8,128)} %copy-done.56), channel_id=1, source_target_pairs={{0,4},{1,5},{2,6},{3,7},{8,12},{9,13},{10,14},{11,15},{4,0},{5,1},... | collective-permute-start | bytes 1572872 | tf_op jit(solution)/shard_map/ppermute | solution.py:455
  242.6 25.4 %collective-permute-start.17 = (f32[4,4,2,32,128]{4,3,2,1,0:T(8,128)S(1)}, f32[4,4,2,32,128]{4,3,2,1,0:T(8,128)S(1)}, u32[]{:S(2)}, u32[]{:S(2)}) collective-permute-start(f32[4,4,2,32,128]{4,3,2,1,0:T(8,128)S(1)} %get-tuple-element.157.refs_6_), channel_id=1, source_target_pairs={{4,8},{5,9},{6,10},{7,11},{8,4},{9,5},{10,6},{11,7},{20,24},{21,25... | collective-permute-start | bytes 1572872 | tf_op jit(solution)/shard_map/ppermute | solution.py:455
  244.6 30.2 %collective-permute-start.18 = (f32[4,4,2,32,128]{4,3,2,1,0:T(8,128)S(1)}, f32[4,4,2,32,128]{4,3,2,1,0:T(8,128)S(1)}, u32[]{:S(2)}, u32[]{:S(2)}) collective-permute-start(f32[4,4,2,32,128]{4,3,2,1,0:T(8,128)S(1)} %get-tuple-element.164), channel_id=1, source_target_pairs={{4,12},{5,13},{6,14},{7,15},{8,0},{9,1},{10,2},{11,3},{20,28},{21,... | collective-permute-start | bytes 1572872 | tf_op jit(solution)/shard_map/ppermute | solution.py:455
  257.8 26.9 %collective-permute-start.16 = (f32[4,4,2,32,128]{4,3,2,1,0:T(8,128)S(1)}, f32[4,4,2,32,128]{4,3,2,1,0:T(8,128)S(1)}, u32[]{:S(2)}, u32[]{:S(2)}) collective-permute-start(f32[4,4,2,32,128]{4,3,2,1,0:T(8,128)S(1)} %get-tuple-element.161), channel_id=1, source_target_pairs={{0,4},{1,5},{2,6},{3,7},{8,12},{9,13},{10,14},{11,15},{4,0},{5,1},... | collective-permute-start | bytes 1572872 | tf_op jit(solution)/shard_map/ppermute | solution.py:455
  264.7 26.3 %collective-permute-start.11 = (f32[4,4,2,32,128]{4,3,2,1,0:T(8,128)S(1)}, f32[4,4,2,32,128]{4,3,2,1,0:T(8,128)S(1)}, u32[]{:S(2)}, u32[]{:S(2)}) collective-permute-start(f32[4,4,2,32,128]{4,3,2,1,0:T(8,128)S(1)} %get-tuple-element.152.refs_6_), channel_id=1, source_target_pairs={{4,8},{5,9},{6,10},{7,11},{8,4},{9,5},{10,6},{11,7},{20,24},{21,25... | collective-permute-start | bytes 1572872 | tf_op jit(solution)/shard_map/ppermute | solution.py:455
  266.6 30.7 %collective-permute-start.12 = (f32[4,4,2,32,128]{4,3,2,1,0:T(8,128)S(1)}, f32[4,4,2,32,128]{4,3,2,1,0:T(8,128)S(1)}, u32[]{:S(2)}, u32[]{:S(2)}) collective-permute-start(f32[4,4,2,32,128]{4,3,2,1,0:T(8,128)S(1)} %get-tuple-element.153), channel_id=1, source_target_pairs={{4,12},{5,13},{6,14},{7,15},{8,0},{9,1},{10,2},{11,3},{20,28},{21,... | collective-permute-start | bytes 1572872 | tf_op jit(solution)/shard_map/ppermute | solution.py:455
  280.2 26.6 %collective-permute-start.24 = (f32[4,4,2,32,128]{4,3,2,1,0:T(8,128)S(1)}, f32[4,4,2,32,128]{4,3,2,1,0:T(8,128)S(1)}, u32[]{:S(2)}, u32[]{:S(2)}) collective-permute-start(f32[4,4,2,32,128]{4,3,2,1,0:T(8,128)S(1)} %get-tuple-element.174), channel_id=1, source_target_pairs={{0,4},{1,5},{2,6},{3,7},{8,12},{9,13},{10,14},{11,15},{4,0},{5,1},... | collective-permute-start | bytes 1572872 | tf_op jit(solution)/shard_map/ppermute | solution.py:455
  287.6 27.6 %collective-permute-start.22 = (f32[4,4,2,32,128]{4,3,2,1,0:T(8,128)S(1)}, f32[4,4,2,32,128]{4,3,2,1,0:T(8,128)S(1)}, u32[]{:S(2)}, u32[]{:S(2)}) collective-permute-start(f32[4,4,2,32,128]{4,3,2,1,0:T(8,128)S(1)} %get-tuple-element.163.refs_6_), channel_id=1, source_target_pairs={{4,8},{5,9},{6,10},{7,11},{8,4},{9,5},{10,6},{11,7},{20,24},{21,25... | collective-permute-start | bytes 1572872 | tf_op jit(solution)/shard_map/ppermute | solution.py:455
  289.7 30.1 %collective-permute-start.23 = (f32[4,4,2,32,128]{4,3,2,1,0:T(8,128)S(1)}, f32[4,4,2,32,128]{4,3,2,1,0:T(8,128)S(1)}, u32[]{:S(2)}, u32[]{:S(2)}) collective-permute-start(f32[4,4,2,32,128]{4,3,2,1,0:T(8,128)S(1)} %get-tuple-element.173), channel_id=1, source_target_pairs={{4,12},{5,13},{6,14},{7,15},{8,0},{9,1},{10,2},{11,3},{20,28},{21,... | collective-permute-start | bytes 1572872 | tf_op jit(solution)/shard_map/ppermute | solution.py:455
  302.8 47.1 %collective-permute-start.19 = (f32[4,4,2,32,128]{4,3,2,1,0:T(8,128)}, f32[4,4,2,32,128]{4,3,2,1,0:T(8,128)}, u32[]{:S(2)}, u32[]{:S(2)}) collective-permute-start(f32[4,4,2,32,128]{4,3,2,1,0:T(8,128)} %get-tuple-element.169), channel_id=1, source_target_pairs={{0,4},{1,5},{2,6},{3,7},{8,12},{9,13},{10,14},{11,15},{4,0},{5,1},... | collective-permute-start | bytes 1572872 | tf_op jit(solution)/shard_map/ppermute | solution.py:455
  310.6 45.5 %collective-permute-start.26 = (f32[4,4,2,32,128]{4,3,2,1,0:T(8,128)}, f32[4,4,2,32,128]{4,3,2,1,0:T(8,128)}, u32[]{:S(2)}, u32[]{:S(2)}) collective-permute-start(f32[4,4,2,32,128]{4,3,2,1,0:T(8,128)} %get-tuple-element.176.refs_6_), channel_id=1, source_target_pairs={{4,8},{5,9},{6,10},{7,11},{8,4},{9,5},{10,6},{11,7},{20,24},{21,25... | collective-permute-start | bytes 1572872 | tf_op jit(solution)/shard_map/ppermute | solution.py:455
  312.6 43.6 %collective-permute-start.27 = (f32[4,4,2,32,128]{4,3,2,1,0:T(8,128)}, f32[4,4,2,32,128]{4,3,2,1,0:T(8,128)}, u32[]{:S(2)}, u32[]{:S(2)}) collective-permute-start(f32[4,4,2,32,128]{4,3,2,1,0:T(8,128)} %get-tuple-element.182), channel_id=1, source_target_pairs={{4,12},{5,13},{6,14},{7,15},{8,0},{9,1},{10,2},{11,3},{20,28},{21,... | collective-permute-start | bytes 1572872 | tf_op jit(solution)/shard_map/ppermute | solution.py:455
  342.2 19.6 %collective-permute-start.25 = (f32[4,4,2,32,128]{4,3,2,1,0:T(8,128)S(1)}, f32[4,4,2,32,128]{4,3,2,1,0:T(8,128)S(1)}, u32[]{:S(2)}, u32[]{:S(2)}) collective-permute-start(f32[4,4,2,32,128]{4,3,2,1,0:T(8,128)S(1)} %get-tuple-element.179), channel_id=1, source_target_pairs={{0,4},{1,5},{2,6},{3,7},{8,12},{9,13},{10,14},{11,15},{4,0},{5,1},... | collective-permute-start | bytes 1572872 | tf_op jit(solution)/shard_map/ppermute | solution.py:455
  352.9 17.1 %collective-permute-start.20 = (f32[4,4,2,32,128]{4,3,2,1,0:T(8,128)S(1)}, f32[4,4,2,32,128]{4,3,2,1,0:T(8,128)S(1)}, u32[]{:S(2)}, u32[]{:S(2)}) collective-permute-start(f32[4,4,2,32,128]{4,3,2,1,0:T(8,128)S(1)} %get-tuple-element.171.refs_6_), channel_id=1, source_target_pairs={{4,8},{5,9},{6,10},{7,11},{8,4},{9,5},{10,6},{11,7},{20,24},{21,25... | collective-permute-start | bytes 1572872 | tf_op jit(solution)/shard_map/ppermute | solution.py:455
  354.8 23.6 %collective-permute-start.21 = (f32[4,4,2,32,128]{4,3,2,1,0:T(8,128)S(1)}, f32[4,4,2,32,128]{4,3,2,1,0:T(8,128)S(1)}, u32[]{:S(2)}, u32[]{:S(2)}) collective-permute-start(f32[4,4,2,32,128]{4,3,2,1,0:T(8,128)S(1)} %get-tuple-element.172), channel_id=1, source_target_pairs={{4,12},{5,13},{6,14},{7,15},{8,0},{9,1},{10,2},{11,3},{20,28},{21,... | collective-permute-start | bytes 1572872 | tf_op jit(solution)/shard_map/ppermute | solution.py:455
  361.8 26.1 %collective-permute-start.33 = (f32[4,4,2,32,128]{4,3,2,1,0:T(8,128)S(1)}, f32[4,4,2,32,128]{4,3,2,1,0:T(8,128)S(1)}, u32[]{:S(2)}, u32[]{:S(2)}) collective-permute-start(f32[4,4,2,32,128]{4,3,2,1,0:T(8,128)S(1)} %get-tuple-element.192), channel_id=1, source_target_pairs={{0,4},{1,5},{2,6},{3,7},{8,12},{9,13},{10,14},{11,15},{4,0},{5,1},... | collective-permute-start | bytes 1572872 | tf_op jit(solution)/shard_map/ppermute | solution.py:455
  364.7 29.3 %collective-permute-start.31 = (f32[4,4,2,32,128]{4,3,2,1,0:T(8,128)S(1)}, f32[4,4,2,32,128]{4,3,2,1,0:T(8,128)S(1)}, u32[]{:S(2)}, u32[]{:S(2)}) collective-permute-start(f32[4,4,2,32,128]{4,3,2,1,0:T(8,128)S(1)} %get-tuple-element.181.refs_6_), channel_id=1, source_target_pairs={{4,8},{5,9},{6,10},{7,11},{8,4},{9,5},{10,6},{11,7},{20,24},{21,25... | collective-permute-start | bytes 1572872 | tf_op jit(solution)/shard_map/ppermute | solution.py:455
  368.6 32.3 %collective-permute-start.32 = (f32[4,4,2,32,128]{4,3,2,1,0:T(8,128)S(1)}, f32[4,4,2,32,128]{4,3,2,1,0:T(8,128)S(1)}, u32[]{:S(2)}, u32[]{:S(2)}) collective-permute-start(f32[4,4,2,32,128]{4,3,2,1,0:T(8,128)S(1)} %get-tuple-element.191), channel_id=1, source_target_pairs={{4,12},{5,13},{6,14},{7,15},{8,0},{9,1},{10,2},{11,3},{20,28},{21,... | collective-permute-start | bytes 1572872 | tf_op jit(solution)/shard_map/ppermute | solution.py:455
  384.0 26.3 %collective-permute-start.28 = (f32[4,4,2,32,128]{4,3,2,1,0:T(8,128)S(1)}, f32[4,4,2,32,128]{4,3,2,1,0:T(8,128)S(1)}, u32[]{:S(2)}, u32[]{:S(2)}) collective-permute-start(f32[4,4,2,32,128]{4,3,2,1,0:T(8,128)S(1)} %get-tuple-element.187), channel_id=1, source_target_pairs={{0,4},{1,5},{2,6},{3,7},{8,12},{9,13},{10,14},{11,15},{4,0},{5,1},... | collective-permute-start | bytes 1572872 | tf_op jit(solution)/shard_map/ppermute | solution.py:455
  390.7 24.3 %collective-permute-start.35 = (f32[4,4,2,32,128]{4,3,2,1,0:T(8,128)S(1)}, f32[4,4,2,32,128]{4,3,2,1,0:T(8,128)S(1)}, u32[]{:S(2)}, u32[]{:S(2)}) collective-permute-start(f32[4,4,2,32,128]{4,3,2,1,0:T(8,128)S(1)} %get-tuple-element.194.refs_6_), channel_id=1, source_target_pairs={{4,8},{5,9},{6,10},{7,11},{8,4},{9,5},{10,6},{11,7},{20,24},{21,25... | collective-permute-start | bytes 1572872 | tf_op jit(solution)/shard_map/ppermute | solution.py:455
  392.7 30.8 %collective-permute-start.36 = (f32[4,4,2,32,128]{4,3,2,1,0:T(8,128)S(1)}, f32[4,4,2,32,128]{4,3,2,1,0:T(8,128)S(1)}, u32[]{:S(2)}, u32[]{:S(2)}) collective-permute-start(f32[4,4,2,32,128]{4,3,2,1,0:T(8,128)S(1)} %get-tuple-element.200), channel_id=1, source_target_pairs={{4,12},{5,13},{6,14},{7,15},{8,0},{9,1},{10,2},{11,3},{20,28},{21,... | collective-permute-start | bytes 1572872 | tf_op jit(solution)/shard_map/ppermute | solution.py:455
  406.4 27.9 %collective-permute-start.34 = (f32[4,4,2,32,128]{4,3,2,1,0:T(8,128)S(1)}, f32[4,4,2,32,128]{4,3,2,1,0:T(8,128)S(1)}, u32[]{:S(2)}, u32[]{:S(2)}) collective-permute-start(f32[4,4,2,32,128]{4,3,2,1,0:T(8,128)S(1)} %get-tuple-element.197), channel_id=1, source_target_pairs={{0,4},{1,5},{2,6},{3,7},{8,12},{9,13},{10,14},{11,15},{4,0},{5,1},... | collective-permute-start | bytes 1572872 | tf_op jit(solution)/shard_map/ppermute | solution.py:455
  413.1 41.9 %collective-permute-start.29 = (f32[4,4,2,32,128]{4,3,2,1,0:T(8,128)S(1)}, f32[4,4,2,32,128]{4,3,2,1,0:T(8,128)S(1)}, u32[]{:S(2)}, u32[]{:S(2)}) collective-permute-start(f32[4,4,2,32,128]{4,3,2,1,0:T(8,128)S(1)} %get-tuple-element.189.refs_6_), channel_id=1, source_target_pairs={{4,8},{5,9},{6,10},{7,11},{8,4},{9,5},{10,6},{11,7},{20,24},{21,25... | collective-permute-start | bytes 1572872 | tf_op jit(solution)/shard_map/ppermute | solution.py:455
  428.9 23.3 %collective-permute-start.39 = (f32[4,4,2,32,128]{4,3,2,1,0:T(8,128)S(1)}, f32[4,4,2,32,128]{4,3,2,1,0:T(8,128)S(1)}, u32[]{:S(2)}, u32[]{:S(2)}) collective-permute-start(f32[4,4,2,32,128]{4,3,2,1,0:T(8,128)S(1)} %get-tuple-element.207), channel_id=1, source_target_pairs={{0,4},{1,5},{2,6},{3,7},{8,12},{9,13},{10,14},{11,15},{4,0},{5,1},... | collective-permute-start | bytes 1572872 | tf_op jit(solution)/shard_map/ppermute | solution.py:455
  432.8 22.2 %collective-permute-start.30 = (f32[4,4,2,32,128]{4,3,2,1,0:T(8,128)S(1)}, f32[4,4,2,32,128]{4,3,2,1,0:T(8,128)S(1)}, u32[]{:S(2)}, u32[]{:S(2)}) collective-permute-start(f32[4,4,2,32,128]{4,3,2,1,0:T(8,128)S(1)} %get-tuple-element.190), channel_id=1, source_target_pairs={{4,12},{5,13},{6,14},{7,15},{8,0},{9,1},{10,2},{11,3},{20,28},{21,... | collective-permute-start | bytes 1572872 | tf_op jit(solution)/shard_map/ppermute | solution.py:455
  437.2 23.6 %collective-permute-start.37 = (f32[4,4,2,32,128]{4,3,2,1,0:T(8,128)S(1)}, f32[4,4,2,32,128]{4,3,2,1,0:T(8,128)S(1)}, u32[]{:S(2)}, u32[]{:S(2)}) collective-permute-start(f32[4,4,2,32,128]{4,3,2,1,0:T(8,128)S(1)} %get-tuple-element.199.refs_6_), channel_id=1, source_target_pairs={{4,8},{5,9},{6,10},{7,11},{8,4},{9,5},{10,6},{11,7},{20,24},{21,25... | collective-permute-start | bytes 1572872 | tf_op jit(solution)/shard_map/ppermute | solution.py:455
  441.0 26.0 %collective-permute-start.38 = (f32[4,4,2,32,128]{4,3,2,1,0:T(8,128)S(1)}, f32[4,4,2,32,128]{4,3,2,1,0:T(8,128)S(1)}, u32[]{:S(2)}, u32[]{:S(2)}) collective-permute-start(f32[4,4,2,32,128]{4,3,2,1,0:T(8,128)S(1)} %get-tuple-element.206), channel_id=1, source_target_pairs={{4,12},{5,13},{6,14},{7,15},{8,0},{9,1},{10,2},{11,3},{20,28},{21,... | collective-permute-start | bytes 1572872 | tf_op jit(solution)/shard_map/ppermute | solution.py:455
  474.2 105.8 %all-to-all-start.5 = ((f32[4,36,2,32,128]{4,3,2,1,0:T(8,128)}), f32[4,36,2,32,128]{4,3,2,1,0:T(8,128)}, u32[]{:S(2)}, u32[]{:S(2)}) async-start(f32[4,36,2,32,128]{4,3,2,1,0:T(8,128)} %gate.13), calls=%async_computation.5 | async-start | bytes 9437184 | tf_op jit(solution)/shard_map/all_to_all | solution.py:452
  479.2 16.7 %collective-permute-start.42 = (f32[4,4,2,32,128]{4,3,2,1,0:T(8,128)}, f32[4,4,2,32,128]{4,3,2,1,0:T(8,128)S(1)}, u32[]{:S(2)}, u32[]{:S(2)}) collective-permute-start(f32[4,4,2,32,128]{4,3,2,1,0:T(8,128)} %copy-done.59), channel_id=1, source_target_pairs={{0,4},{1,5},{2,6},{3,7},{8,12},{9,13},{10,14},{11,15},{4,0},{5,1},... | collective-permute-start | bytes 1572872 | tf_op jit(solution)/shard_map/ppermute | solution.py:455
  483.0 19.4 %collective-permute-start.40 = (f32[4,4,2,32,128]{4,3,2,1,0:T(8,128)S(1)}, f32[4,4,2,32,128]{4,3,2,1,0:T(8,128)S(1)}, u32[]{:S(2)}, u32[]{:S(2)}) collective-permute-start(f32[4,4,2,32,128]{4,3,2,1,0:T(8,128)S(1)} %copy-done.37), channel_id=1, source_target_pairs={{4,8},{5,9},{6,10},{7,11},{8,4},{9,5},{10,6},{11,7},{20,24},{21,25... | collective-permute-start | bytes 1572872 | tf_op jit(solution)/shard_map/ppermute | solution.py:455
  485.2 23.5 %collective-permute-start.41 = (f32[4,4,2,32,128]{4,3,2,1,0:T(8,128)S(1)}, f32[4,4,2,32,128]{4,3,2,1,0:T(8,128)S(1)}, u32[]{:S(2)}, u32[]{:S(2)}) collective-permute-start(f32[4,4,2,32,128]{4,3,2,1,0:T(8,128)S(1)} %copy-done.53), channel_id=1, source_target_pairs={{4,12},{5,13},{6,14},{7,15},{8,0},{9,1},{10,2},{11,3},{20,28},{21,... | collective-permute-start | bytes 1572872 | tf_op jit(solution)/shard_map/ppermute | solution.py:455
  486.5 30.9 %collective-permute-start.48 = (f32[4,4,2,32,128]{4,3,2,1,0:T(8,128)}, f32[4,4,2,32,128]{4,3,2,1,0:T(8,128)S(1)}, u32[]{:S(2)}, u32[]{:S(2)}) collective-permute-start(f32[4,4,2,32,128]{4,3,2,1,0:T(8,128)} %copy-done.54), channel_id=1, source_target_pairs={{0,4},{1,5},{2,6},{3,7},{8,12},{9,13},{10,14},{11,15},{4,0},{5,1},... | collective-permute-start | bytes 1572872 | tf_op jit(solution)/shard_map/ppermute | solution.py:455
  498.8 27.6 %collective-permute-start.46 = (f32[4,4,2,32,128]{4,3,2,1,0:T(8,128)S(1)}, f32[4,4,2,32,128]{4,3,2,1,0:T(8,128)S(1)}, u32[]{:S(2)}, u32[]{:S(2)}) collective-permute-start(f32[4,4,2,32,128]{4,3,2,1,0:T(8,128)S(1)} %get-tuple-element.215.refs_6_), channel_id=1, source_target_pairs={{4,8},{5,9},{6,10},{7,11},{8,4},{9,5},{10,6},{11,7},{20,24},{21,25... | collective-permute-start | bytes 1572872 | tf_op jit(solution)/shard_map/ppermute | solution.py:455
  501.0 30.3 %collective-permute-start.47 = (f32[4,4,2,32,128]{4,3,2,1,0:T(8,128)S(1)}, f32[4,4,2,32,128]{4,3,2,1,0:T(8,128)S(1)}, u32[]{:S(2)}, u32[]{:S(2)}) collective-permute-start(f32[4,4,2,32,128]{4,3,2,1,0:T(8,128)S(1)} %get-tuple-element.222), channel_id=1, source_target_pairs={{4,12},{5,13},{6,14},{7,15},{8,0},{9,1},{10,2},{11,3},{20,28},{21,... | collective-permute-start | bytes 1572872 | tf_op jit(solution)/shard_map/ppermute | solution.py:455
  514.1 23.7 %collective-permute-start.43 = (f32[4,4,2,32,128]{4,3,2,1,0:T(8,128)S(1)}, f32[4,4,2,32,128]{4,3,2,1,0:T(8,128)S(1)}, u32[]{:S(2)}, u32[]{:S(2)}) collective-permute-start(f32[4,4,2,32,128]{4,3,2,1,0:T(8,128)S(1)} %get-tuple-element.218), channel_id=1, source_target_pairs={{4,0},{5,1},{6,2},{7,3},{12,8},{13,9},{14,10},{15,11},{20,16},{21,... | collective-permute-start | bytes 1572872 | tf_op jit(solution)/shard_map/ppermute | solution.py:455
  520.3 25.7 %collective-permute-start.50 = (f32[4,4,2,32,128]{4,3,2,1,0:T(8,128)S(1)}, f32[4,4,2,32,128]{4,3,2,1,0:T(8,128)S(1)}, u32[]{:S(2)}, u32[]{:S(2)}) collective-permute-start(f32[4,4,2,32,128]{4,3,2,1,0:T(8,128)S(1)} %get-tuple-element.224.refs_6_), channel_id=1, source_target_pairs={{4,8},{5,9},{6,10},{7,11},{8,4},{9,5},{10,6},{11,7},{20,24},{21,25... | collective-permute-start | bytes 1572872 | tf_op jit(solution)/shard_map/ppermute | solution.py:455
  525.0 28.7 %collective-permute-start.51 = (f32[4,4,2,32,128]{4,3,2,1,0:T(8,128)S(1)}, f32[4,4,2,32,128]{4,3,2,1,0:T(8,128)S(1)}, u32[]{:S(2)}, u32[]{:S(2)}) collective-permute-start(f32[4,4,2,32,128]{4,3,2,1,0:T(8,128)S(1)} %get-tuple-element.230), channel_id=1, source_target_pairs={{4,12},{5,13},{6,14},{7,15},{8,0},{9,1},{10,2},{11,3},{20,28},{21,... | collective-permute-start | bytes 1572872 | tf_op jit(solution)/shard_map/ppermute | solution.py:455
  536.6 23.4 %collective-permute-start.49 = (f32[4,4,2,32,128]{4,3,2,1,0:T(8,128)S(1)}, f32[4,4,2,32,128]{4,3,2,1,0:T(8,128)S(1)}, u32[]{:S(2)}, u32[]{:S(2)}) collective-permute-start(f32[4,4,2,32,128]{4,3,2,1,0:T(8,128)S(1)} %get-tuple-element.227), channel_id=1, source_target_pairs={{4,0},{5,1},{6,2},{7,3},{12,8},{13,9},{14,10},{15,11},{20,16},{21,... | collective-permute-start | bytes 1572872 | tf_op jit(solution)/shard_map/ppermute | solution.py:455
  539.2 25.8 %collective-permute-start.44 = (f32[4,4,2,32,128]{4,3,2,1,0:T(8,128)S(1)}, f32[4,4,2,32,128]{4,3,2,1,0:T(8,128)S(1)}, u32[]{:S(2)}, u32[]{:S(2)}) collective-permute-start(f32[4,4,2,32,128]{4,3,2,1,0:T(8,128)S(1)} %get-tuple-element.220.refs_6_), channel_id=1, source_target_pairs={{8,4},{9,5},{10,6},{11,7},{24,20},{25,21},{26,22},{27,23}} | collective-permute-start | bytes 1572872 | tf_op jit(solution)/shard_map/ppermute | solution.py:455
  544.7 30.7 %collective-permute-start.45 = (f32[4,4,2,32,128]{4,3,2,1,0:T(8,128)S(1)}, f32[4,4,2,32,128]{4,3,2,1,0:T(8,128)S(1)}, u32[]{:S(2)}, u32[]{:S(2)}) collective-permute-start(f32[4,4,2,32,128]{4,3,2,1,0:T(8,128)S(1)} %get-tuple-element.221), channel_id=1, source_target_pairs={{8,0},{9,1},{10,2},{11,3},{24,16},{25,17},{26,18},{27,19}} | collective-permute-start | bytes 1572872 | tf_op jit(solution)/shard_map/ppermute | solution.py:455
  580.0 60.2 %all-to-all-start.6 = ((f32[4,20,2,32,128]{4,3,2,1,0:T(8,128)}), f32[4,20,2,32,128]{4,3,2,1,0:T(8,128)}, u32[]{:S(2)}, u32[]{:S(2)}) async-start(f32[4,20,2,32,128]{4,3,2,1,0:T(8,128)} %gate.14), calls=%async_computation.6 | async-start | bytes 5242880 | tf_op jit(solution)/shard_map/all_to_all | solution.py:452
  584.7 16.4 %collective-permute-start.53 = (f32[4,4,2,32,128]{4,3,2,1,0:T(8,128)}, f32[4,4,2,32,128]{4,3,2,1,0:T(8,128)S(1)}, u32[]{:S(2)}, u32[]{:S(2)}) collective-permute-start(f32[4,4,2,32,128]{4,3,2,1,0:T(8,128)} %copy-done.57), channel_id=1, source_target_pairs={{4,0},{5,1},{6,2},{7,3},{12,8},{13,9},{14,10},{15,11},{20,16},{21,... | collective-permute-start | bytes 1572872 | tf_op jit(solution)/shard_map/ppermute | solution.py:455
  586.0 33.8 %collective-permute-start.58 = (f32[4,4,2,32,128]{4,3,2,1,0:T(8,128)S(1)}, f32[4,4,2,32,128]{4,3,2,1,0:T(8,128)S(1)}, u32[]{:S(2)}, u32[]{:S(2)}) collective-permute-start(f32[4,4,2,32,128]{4,3,2,1,0:T(8,128)S(1)} %get-tuple-element.229.refs_6_), channel_id=1, source_target_pairs={{8,4},{9,5},{10,6},{11,7},{24,20},{25,21},{26,22},{27,23}} | collective-permute-start | bytes 1572872 | tf_op jit(solution)/shard_map/ppermute | solution.py:455
  592.5 27.3 %collective-permute-start.59 = (f32[4,4,2,32,128]{4,3,2,1,0:T(8,128)S(1)}, f32[4,4,2,32,128]{4,3,2,1,0:T(8,128)S(1)}, u32[]{:S(2)}, u32[]{:S(2)}) collective-permute-start(f32[4,4,2,32,128]{4,3,2,1,0:T(8,128)S(1)} %copy-done.49), channel_id=1, source_target_pairs={{8,0},{9,1},{10,2},{11,3},{24,16},{25,17},{26,18},{27,19}} | collective-permute-start | bytes 1572872 | tf_op jit(solution)/shard_map/ppermute | solution.py:455
  602.4 24.8 %collective-permute-start.54 = (f32[4,4,2,32,128]{4,3,2,1,0:T(8,128)S(1)}, f32[4,4,2,32,128]{4,3,2,1,0:T(8,128)S(1)}, u32[]{:S(2)}, u32[]{:S(2)}) collective-permute-start(f32[4,4,2,32,128]{4,3,2,1,0:T(8,128)S(1)} %get-tuple-element.239.refs_6_), channel_id=1, source_target_pairs={{8,4},{9,5},{10,6},{11,7},{24,20},{25,21},{26,22},{27,23}} | collective-permute-start | bytes 1572872 | tf_op jit(solution)/shard_map/ppermute | solution.py:455
  604.8 33.0 %collective-permute-start.55 = (f32[4,4,2,32,128]{4,3,2,1,0:T(8,128)S(1)}, f32[4,4,2,32,128]{4,3,2,1,0:T(8,128)S(1)}, u32[]{:S(2)}, u32[]{:S(2)}) collective-permute-start(f32[4,4,2,32,128]{4,3,2,1,0:T(8,128)S(1)} %get-tuple-element.240), channel_id=1, source_target_pairs={{8,0},{9,1},{10,2},{11,3},{24,16},{25,17},{26,18},{27,19}} | collective-permute-start | bytes 1572872 | tf_op jit(solution)/shard_map/ppermute | solution.py:455
  640.2 23.2 %all-to-all-start.7 = ((f32[4,8,2,32,128]{4,3,2,1,0:T(8,128)}), f32[4,8,2,32,128]{4,3,2,1,0:T(8,128)S(1)}, u32[]{:S(2)}, u32[]{:S(2)}) async-start(f32[4,8,2,32,128]{4,3,2,1,0:T(8,128)} %gate.15), calls=%async_computation.7 | async-start | bytes 2097152 | tf_op jit(solution)/shard_map/all_to_all | solution.py:452
  (66 other events, 537.4 us)

commit v5 on v4

--- a/solution.py
+++ b/solution.py
@@ -468,11 +468,11 @@
     def sums_over_slab(values):
         if devices & (devices - 1):
             yield lax.psum(values, "slab")
-        step = 1
-        while step < devices and not devices & (devices - 1):
-            values = values + lax.ppermute(values, "slab", [(q, q ^ step) for q in range(devices)])
-            yield values
-            step *= 2
+        else:
+            steps = [1 << bit for bit in range(devices.bit_length() - 1)]
+            for step in steps[1:] + steps[:1]:
+                values = values + lax.ppermute(values, "slab", [(q, q ^ step) for q in range(devices)])
+                yield values
 
     def part_of(kind, c):
         i = next(i for i, (low, high) in enumerate(spans[kind]) if low <= c * chunk < high)

time: 683 us -> 681 us (level)
    ppermute x57, waiting for transfers between devices: 180 us -> 161 us  [move(): lax.ppermute(values, 'slab', [(a * peers + q, b * peers + q) for a, b in...]
    ppermute x4, waiting for transfers between devices: 12.3 us -> 29.2 us  [sums_over_slab(): lax.ppermute(values, 'slab', [(q, q ^ step) for q in range(devices)])]
  transfers between devices with their start and end apart: 69 -> 69, of which waited for: 33 -> 31; matrix products, arithmetic and copies ran while one was open for 0% -> 0% of each run, Pallas kernels for 25% -> 25%
where the time goes in v5:
time: 681 us; the launch traced here: 672 us
  waiting for transfers between devices  267 us (39%)
  Pallas kernels  192 us (28%)
  starting transfers between devices  175 us (26%)
  local copies, waits for them, and re-layouts  33.6 us (5%)
    ppermute x57, waiting for transfers between devices, move(): lax.ppermute(values, 'slab', [(a * peers + q, b * peers + q) for a, b in...  161 us
    ppermute x57, starting transfers between devices, move(): lax.ppermute(values, 'slab', [(a * peers + q, b * peers + q) for a, b in...  132 us
    pallas_call x19, Pallas kernels, cells(): pl.pallas_call(kernel, grid=(rows,), in_specs=specs, out_specs=out_specs,...  86.9 us
    all_to_all x8, waiting for transfers between devices, exchange(): lax.all_to_all(values, 'slab', 0, 0, tiled=True, axis_index_groups=in_layer)  76.8 us
    pallas_call x19, Pallas kernels, cross_terms(): pl.pallas_call(kernel, grid=(rows,), in_specs=specs, out_specs=[rows_of(s...  45.9 us
    all_to_all x8, starting transfers between devices, exchange(): lax.all_to_all(values, 'slab', 0, 0, tiled=True, axis_index_groups=in_layer)  37.9 us
    unnamed x122, local copies, waits for them, and re-layouts  30.4 us
    ppermute x4, waiting for transfers between devices, sums_over_slab(): lax.ppermute(values, 'slab', [(q, q ^ step) for q in range(devices)])  29.2 us
  transfers between devices with their start and end apart: 69, of which 31 were waited for; matrix products, arithmetic and copies ran while one was open for 0% of the time, Pallas kernels for 25%

profile of v5, /device:TPU:18, one launch (start us, length us, event | category | flops | bytes accessed | tf_op | source)
XLA Modules:
  0.0 672.2 jit_solution(17534937278635454112)
XLA Ops:
  0.6 3.8 packed.3._
  4.5 4.4 all-to-all-start
  9.1 12.5 %field.1 = (f32[32,2,32,128]{3,2,1,0:T(8,128)S(1)}, f32[224,2,32,128]{3,2,1,0:T(8,128)}, f32[8,256]{1,0:T(8,128)S(1)}) custom-call(f32[32,256,256]{2,1,0:T(8,128)} %w.3, bf16[256,256]{1,0:T(8,128)(2,1)S(1)} %get-tuple-element.122.north_high, bf16[256,256]{1,0:T(8,128)(2,1)S(1)} %get-tuple-element.123.north_low, ...), custom_call_target="tpu_custom_call" | custom-call | flops 1 | bytes 1 | tf_op jit(solution)/shard_map/field/pallas_call | solution.py:154
  22.6 12.1 %all-to-all-done.__1_.refs_10_ = f32[4,2,2,32,8,128]{5,4,3,2,1,0:T(8,128)} async-done(((f32[4,2,2,32,8,128]{5,4,3,2,1,0:T(8,128)}), f32[4,2,2,32,8,128]{5,4,3,2,1,0:T(8,128)}, u32[]{:S(2)}, u32[]{:S(2)}) %all-to-all-start) | async-done | bytes 2097184 | tf_op jit(solution)/shard_map/all_to_all | solution.py:452
  39.5 4.9 packed.4.__1_.__0_
  55.7 5.6 all-to-all-start.2
  66.2 10.9 %collective-permute-done.3.rest_0_.refs_5_ = f32[4,4,2,32,128]{4,3,2,1,0:T(8,128)S(1)} collective-permute-done((f32[4,4,2,32,128]{4,3,2,1,0:T(8,128)S(1)}, f32[4,4,2,32,128]{4,3,2,1,0:T(8,128)S(1)}, u32[]{:S(2)}, u32[]{:S(2)}) %collective-permute-start.3) | collective-permute-done | bytes 524320 | tf_op jit(solution)/shard_map/ppermute | solution.py:455
  79.4 14.7 %packed.5.rest_3_.__0_ = f32[4,2,2,32,40,128]{5,4,3,2,1,0:T(8,128)} custom-call(s32[32,256,256]{2,1,0:T(8,128)} %c.5, s32[32,256,256]{2,1,0:T(8,128)} %e.5, f32[4,4,2,32,128]{4,3,2,1,0:T(8,128)S(1)} %get-tuple-element.138.rest_0_), custom_call_target="tpu_custom_call" | custom-call | flops 1 | bytes 1 | tf_op jit(solution)/shard_map/packed/pallas_call | solution.py:180
  96.5 46.8 %all-to-all-done.2.rest_1_.refs_12_.__1_.refs_9_ = f32[4,56,2,32,128]{4,3,2,1,0:T(8,128)} async-done(((f32[4,56,2,32,128]{4,3,2,1,0:T(8,128)}), f32[4,56,2,32,128]{4,3,2,1,0:T(8,128)}, u32[]{:S(2)}, u32[]{:S(2)}) %all-to-all-start.2) | async-done | bytes 7340064 | tf_op jit(solution)/shard_map/all_to_all | solution.py:452
  149.3 4.8 all-to-all-start.3
  160.9 10.1 %collective-permute-done.rest_0_.refs_5_ = f32[4,4,2,32,128]{4,3,2,1,0:T(8,128)S(1)} collective-permute-done((f32[4,4,2,32,128]{4,3,2,1,0:T(8,128)S(1)}, f32[4,4,2,32,128]{4,3,2,1,0:T(8,128)S(1)}, u32[]{:S(2)}, u32[]{:S(2)}) %collective-permute-start) | collective-permute-done | bytes 524320 | tf_op jit(solution)/shard_map/ppermute | solution.py:455
  175.3 17.8 %collective-permute-done.7.rest_0_.refs_5_ = f32[4,4,2,32,128]{4,3,2,1,0:T(8,128)S(1)} collective-permute-done((f32[4,4,2,32,128]{4,3,2,1,0:T(8,128)}, f32[4,4,2,32,128]{4,3,2,1,0:T(8,128)S(1)}, u32[]{:S(2)}, u32[]{:S(2)}) %collective-permute-start.7) | collective-permute-done | bytes 524320 | tf_op jit(solution)/shard_map/ppermute | solution.py:455
  196.8 3.9 cells.20
  207.4 3.9 cells.21
  212.9 6.1 all-to-all-start.4
  219.0 7.8 %collective-permute-start.15 = (f32[4,4,2,32,128]{4,3,2,1,0:T(8,128)}, f32[4,4,2,32,128]{4,3,2,1,0:T(8,128)S(1)}, u32[]{:S(2)}, u32[]{:S(2)}) collective-permute-start(f32[4,4,2,32,128]{4,3,2,1,0:T(8,128)} %copy-done.58), channel_id=1, source_target_pairs={{0,4},{1,5},{2,6},{3,7},{8,12},{9,13},{10,14},{11,15},{4,0},{5,1},... | collective-permute-start | bytes 1572872 | tf_op jit(solution)/shard_map/ppermute | solution.py:455
  230.2 9.6 %collective-permute-done.15.rest_0_.refs_5_ = f32[4,4,2,32,128]{4,3,2,1,0:T(8,128)S(1)} collective-permute-done((f32[4,4,2,32,128]{4,3,2,1,0:T(8,128)}, f32[4,4,2,32,128]{4,3,2,1,0:T(8,128)S(1)}, u32[]{:S(2)}, u32[]{:S(2)}) %collective-permute-start.15) | collective-permute-done | bytes 524320 | tf_op jit(solution)/shard_map/ppermute | solution.py:455
  246.0 6.3 collective-permute-done.14.refs_4_
  252.3 5.5 cells.22
  257.8 3.9 collective-permute-start.16
  268.0 6.8 %collective-permute-done.18.refs_4_ = f32[4,4,2,32,128]{4,3,2,1,0:T(8,128)S(1)} collective-permute-done((f32[4,4,2,32,128]{4,3,2,1,0:T(8,128)S(1)}, f32[4,4,2,32,128]{4,3,2,1,0:T(8,128)S(1)}, u32[]{:S(2)}, u32[]{:S(2)}) %collective-permute-start.18) | collective-permute-done | bytes 524320 | tf_op jit(solution)/shard_map/ppermute | solution.py:455
  274.8 5.5 cells.23
  280.2 3.9 collective-permute-start.24
  291.1 6.2 collective-permute-done.12.refs_4_
  297.3 5.5 cells.24
  302.8 3.9 collective-permute-start.19
  306.8 3.8 cross_terms.27
  316.0 3.8 collective-permute-done.23.refs_4_
  320.6 14.0 %all-to-all-done.4.refs_10_.__1_ = f32[4,2,2,32,40,128]{5,4,3,2,1,0:T(8,128)} async-done(((f32[4,2,2,32,40,128]{5,4,3,2,1,0:T(8,128)}), f32[4,2,2,32,40,128]{5,4,3,2,1,0:T(8,128)}, u32[]{:S(2)}, u32[]{:S(2)}) %all-to-all-start.4) | async-done | bytes 10485792 | tf_op jit(solution)/shard_map/all_to_all | solution.py:452
  336.8 5.5 cells.25
  342.2 7.7 %collective-permute-start.25 = (f32[4,4,2,32,128]{4,3,2,1,0:T(8,128)S(1)}, f32[4,4,2,32,128]{4,3,2,1,0:T(8,128)S(1)}, u32[]{:S(2)}, u32[]{:S(2)}) collective-permute-start(f32[4,4,2,32,128]{4,3,2,1,0:T(8,128)S(1)} %get-tuple-element.179), channel_id=1, source_target_pairs={{0,4},{1,5},{2,6},{3,7},{8,12},{9,13},{10,14},{11,15},{4,0},{5,1},... | collective-permute-start | bytes 1572872 | tf_op jit(solution)/shard_map/ppermute | solution.py:455
  356.1 5.7 cells.26
  364.7 3.9 collective-permute-start.31
  370.0 8.5 %collective-permute-done.21.refs_4_ = f32[4,4,2,32,128]{4,3,2,1,0:T(8,128)S(1)} collective-permute-done((f32[4,4,2,32,128]{4,3,2,1,0:T(8,128)S(1)}, f32[4,4,2,32,128]{4,3,2,1,0:T(8,128)S(1)}, u32[]{:S(2)}, u32[]{:S(2)}) %collective-permute-start.21) | collective-permute-done | bytes 524320 | tf_op jit(solution)/shard_map/ppermute | solution.py:455
  378.4 5.6 cells.27
  384.0 3.9 collective-permute-start.28
  394.0 6.9 %collective-permute-done.32.refs_4_ = f32[4,4,2,32,128]{4,3,2,1,0:T(8,128)S(1)} collective-permute-done((f32[4,4,2,32,128]{4,3,2,1,0:T(8,128)S(1)}, f32[4,4,2,32,128]{4,3,2,1,0:T(8,128)S(1)}, u32[]{:S(2)}, u32[]{:S(2)}) %collective-permute-start.32) | collective-permute-done | bytes 524320 | tf_op jit(solution)/shard_map/ppermute | solution.py:455
  400.9 5.5 cells.28
  406.4 3.9 collective-permute-start.34
  415.1 8.4 %collective-permute-done.36.refs_4_ = f32[4,4,2,32,128]{4,3,2,1,0:T(8,128)S(1)} collective-permute-done((f32[4,4,2,32,128]{4,3,2,1,0:T(8,128)S(1)}, f32[4,4,2,32,128]{4,3,2,1,0:T(8,128)S(1)}, u32[]{:S(2)}, u32[]{:S(2)}) %collective-permute-start.36) | collective-permute-done | bytes 524320 | tf_op jit(solution)/shard_map/ppermute | solution.py:455
  423.4 5.5 cells.29
  428.9 3.9 collective-permute-start.39
  437.2 3.8 collective-permute-start.37
  442.3 9.8 %collective-permute-done.39.rest_0_.refs_5_ = f32[4,4,2,32,128]{4,3,2,1,0:T(8,128)S(1)} collective-permute-done((f32[4,4,2,32,128]{4,3,2,1,0:T(8,128)S(1)}, f32[4,4,2,32,128]{4,3,2,1,0:T(8,128)S(1)}, u32[]{:S(2)}, u32[]{:S(2)}) %collective-permute-start.39) | collective-permute-done | bytes 524320 | tf_op jit(solution)/shard_map/ppermute | solution.py:455
  455.0 5.7 cells.30
  460.8 6.3 collective-permute-done.38.refs_4_
  467.1 5.5 cells.31
  474.2 5.1 all-to-all-start.5
  486.6 9.3 %collective-permute-done.42.rest_0_.refs_5_ = f32[4,4,2,32,128]{4,3,2,1,0:T(8,128)S(1)} collective-permute-done((f32[4,4,2,32,128]{4,3,2,1,0:T(8,128)}, f32[4,4,2,32,128]{4,3,2,1,0:T(8,128)S(1)}, u32[]{:S(2)}, u32[]{:S(2)}) %collective-permute-start.42) | collective-permute-done | bytes 524320 | tf_op jit(solution)/shard_map/ppermute | solution.py:455
  502.3 6.4 collective-permute-done.41.refs_4_
  508.8 5.4 cells.32
  520.3 4.7 collective-permute-start.50
  526.4 4.9 collective-permute-done.47.refs_4_
  531.3 5.3 cells.33
  539.2 5.5 collective-permute-start.44
  546.0 7.7 %collective-permute-done.51.refs_4_ = f32[4,4,2,32,128]{4,3,2,1,0:T(8,128)S(1)} collective-permute-done((f32[4,4,2,32,128]{4,3,2,1,0:T(8,128)S(1)}, f32[4,4,2,32,128]{4,3,2,1,0:T(8,128)S(1)}, u32[]{:S(2)}, u32[]{:S(2)}) %collective-permute-start.51) | collective-permute-done | bytes 524320 | tf_op jit(solution)/shard_map/ppermute | solution.py:455
  553.8 5.3 cells.34
  565.0 10.4 %collective-permute-done.45.refs_4_ = f32[4,4,2,32,128]{4,3,2,1,0:T(8,128)S(1)} collective-permute-done((f32[4,4,2,32,128]{4,3,2,1,0:T(8,128)S(1)}, f32[4,4,2,32,128]{4,3,2,1,0:T(8,128)S(1)}, u32[]{:S(2)}, u32[]{:S(2)}) %collective-permute-start.45) | collective-permute-done | bytes 524320 | tf_op jit(solution)/shard_map/ppermute | solution.py:455
  580.0 4.7 all-to-all-start.6
  586.0 6.5 collective-permute-start.58
  593.9 7.2 %collective-permute-done.53.rest_0_.refs_5_ = f32[4,4,2,32,128]{4,3,2,1,0:T(8,128)S(1)} collective-permute-done((f32[4,4,2,32,128]{4,3,2,1,0:T(8,128)}, f32[4,4,2,32,128]{4,3,2,1,0:T(8,128)S(1)}, u32[]{:S(2)}, u32[]{:S(2)}) %collective-permute-start.53) | collective-permute-done | bytes 524320 | tf_op jit(solution)/shard_map/ppermute | solution.py:455
  613.5 24.5 %collective-permute-done.57 = f32[8,256]{1,0:T(8,128)S(1)} collective-permute-done((f32[8,256]{1,0:T(8,128)S(1)}, f32[8,256]{1,0:T(8,128)S(1)}, u32[]{:S(2)}, u32[]{:S(2)}) %collective-permute-start.57) | collective-permute-done | bytes 8224 | tf_op jit(solution)/shard_map/ppermute | solution.py:474
  648.0 13.4 %finish.2.w = f32[32,256,256]{2,1,0:T(8,128)} custom-call(f32[32,256,256]{2,1,0:T(8,128)} %w.3, bf16[256,224]{1,0:T(8,128)(2,1)S(1)} %get-tuple-element.127.north_high, bf16[256,224]{1,0:T(8,128)(2,1)S(1)} %copy-done.43, bf16[256,256]{1,0:T(8,128)(2,1)S(1)} %get-tuple-element.129.time_high, bf16[256,256]{1,0:T(8,128)(2,1)S(1)} %get-tuple-element.130.time_low, ...), custom_call_target="tpu_custom_call" | custom-call | flops 1 | bytes 1 | tf_op jit(solution)/shard_map/finish/pallas_call | solution.py:420
  661.4 9.6 %finish.3 = f32[32,256,256]{2,1,0:T(8,128)} custom-call(f32[32,256,256]{2,1,0:T(8,128)} %finish.2.w, bf16[256,32]{1,0:T(8,128)(2,1)S(1)} %get-tuple-element.236.north_high, bf16[256,32]{1,0:T(8,128)(2,1)S(1)} %copy-done.45, bf16[256,256]{1,0:T(8,128)(2,1)S(1)} %get-tuple-element.129.time_high, bf16[256,256]{1,0:T(8,128)(2,1)S(1)} %get-tuple-element.130.time_low, ...), custom_call_target="tpu_custom_call" | custom-call | flops 1 | bytes 1 | tf_op jit(solution)/shard_map/finish/pallas_call | solution.py:420
  (257 shorter events, 177.5 us)
Async XLA Ops:
  4.5 30.2 %all-to-all-start = ((f32[4,2,2,32,8,128]{5,4,3,2,1,0:T(8,128)}), f32[4,2,2,32,8,128]{5,4,3,2,1,0:T(8,128)}, u32[]{:S(2)}, u32[]{:S(2)}) async-start(f32[4,2,2,32,8,128]{5,4,3,2,1,0:T(8,128)} %packed.3._), calls=%async_computation | async-start | bytes 4194304 | tf_op jit(solution)/shard_map/all_to_all | solution.py:452
  34.7 18.0 %all-to-all-start.1 = ((f32[4,8,2,32,128]{4,3,2,1,0:T(8,128)}), f32[4,8,2,32,128]{4,3,2,1,0:T(8,128)S(1)}, u32[]{:S(2)}, u32[]{:S(2)}) async-start(f32[4,8,2,32,128]{4,3,2,1,0:T(8,128)} %gate.8._.rest_0_), calls=%async_computation.1 | async-start | bytes 2097152 | tf_op jit(solution)/shard_map/all_to_all | solution.py:452
  55.7 87.6 %all-to-all-start.2 = ((f32[4,56,2,32,128]{4,3,2,1,0:T(8,128)}), f32[4,56,2,32,128]{4,3,2,1,0:T(8,128)}, u32[]{:S(2)}, u32[]{:S(2)}) async-start(f32[4,56,2,32,128]{4,3,2,1,0:T(8,128)} %gate.10), calls=%async_computation.2 | async-start | bytes 14680064 | tf_op jit(solution)/shard_map/all_to_all | solution.py:452
  64.9 29.2 %collective-permute-start.6 = (f32[4,4,2,32,128]{4,3,2,1,0:T(8,128)}, f32[4,4,2,32,128]{4,3,2,1,0:T(8,128)S(1)}, u32[]{:S(2)}, u32[]{:S(2)}) collective-permute-start(f32[4,4,2,32,128]{4,3,2,1,0:T(8,128)} %get-tuple-element.243.__2_), channel_id=1, source_target_pairs={{0,4},{1,5},{2,6},{3,7},{8,12},{9,13},{10,14},{11,15},{16,20},{17,... | collective-permute-start | bytes 1572872 | tf_op jit(solution)/shard_map/ppermute | solution.py:455
  77.4 16.8 %collective-permute-start.4 = (f32[4,4,2,32,128]{4,3,2,1,0:T(8,128)S(1)}, f32[4,4,2,32,128]{4,3,2,1,0:T(8,128)S(1)}, u32[]{:S(2)}, u32[]{:S(2)}) collective-permute-start(f32[4,4,2,32,128]{4,3,2,1,0:T(8,128)S(1)} %get-tuple-element.138.rest_0_), channel_id=1, source_target_pairs={{4,8},{5,9},{6,10},{7,11},{20,24},{21,25},{22,26},{23,27}} | collective-permute-start | bytes 1572872 | tf_op jit(solution)/shard_map/ppermute | solution.py:455
  78.7 17.8 %collective-permute-start.5 = (f32[4,4,2,32,128]{4,3,2,1,0:T(8,128)S(1)}, f32[4,4,2,32,128]{4,3,2,1,0:T(8,128)S(1)}, u32[]{:S(2)}, u32[]{:S(2)}) collective-permute-start(f32[4,4,2,32,128]{4,3,2,1,0:T(8,128)S(1)} %get-tuple-element.139), channel_id=1, source_target_pairs={{4,12},{5,13},{6,14},{7,15},{20,28},{21,29},{22,30},{23,31}} | collective-permute-start | bytes 1572872 | tf_op jit(solution)/shard_map/ppermute | solution.py:455
  149.3 53.9 %all-to-all-start.3 = ((f32[4,2,2,32,16,128]{5,4,3,2,1,0:T(8,128)}), f32[4,2,2,32,16,128]{5,4,3,2,1,0:T(8,128)}, u32[]{:S(2)}, u32[]{:S(2)}) async-start(f32[4,2,2,32,16,128]{5,4,3,2,1,0:T(8,128)} %gate.11), calls=%async_computation.3 | async-start | bytes 8388608 | tf_op jit(solution)/shard_map/all_to_all | solution.py:452
  158.8 37.9 %collective-permute-start.8 = (f32[4,4,2,32,128]{4,3,2,1,0:T(8,128)}, f32[4,4,2,32,128]{4,3,2,1,0:T(8,128)S(1)}, u32[]{:S(2)}, u32[]{:S(2)}) collective-permute-start(f32[4,4,2,32,128]{4,3,2,1,0:T(8,128)} %get-tuple-element.140.refs_6_), channel_id=1, source_target_pairs={{4,8},{5,9},{6,10},{7,11},{20,24},{21,25},{22,26},{23,27}} | collective-permute-start | bytes 1572872 | tf_op jit(solution)/shard_map/ppermute | solution.py:455
  160.1 33.0 %collective-permute-start.7 = (f32[4,4,2,32,128]{4,3,2,1,0:T(8,128)}, f32[4,4,2,32,128]{4,3,2,1,0:T(8,128)S(1)}, u32[]{:S(2)}, u32[]{:S(2)}) collective-permute-start(f32[4,4,2,32,128]{4,3,2,1,0:T(8,128)} %copy-done.60), channel_id=1, source_target_pairs={{0,4},{1,5},{2,6},{3,7},{8,12},{9,13},{10,14},{11,15},{4,0},{5,1},... | collective-permute-start | bytes 1572872 | tf_op jit(solution)/shard_map/ppermute | solution.py:455
  160.2 36.6 %collective-permute-start.9 = (f32[4,4,2,32,128]{4,3,2,1,0:T(8,128)}, f32[4,4,2,32,128]{4,3,2,1,0:T(8,128)S(1)}, u32[]{:S(2)}, u32[]{:S(2)}) collective-permute-start(f32[4,4,2,32,128]{4,3,2,1,0:T(8,128)} %copy-done.55), channel_id=1, source_target_pairs={{4,12},{5,13},{6,14},{7,15},{20,28},{21,29},{22,30},{23,31}} | collective-permute-start | bytes 1572872 | tf_op jit(solution)/shard_map/ppermute | solution.py:455
  173.2 28.4 %collective-permute-start.1 = (f32[4,4,2,32,128]{4,3,2,1,0:T(8,128)S(1)}, f32[4,4,2,32,128]{4,3,2,1,0:T(8,128)S(1)}, u32[]{:S(2)}, u32[]{:S(2)}) collective-permute-start(f32[4,4,2,32,128]{4,3,2,1,0:T(8,128)S(1)} %get-tuple-element.136.refs_6_), channel_id=1, source_target_pairs={{4,8},{5,9},{6,10},{7,11},{20,24},{21,25},{22,26},{23,27}} | collective-permute-start | bytes 1572872 | tf_op jit(solution)/shard_map/ppermute | solution.py:455
  174.6 27.8 %collective-permute-start.2 = (f32[4,4,2,32,128]{4,3,2,1,0:T(8,128)S(1)}, f32[4,4,2,32,128]{4,3,2,1,0:T(8,128)S(1)}, u32[]{:S(2)}, u32[]{:S(2)}) collective-permute-start(f32[4,4,2,32,128]{4,3,2,1,0:T(8,128)S(1)} %get-tuple-element.137), channel_id=1, source_target_pairs={{4,12},{5,13},{6,14},{7,15},{20,28},{21,29},{22,30},{23,31}} | collective-permute-start | bytes 1572872 | tf_op jit(solution)/shard_map/ppermute | solution.py:455
  212.9 121.8 %all-to-all-start.4 = ((f32[4,2,2,32,40,128]{5,4,3,2,1,0:T(8,128)}), f32[4,2,2,32,40,128]{5,4,3,2,1,0:T(8,128)}, u32[]{:S(2)}, u32[]{:S(2)}) async-start(f32[4,2,2,32,40,128]{5,4,3,2,1,0:T(8,128)} %gate.12), calls=%async_computation.4 | async-start | bytes 20971520 | tf_op jit(solution)/shard_map/all_to_all | solution.py:452
  219.0 20.8 %collective-permute-start.15 = (f32[4,4,2,32,128]{4,3,2,1,0:T(8,128)}, f32[4,4,2,32,128]{4,3,2,1,0:T(8,128)S(1)}, u32[]{:S(2)}, u32[]{:S(2)}) collective-permute-start(f32[4,4,2,32,128]{4,3,2,1,0:T(8,128)} %copy-done.58), channel_id=1, source_target_pairs={{0,4},{1,5},{2,6},{3,7},{8,12},{9,13},{10,14},{11,15},{4,0},{5,1},... | collective-permute-start | bytes 1572872 | tf_op jit(solution)/shard_map/ppermute | solution.py:455
  226.8 19.1 %collective-permute-start.13 = (f32[4,4,2,32,128]{4,3,2,1,0:T(8,128)S(1)}, f32[4,4,2,32,128]{4,3,2,1,0:T(8,128)S(1)}, u32[]{:S(2)}, u32[]{:S(2)}) collective-permute-start(f32[4,4,2,32,128]{4,3,2,1,0:T(8,128)S(1)} %copy-done.35), channel_id=1, source_target_pairs={{4,8},{5,9},{6,10},{7,11},{8,4},{9,5},{10,6},{11,7},{20,24},{21,25... | collective-permute-start | bytes 1572872 | tf_op jit(solution)/shard_map/ppermute | solution.py:455
  228.8 23.5 %collective-permute-start.14 = (f32[4,4,2,32,128]{4,3,2,1,0:T(8,128)S(1)}, f32[4,4,2,32,128]{4,3,2,1,0:T(8,128)S(1)}, u32[]{:S(2)}, u32[]{:S(2)}) collective-permute-start(f32[4,4,2,32,128]{4,3,2,1,0:T(8,128)S(1)} %copy-done.51), channel_id=1, source_target_pairs={{4,12},{5,13},{6,14},{7,15},{8,0},{9,1},{10,2},{11,3},{20,28},{21,... | collective-permute-start | bytes 1572872 | tf_op jit(solution)/shard_map/ppermute | solution.py:455
  230.1 31.8 %collective-permute-start.10 = (f32[4,4,2,32,128]{4,3,2,1,0:T(8,128)}, f32[4,4,2,32,128]{4,3,2,1,0:T(8,128)S(1)}, u32[]{:S(2)}, u32[]{:S(2)}) collective-permute-start(f32[4,4,2,32,128]{4,3,2,1,0:T(8,128)} %copy-done.56), channel_id=1, source_target_pairs={{0,4},{1,5},{2,6},{3,7},{8,12},{9,13},{10,14},{11,15},{4,0},{5,1},... | collective-permute-start | bytes 1572872 | tf_op jit(solution)/shard_map/ppermute | solution.py:455
  242.6 25.4 %collective-permute-start.17 = (f32[4,4,2,32,128]{4,3,2,1,0:T(8,128)S(1)}, f32[4,4,2,32,128]{4,3,2,1,0:T(8,128)S(1)}, u32[]{:S(2)}, u32[]{:S(2)}) collective-permute-start(f32[4,4,2,32,128]{4,3,2,1,0:T(8,128)S(1)} %get-tuple-element.157.refs_6_), channel_id=1, source_target_pairs={{4,8},{5,9},{6,10},{7,11},{8,4},{9,5},{10,6},{11,7},{20,24},{21,25... | collective-permute-start | bytes 1572872 | tf_op jit(solution)/shard_map/ppermute | solution.py:455
  244.6 30.2 %collective-permute-start.18 = (f32[4,4,2,32,128]{4,3,2,1,0:T(8,128)S(1)}, f32[4,4,2,32,128]{4,3,2,1,0:T(8,128)S(1)}, u32[]{:S(2)}, u32[]{:S(2)}) collective-permute-start(f32[4,4,2,32,128]{4,3,2,1,0:T(8,128)S(1)} %get-tuple-element.164), channel_id=1, source_target_pairs={{4,12},{5,13},{6,14},{7,15},{8,0},{9,1},{10,2},{11,3},{20,28},{21,... | collective-permute-start | bytes 1572872 | tf_op jit(solution)/shard_map/ppermute | solution.py:455
  257.8 26.9 %collective-permute-start.16 = (f32[4,4,2,32,128]{4,3,2,1,0:T(8,128)S(1)}, f32[4,4,2,32,128]{4,3,2,1,0:T(8,128)S(1)}, u32[]{:S(2)}, u32[]{:S(2)}) collective-permute-start(f32[4,4,2,32,128]{4,3,2,1,0:T(8,128)S(1)} %get-tuple-element.161), channel_id=1, source_target_pairs={{0,4},{1,5},{2,6},{3,7},{8,12},{9,13},{10,14},{11,15},{4,0},{5,1},... | collective-permute-start | bytes 1572872 | tf_op jit(solution)/shard_map/ppermute | solution.py:455
  264.7 26.3 %collective-permute-start.11 = (f32[4,4,2,32,128]{4,3,2,1,0:T(8,128)S(1)}, f32[4,4,2,32,128]{4,3,2,1,0:T(8,128)S(1)}, u32[]{:S(2)}, u32[]{:S(2)}) collective-permute-start(f32[4,4,2,32,128]{4,3,2,1,0:T(8,128)S(1)} %get-tuple-element.152.refs_6_), channel_id=1, source_target_pairs={{4,8},{5,9},{6,10},{7,11},{8,4},{9,5},{10,6},{11,7},{20,24},{21,25... | collective-permute-start | bytes 1572872 | tf_op jit(solution)/shard_map/ppermute | solution.py:455
  266.6 30.7 %collective-permute-start.12 = (f32[4,4,2,32,128]{4,3,2,1,0:T(8,128)S(1)}, f32[4,4,2,32,128]{4,3,2,1,0:T(8,128)S(1)}, u32[]{:S(2)}, u32[]{:S(2)}) collective-permute-start(f32[4,4,2,32,128]{4,3,2,1,0:T(8,128)S(1)} %get-tuple-element.153), channel_id=1, source_target_pairs={{4,12},{5,13},{6,14},{7,15},{8,0},{9,1},{10,2},{11,3},{20,28},{21,... | collective-permute-start | bytes 1572872 | tf_op jit(solution)/shard_map/ppermute | solution.py:455
  280.2 26.6 %collective-permute-start.24 = (f32[4,4,2,32,128]{4,3,2,1,0:T(8,128)S(1)}, f32[4,4,2,32,128]{4,3,2,1,0:T(8,128)S(1)}, u32[]{:S(2)}, u32[]{:S(2)}) collective-permute-start(f32[4,4,2,32,128]{4,3,2,1,0:T(8,128)S(1)} %get-tuple-element.174), channel_id=1, source_target_pairs={{0,4},{1,5},{2,6},{3,7},{8,12},{9,13},{10,14},{11,15},{4,0},{5,1},... | collective-permute-start | bytes 1572872 | tf_op jit(solution)/shard_map/ppermute | solution.py:455
  287.6 27.6 %collective-permute-start.22 = (f32[4,4,2,32,128]{4,3,2,1,0:T(8,128)S(1)}, f32[4,4,2,32,128]{4,3,2,1,0:T(8,128)S(1)}, u32[]{:S(2)}, u32[]{:S(2)}) collective-permute-start(f32[4,4,2,32,128]{4,3,2,1,0:T(8,128)S(1)} %get-tuple-element.163.refs_6_), channel_id=1, source_target_pairs={{4,8},{5,9},{6,10},{7,11},{8,4},{9,5},{10,6},{11,7},{20,24},{21,25... | collective-permute-start | bytes 1572872 | tf_op jit(solution)/shard_map/ppermute | solution.py:455
  289.7 30.1 %collective-permute-start.23 = (f32[4,4,2,32,128]{4,3,2,1,0:T(8,128)S(1)}, f32[4,4,2,32,128]{4,3,2,1,0:T(8,128)S(1)}, u32[]{:S(2)}, u32[]{:S(2)}) collective-permute-start(f32[4,4,2,32,128]{4,3,2,1,0:T(8,128)S(1)} %get-tuple-element.173), channel_id=1, source_target_pairs={{4,12},{5,13},{6,14},{7,15},{8,0},{9,1},{10,2},{11,3},{20,28},{21,... | collective-permute-start | bytes 1572872 | tf_op jit(solution)/shard_map/ppermute | solution.py:455
  302.8 47.1 %collective-permute-start.19 = (f32[4,4,2,32,128]{4,3,2,1,0:T(8,128)}, f32[4,4,2,32,128]{4,3,2,1,0:T(8,128)}, u32[]{:S(2)}, u32[]{:S(2)}) collective-permute-start(f32[4,4,2,32,128]{4,3,2,1,0:T(8,128)} %get-tuple-element.169), channel_id=1, source_target_pairs={{0,4},{1,5},{2,6},{3,7},{8,12},{9,13},{10,14},{11,15},{4,0},{5,1},... | collective-permute-start | bytes 1572872 | tf_op jit(solution)/shard_map/ppermute | solution.py:455
  310.6 45.5 %collective-permute-start.26 = (f32[4,4,2,32,128]{4,3,2,1,0:T(8,128)}, f32[4,4,2,32,128]{4,3,2,1,0:T(8,128)}, u32[]{:S(2)}, u32[]{:S(2)}) collective-permute-start(f32[4,4,2,32,128]{4,3,2,1,0:T(8,128)} %get-tuple-element.176.refs_6_), channel_id=1, source_target_pairs={{4,8},{5,9},{6,10},{7,11},{8,4},{9,5},{10,6},{11,7},{20,24},{21,25... | collective-permute-start | bytes 1572872 | tf_op jit(solution)/shard_map/ppermute | solution.py:455
  312.6 43.6 %collective-permute-start.27 = (f32[4,4,2,32,128]{4,3,2,1,0:T(8,128)}, f32[4,4,2,32,128]{4,3,2,1,0:T(8,128)}, u32[]{:S(2)}, u32[]{:S(2)}) collective-permute-start(f32[4,4,2,32,128]{4,3,2,1,0:T(8,128)} %get-tuple-element.182), channel_id=1, source_target_pairs={{4,12},{5,13},{6,14},{7,15},{8,0},{9,1},{10,2},{11,3},{20,28},{21,... | collective-permute-start | bytes 1572872 | tf_op jit(solution)/shard_map/ppermute | solution.py:455
  342.2 19.6 %collective-permute-start.25 = (f32[4,4,2,32,128]{4,3,2,1,0:T(8,128)S(1)}, f32[4,4,2,32,128]{4,3,2,1,0:T(8,128)S(1)}, u32[]{:S(2)}, u32[]{:S(2)}) collective-permute-start(f32[4,4,2,32,128]{4,3,2,1,0:T(8,128)S(1)} %get-tuple-element.179), channel_id=1, source_target_pairs={{0,4},{1,5},{2,6},{3,7},{8,12},{9,13},{10,14},{11,15},{4,0},{5,1},... | collective-permute-start | bytes 1572872 | tf_op jit(solution)/shard_map/ppermute | solution.py:455
  352.9 17.1 %collective-permute-start.20 = (f32[4,4,2,32,128]{4,3,2,1,0:T(8,128)S(1)}, f32[4,4,2,32,128]{4,3,2,1,0:T(8,128)S(1)}, u32[]{:S(2)}, u32[]{:S(2)}) collective-permute-start(f32[4,4,2,32,128]{4,3,2,1,0:T(8,128)S(1)} %get-tuple-element.171.refs_6_), channel_id=1, source_target_pairs={{4,8},{5,9},{6,10},{7,11},{8,4},{9,5},{10,6},{11,7},{20,24},{21,25... | collective-permute-start | bytes 1572872 | tf_op jit(solution)/shard_map/ppermute | solution.py:455
  354.8 23.6 %collective-permute-start.21 = (f32[4,4,2,32,128]{4,3,2,1,0:T(8,128)S(1)}, f32[4,4,2,32,128]{4,3,2,1,0:T(8,128)S(1)}, u32[]{:S(2)}, u32[]{:S(2)}) collective-permute-start(f32[4,4,2,32,128]{4,3,2,1,0:T(8,128)S(1)} %get-tuple-element.172), channel_id=1, source_target_pairs={{4,12},{5,13},{6,14},{7,15},{8,0},{9,1},{10,2},{11,3},{20,28},{21,... | collective-permute-start | bytes 1572872 | tf_op jit(solution)/shard_map/ppermute | solution.py:455
  361.8 26.1 %collective-permute-start.33 = (f32[4,4,2,32,128]{4,3,2,1,0:T(8,128)S(1)}, f32[4,4,2,32,128]{4,3,2,1,0:T(8,128)S(1)}, u32[]{:S(2)}, u32[]{:S(2)}) collective-permute-start(f32[4,4,2,32,128]{4,3,2,1,0:T(8,128)S(1)} %get-tuple-element.192), channel_id=1, source_target_pairs={{0,4},{1,5},{2,6},{3,7},{8,12},{9,13},{10,14},{11,15},{4,0},{5,1},... | collective-permute-start | bytes 1572872 | tf_op jit(solution)/shard_map/ppermute | solution.py:455
  364.7 29.3 %collective-permute-start.31 = (f32[4,4,2,32,128]{4,3,2,1,0:T(8,128)S(1)}, f32[4,4,2,32,128]{4,3,2,1,0:T(8,128)S(1)}, u32[]{:S(2)}, u32[]{:S(2)}) collective-permute-start(f32[4,4,2,32,128]{4,3,2,1,0:T(8,128)S(1)} %get-tuple-element.181.refs_6_), channel_id=1, source_target_pairs={{4,8},{5,9},{6,10},{7,11},{8,4},{9,5},{10,6},{11,7},{20,24},{21,25... | collective-permute-start | bytes 1572872 | tf_op jit(solution)/shard_map/ppermute | solution.py:455
  368.6 32.3 %collective-permute-start.32 = (f32[4,4,2,32,128]{4,3,2,1,0:T(8,128)S(1)}, f32[4,4,2,32,128]{4,3,2,1,0:T(8,128)S(1)}, u32[]{:S(2)}, u32[]{:S(2)}) collective-permute-start(f32[4,4,2,32,128]{4,3,2,1,0:T(8,128)S(1)} %get-tuple-element.191), channel_id=1, source_target_pairs={{4,12},{5,13},{6,14},{7,15},{8,0},{9,1},{10,2},{11,3},{20,28},{21,... | collective-permute-start | bytes 1572872 | tf_op jit(solution)/shard_map/ppermute | solution.py:455
  384.0 26.3 %collective-permute-start.28 = (f32[4,4,2,32,128]{4,3,2,1,0:T(8,128)S(1)}, f32[4,4,2,32,128]{4,3,2,1,0:T(8,128)S(1)}, u32[]{:S(2)}, u32[]{:S(2)}) collective-permute-start(f32[4,4,2,32,128]{4,3,2,1,0:T(8,128)S(1)} %get-tuple-element.187), channel_id=1, source_target_pairs={{0,4},{1,5},{2,6},{3,7},{8,12},{9,13},{10,14},{11,15},{4,0},{5,1},... | collective-permute-start | bytes 1572872 | tf_op jit(solution)/shard_map/ppermute | solution.py:455
  390.7 24.3 %collective-permute-start.35 = (f32[4,4,2,32,128]{4,3,2,1,0:T(8,128)S(1)}, f32[4,4,2,32,128]{4,3,2,1,0:T(8,128)S(1)}, u32[]{:S(2)}, u32[]{:S(2)}) collective-permute-start(f32[4,4,2,32,128]{4,3,2,1,0:T(8,128)S(1)} %get-tuple-element.194.refs_6_), channel_id=1, source_target_pairs={{4,8},{5,9},{6,10},{7,11},{8,4},{9,5},{10,6},{11,7},{20,24},{21,25... | collective-permute-start | bytes 1572872 | tf_op jit(solution)/shard_map/ppermute | solution.py:455
  392.7 30.8 %collective-permute-start.36 = (f32[4,4,2,32,128]{4,3,2,1,0:T(8,128)S(1)}, f32[4,4,2,32,128]{4,3,2,1,0:T(8,128)S(1)}, u32[]{:S(2)}, u32[]{:S(2)}) collective-permute-start(f32[4,4,2,32,128]{4,3,2,1,0:T(8,128)S(1)} %get-tuple-element.200), channel_id=1, source_target_pairs={{4,12},{5,13},{6,14},{7,15},{8,0},{9,1},{10,2},{11,3},{20,28},{21,... | collective-permute-start | bytes 1572872 | tf_op jit(solution)/shard_map/ppermute | solution.py:455
  406.4 27.9 %collective-permute-start.34 = (f32[4,4,2,32,128]{4,3,2,1,0:T(8,128)S(1)}, f32[4,4,2,32,128]{4,3,2,1,0:T(8,128)S(1)}, u32[]{:S(2)}, u32[]{:S(2)}) collective-permute-start(f32[4,4,2,32,128]{4,3,2,1,0:T(8,128)S(1)} %get-tuple-element.197), channel_id=1, source_target_pairs={{0,4},{1,5},{2,6},{3,7},{8,12},{9,13},{10,14},{11,15},{4,0},{5,1},... | collective-permute-start | bytes 1572872 | tf_op jit(solution)/shard_map/ppermute | solution.py:455
  413.1 41.9 %collective-permute-start.29 = (f32[4,4,2,32,128]{4,3,2,1,0:T(8,128)S(1)}, f32[4,4,2,32,128]{4,3,2,1,0:T(8,128)S(1)}, u32[]{:S(2)}, u32[]{:S(2)}) collective-permute-start(f32[4,4,2,32,128]{4,3,2,1,0:T(8,128)S(1)} %get-tuple-element.189.refs_6_), channel_id=1, source_target_pairs={{4,8},{5,9},{6,10},{7,11},{8,4},{9,5},{10,6},{11,7},{20,24},{21,25... | collective-permute-start | bytes 1572872 | tf_op jit(solution)/shard_map/ppermute | solution.py:455
  428.9 23.3 %collective-permute-start.39 = (f32[4,4,2,32,128]{4,3,2,1,0:T(8,128)S(1)}, f32[4,4,2,32,128]{4,3,2,1,0:T(8,128)S(1)}, u32[]{:S(2)}, u32[]{:S(2)}) collective-permute-start(f32[4,4,2,32,128]{4,3,2,1,0:T(8,128)S(1)} %get-tuple-element.207), channel_id=1, source_target_pairs={{0,4},{1,5},{2,6},{3,7},{8,12},{9,13},{10,14},{11,15},{4,0},{5,1},... | collective-permute-start | bytes 1572872 | tf_op jit(solution)/shard_map/ppermute | solution.py:455
  432.8 22.2 %collective-permute-start.30 = (f32[4,4,2,32,128]{4,3,2,1,0:T(8,128)S(1)}, f32[4,4,2,32,128]{4,3,2,1,0:T(8,128)S(1)}, u32[]{:S(2)}, u32[]{:S(2)}) collective-permute-start(f32[4,4,2,32,128]{4,3,2,1,0:T(8,128)S(1)} %get-tuple-element.190), channel_id=1, source_target_pairs={{4,12},{5,13},{6,14},{7,15},{8,0},{9,1},{10,2},{11,3},{20,28},{21,... | collective-permute-start | bytes 1572872 | tf_op jit(solution)/shard_map/ppermute | solution.py:455
  437.2 23.6 %collective-permute-start.37 = (f32[4,4,2,32,128]{4,3,2,1,0:T(8,128)S(1)}, f32[4,4,2,32,128]{4,3,2,1,0:T(8,128)S(1)}, u32[]{:S(2)}, u32[]{:S(2)}) collective-permute-start(f32[4,4,2,32,128]{4,3,2,1,0:T(8,128)S(1)} %get-tuple-element.199.refs_6_), channel_id=1, source_target_pairs={{4,8},{5,9},{6,10},{7,11},{8,4},{9,5},{10,6},{11,7},{20,24},{21,25... | collective-permute-start | bytes 1572872 | tf_op jit(solution)/shard_map/ppermute | solution.py:455
  441.0 26.0 %collective-permute-start.38 = (f32[4,4,2,32,128]{4,3,2,1,0:T(8,128)S(1)}, f32[4,4,2,32,128]{4,3,2,1,0:T(8,128)S(1)}, u32[]{:S(2)}, u32[]{:S(2)}) collective-permute-start(f32[4,4,2,32,128]{4,3,2,1,0:T(8,128)S(1)} %get-tuple-element.206), channel_id=1, source_target_pairs={{4,12},{5,13},{6,14},{7,15},{8,0},{9,1},{10,2},{11,3},{20,28},{21,... | collective-permute-start | bytes 1572872 | tf_op jit(solution)/shard_map/ppermute | solution.py:455
  474.2 105.8 %all-to-all-start.5 = ((f32[4,36,2,32,128]{4,3,2,1,0:T(8,128)}), f32[4,36,2,32,128]{4,3,2,1,0:T(8,128)}, u32[]{:S(2)}, u32[]{:S(2)}) async-start(f32[4,36,2,32,128]{4,3,2,1,0:T(8,128)} %gate.13), calls=%async_computation.5 | async-start | bytes 9437184 | tf_op jit(solution)/shard_map/all_to_all | solution.py:452
  479.2 16.7 %collective-permute-start.42 = (f32[4,4,2,32,128]{4,3,2,1,0:T(8,128)}, f32[4,4,2,32,128]{4,3,2,1,0:T(8,128)S(1)}, u32[]{:S(2)}, u32[]{:S(2)}) collective-permute-start(f32[4,4,2,32,128]{4,3,2,1,0:T(8,128)} %copy-done.59), channel_id=1, source_target_pairs={{0,4},{1,5},{2,6},{3,7},{8,12},{9,13},{10,14},{11,15},{4,0},{5,1},... | collective-permute-start | bytes 1572872 | tf_op jit(solution)/shard_map/ppermute | solution.py:455
  483.0 19.4 %collective-permute-start.40 = (f32[4,4,2,32,128]{4,3,2,1,0:T(8,128)S(1)}, f32[4,4,2,32,128]{4,3,2,1,0:T(8,128)S(1)}, u32[]{:S(2)}, u32[]{:S(2)}) collective-permute-start(f32[4,4,2,32,128]{4,3,2,1,0:T(8,128)S(1)} %copy-done.37), channel_id=1, source_target_pairs={{4,8},{5,9},{6,10},{7,11},{8,4},{9,5},{10,6},{11,7},{20,24},{21,25... | collective-permute-start | bytes 1572872 | tf_op jit(solution)/shard_map/ppermute | solution.py:455
  485.2 23.5 %collective-permute-start.41 = (f32[4,4,2,32,128]{4,3,2,1,0:T(8,128)S(1)}, f32[4,4,2,32,128]{4,3,2,1,0:T(8,128)S(1)}, u32[]{:S(2)}, u32[]{:S(2)}) collective-permute-start(f32[4,4,2,32,128]{4,3,2,1,0:T(8,128)S(1)} %copy-done.53), channel_id=1, source_target_pairs={{4,12},{5,13},{6,14},{7,15},{8,0},{9,1},{10,2},{11,3},{20,28},{21,... | collective-permute-start | bytes 1572872 | tf_op jit(solution)/shard_map/ppermute | solution.py:455
  486.5 30.9 %collective-permute-start.48 = (f32[4,4,2,32,128]{4,3,2,1,0:T(8,128)}, f32[4,4,2,32,128]{4,3,2,1,0:T(8,128)S(1)}, u32[]{:S(2)}, u32[]{:S(2)}) collective-permute-start(f32[4,4,2,32,128]{4,3,2,1,0:T(8,128)} %copy-done.54), channel_id=1, source_target_pairs={{0,4},{1,5},{2,6},{3,7},{8,12},{9,13},{10,14},{11,15},{4,0},{5,1},... | collective-permute-start | bytes 1572872 | tf_op jit(solution)/shard_map/ppermute | solution.py:455
  498.8 27.6 %collective-permute-start.46 = (f32[4,4,2,32,128]{4,3,2,1,0:T(8,128)S(1)}, f32[4,4,2,32,128]{4,3,2,1,0:T(8,128)S(1)}, u32[]{:S(2)}, u32[]{:S(2)}) collective-permute-start(f32[4,4,2,32,128]{4,3,2,1,0:T(8,128)S(1)} %get-tuple-element.215.refs_6_), channel_id=1, source_target_pairs={{4,8},{5,9},{6,10},{7,11},{8,4},{9,5},{10,6},{11,7},{20,24},{21,25... | collective-permute-start | bytes 1572872 | tf_op jit(solution)/shard_map/ppermute | solution.py:455
  501.0 30.3 %collective-permute-start.47 = (f32[4,4,2,32,128]{4,3,2,1,0:T(8,128)S(1)}, f32[4,4,2,32,128]{4,3,2,1,0:T(8,128)S(1)}, u32[]{:S(2)}, u32[]{:S(2)}) collective-permute-start(f32[4,4,2,32,128]{4,3,2,1,0:T(8,128)S(1)} %get-tuple-element.222), channel_id=1, source_target_pairs={{4,12},{5,13},{6,14},{7,15},{8,0},{9,1},{10,2},{11,3},{20,28},{21,... | collective-permute-start | bytes 1572872 | tf_op jit(solution)/shard_map/ppermute | solution.py:455
  514.1 23.7 %collective-permute-start.43 = (f32[4,4,2,32,128]{4,3,2,1,0:T(8,128)S(1)}, f32[4,4,2,32,128]{4,3,2,1,0:T(8,128)S(1)}, u32[]{:S(2)}, u32[]{:S(2)}) collective-permute-start(f32[4,4,2,32,128]{4,3,2,1,0:T(8,128)S(1)} %get-tuple-element.218), channel_id=1, source_target_pairs={{4,0},{5,1},{6,2},{7,3},{12,8},{13,9},{14,10},{15,11},{20,16},{21,... | collective-permute-start | bytes 1572872 | tf_op jit(solution)/shard_map/ppermute | solution.py:455
  520.3 25.7 %collective-permute-start.50 = (f32[4,4,2,32,128]{4,3,2,1,0:T(8,128)S(1)}, f32[4,4,2,32,128]{4,3,2,1,0:T(8,128)S(1)}, u32[]{:S(2)}, u32[]{:S(2)}) collective-permute-start(f32[4,4,2,32,128]{4,3,2,1,0:T(8,128)S(1)} %get-tuple-element.224.refs_6_), channel_id=1, source_target_pairs={{4,8},{5,9},{6,10},{7,11},{8,4},{9,5},{10,6},{11,7},{20,24},{21,25... | collective-permute-start | bytes 1572872 | tf_op jit(solution)/shard_map/ppermute | solution.py:455
  525.0 28.7 %collective-permute-start.51 = (f32[4,4,2,32,128]{4,3,2,1,0:T(8,128)S(1)}, f32[4,4,2,32,128]{4,3,2,1,0:T(8,128)S(1)}, u32[]{:S(2)}, u32[]{:S(2)}) collective-permute-start(f32[4,4,2,32,128]{4,3,2,1,0:T(8,128)S(1)} %get-tuple-element.230), channel_id=1, source_target_pairs={{4,12},{5,13},{6,14},{7,15},{8,0},{9,1},{10,2},{11,3},{20,28},{21,... | collective-permute-start | bytes 1572872 | tf_op jit(solution)/shard_map/ppermute | solution.py:455
  536.6 25.3 %collective-permute-start.49 = (f32[4,4,2,32,128]{4,3,2,1,0:T(8,128)S(1)}, f32[4,4,2,32,128]{4,3,2,1,0:T(8,128)S(1)}, u32[]{:S(2)}, u32[]{:S(2)}) collective-permute-start(f32[4,4,2,32,128]{4,3,2,1,0:T(8,128)S(1)} %get-tuple-element.227), channel_id=1, source_target_pairs={{4,0},{5,1},{6,2},{7,3},{12,8},{13,9},{14,10},{15,11},{20,16},{21,... | collective-permute-start | bytes 1572872 | tf_op jit(solution)/shard_map/ppermute | solution.py:455
  539.2 25.8 %collective-permute-start.44 = (f32[4,4,2,32,128]{4,3,2,1,0:T(8,128)S(1)}, f32[4,4,2,32,128]{4,3,2,1,0:T(8,128)S(1)}, u32[]{:S(2)}, u32[]{:S(2)}) collective-permute-start(f32[4,4,2,32,128]{4,3,2,1,0:T(8,128)S(1)} %get-tuple-element.220.refs_6_), channel_id=1, source_target_pairs={{8,4},{9,5},{10,6},{11,7},{24,20},{25,21},{26,22},{27,23}} | collective-permute-start | bytes 1572872 | tf_op jit(solution)/shard_map/ppermute | solution.py:455
  544.7 30.7 %collective-permute-start.45 = (f32[4,4,2,32,128]{4,3,2,1,0:T(8,128)S(1)}, f32[4,4,2,32,128]{4,3,2,1,0:T(8,128)S(1)}, u32[]{:S(2)}, u32[]{:S(2)}) collective-permute-start(f32[4,4,2,32,128]{4,3,2,1,0:T(8,128)S(1)} %get-tuple-element.221), channel_id=1, source_target_pairs={{8,0},{9,1},{10,2},{11,3},{24,16},{25,17},{26,18},{27,19}} | collective-permute-start | bytes 1572872 | tf_op jit(solution)/shard_map/ppermute | solution.py:455
  580.0 61.8 %all-to-all-start.6 = ((f32[4,20,2,32,128]{4,3,2,1,0:T(8,128)}), f32[4,20,2,32,128]{4,3,2,1,0:T(8,128)}, u32[]{:S(2)}, u32[]{:S(2)}) async-start(f32[4,20,2,32,128]{4,3,2,1,0:T(8,128)} %gate.14), calls=%async_computation.6 | async-start | bytes 5242880 | tf_op jit(solution)/shard_map/all_to_all | solution.py:452
  584.7 16.4 %collective-permute-start.53 = (f32[4,4,2,32,128]{4,3,2,1,0:T(8,128)}, f32[4,4,2,32,128]{4,3,2,1,0:T(8,128)S(1)}, u32[]{:S(2)}, u32[]{:S(2)}) collective-permute-start(f32[4,4,2,32,128]{4,3,2,1,0:T(8,128)} %copy-done.57), channel_id=1, source_target_pairs={{4,0},{5,1},{6,2},{7,3},{12,8},{13,9},{14,10},{15,11},{20,16},{21,... | collective-permute-start | bytes 1572872 | tf_op jit(solution)/shard_map/ppermute | solution.py:455
  586.0 52.1 %collective-permute-start.58 = (f32[4,4,2,32,128]{4,3,2,1,0:T(8,128)S(1)}, f32[4,4,2,32,128]{4,3,2,1,0:T(8,128)S(1)}, u32[]{:S(2)}, u32[]{:S(2)}) collective-permute-start(f32[4,4,2,32,128]{4,3,2,1,0:T(8,128)S(1)} %get-tuple-element.229.refs_6_), channel_id=1, source_target_pairs={{8,4},{9,5},{10,6},{11,7},{24,20},{25,21},{26,22},{27,23}} | collective-permute-start | bytes 1572872 | tf_op jit(solution)/shard_map/ppermute | solution.py:455
  592.5 45.6 %collective-permute-start.59 = (f32[4,4,2,32,128]{4,3,2,1,0:T(8,128)S(1)}, f32[4,4,2,32,128]{4,3,2,1,0:T(8,128)S(1)}, u32[]{:S(2)}, u32[]{:S(2)}) collective-permute-start(f32[4,4,2,32,128]{4,3,2,1,0:T(8,128)S(1)} %copy-done.49), channel_id=1, source_target_pairs={{8,0},{9,1},{10,2},{11,3},{24,16},{25,17},{26,18},{27,19}} | collective-permute-start | bytes 1572872 | tf_op jit(solution)/shard_map/ppermute | solution.py:455
  602.4 37.0 %collective-permute-start.54 = (f32[4,4,2,32,128]{4,3,2,1,0:T(8,128)S(1)}, f32[4,4,2,32,128]{4,3,2,1,0:T(8,128)S(1)}, u32[]{:S(2)}, u32[]{:S(2)}) collective-permute-start(f32[4,4,2,32,128]{4,3,2,1,0:T(8,128)S(1)} %get-tuple-element.239.refs_6_), channel_id=1, source_target_pairs={{8,4},{9,5},{10,6},{11,7},{24,20},{25,21},{26,22},{27,23}} | collective-permute-start | bytes 1572872 | tf_op jit(solution)/shard_map/ppermute | solution.py:455
  604.8 34.6 %collective-permute-start.55 = (f32[4,4,2,32,128]{4,3,2,1,0:T(8,128)S(1)}, f32[4,4,2,32,128]{4,3,2,1,0:T(8,128)S(1)}, u32[]{:S(2)}, u32[]{:S(2)}) collective-permute-start(f32[4,4,2,32,128]{4,3,2,1,0:T(8,128)S(1)} %get-tuple-element.240), channel_id=1, source_target_pairs={{8,0},{9,1},{10,2},{11,3},{24,16},{25,17},{26,18},{27,19}} | collective-permute-start | bytes 1572872 | tf_op jit(solution)/shard_map/ppermute | solution.py:455
  611.1 27.0 %collective-permute-start.57 = (f32[8,256]{1,0:T(8,128)S(1)}, f32[8,256]{1,0:T(8,128)S(1)}, u32[]{:S(2)}, u32[]{:S(2)}) collective-permute-start(f32[8,256]{1,0:T(8,128)S(1)} %add.14.refs_7_), channel_id=1, source_target_pairs={{0,8},{1,9},{2,10},{3,11},{4,12},{5,13},{6,14},{7,15},{8,0},{9,1},... | collective-permute-start | bytes 24584 | tf_op jit(solution)/shard_map/ppermute | solution.py:474
  641.7 19.7 %all-to-all-start.7 = ((f32[4,8,2,32,128]{4,3,2,1,0:T(8,128)}), f32[4,8,2,32,128]{4,3,2,1,0:T(8,128)S(1)}, u32[]{:S(2)}, u32[]{:S(2)}) async-start(f32[4,8,2,32,128]{4,3,2,1,0:T(8,128)} %gate.15), calls=%async_computation.7 | async-start | bytes 2097152 | tf_op jit(solution)/shard_map/all_to_all | solution.py:452
  (66 other events, 522.5 us)
